TPU v7x, 32 devices: a whole 2x2x4 slice. The times are simulated.
32 devices in a mesh: dp: 16 (over z, y, core), mp: 2 (over x).
Axes of the slice: x: 2, y: 2, z: 4, core: 2. Of those that a mesh axis runs over, the one named last changes fastest.
Arguments:
- inputs: bfloat16 [3, 1024, 2560], P(None, 'dp'), may hold values from -6 to 6
- gain_attn: float32 [2560], replicated, may hold values from 0.5 to 1.5
- w_query: bfloat16 [2560, 2560], P('dp', 'mp'), may hold values from -0.125 to 0.125
- w_keyval: bfloat16 [2560, 512], P('dp'), may hold values from -0.125 to 0.125
- w_output: bfloat16 [2560, 2560], P('mp', 'dp'), may hold values from -0.3125 to 0.3125
- gain_mlp: float32 [2560], replicated, may hold values from 0.5 to 1.5
- w_gate: bfloat16 [2560, 7680], P('dp', 'mp'), may hold values from -0.125 to 0.125
- b_gate: float32 [7680], P('mp'), may hold values from -3 to 3
- w_up: bfloat16 [2560, 7680], P('dp', 'mp'), may hold values from -0.125 to 0.125
- b_up: float32 [7680], P('mp'), may hold values from -3 to 3
- w_down: bfloat16 [7680, 2560], P('mp', 'dp'), may hold values from -0.125 to 0.125
- b_down: float32 [2560], replicated, may hold values from -3 to 3
- segment_ids: int32 [3, 16, 64], P(None, 'dp'), may hold values from 0 to 7, never falling along the last dimension, each value on 1 to 32 neighbouring positions
- cotangent: bfloat16 [3, 1024, 2560], P(None, 'dp'), may hold values from -12 to 12
Outputs:
- outputs: bfloat16 [3, 1024, 2560], P(None, 'dp')
- inputs_grad: bfloat16 [3, 1024, 2560], P(None, 'dp')
- gain_attn_grad: float32 [2560], replicated
- w_query_grad: float32 [2560, 2560], P('dp', 'mp')
- w_keyval_grad: float32 [2560, 512], P('dp')
- w_output_grad: float32 [2560, 2560], P('mp', 'dp')
- gain_mlp_grad: float32 [2560], replicated
- w_gate_grad: float32 [2560, 7680], P('dp', 'mp')
- b_gate_grad: float32 [7680], P('mp')
- w_up_grad: float32 [2560, 7680], P('dp', 'mp')
- b_up_grad: float32 [7680], P('mp')
- w_down_grad: float32 [7680, 2560], P('mp', 'dp')
- b_down_grad: float32 [2560], replicated
Inputs may be any that keep to these rules, and one draw needn't show every extreme that they name: `segment_ids`: ids never fall within a block of 64 tokens; a sequence holds 1 to 32 tokens and some sequence holds 32.
All inputs are finite; a program needn't handle non-finite values.
Results may differ from a plain program's by a relative error of at most 0.014.
Values may be sent and summed in bfloat16 or wider, within the bound.
No kernel may reach another device: no remote copies, remote signals or barrier semaphores. Data moves between devices by JAX's collectives and lax.ppermute only.
A program may use at most 384 MiB of HBM per device.

v0:
```python
from functools import partial

import jax
import jax.numpy as jnp
from jax import lax
from jax.sharding import PartitionSpec as P

EPS = 1e-06


def positions(segment):
    count = segment.shape[0]
    index = jnp.arange(count, dtype=jnp.int32)
    fresh = jnp.concatenate([jnp.ones((1,), jnp.bool_), segment[1:] != segment[:-1]])
    starts = lax.cummax(jnp.where(fresh, index, 0), axis=0)
    return (index - starts).astype(jnp.float32)


def rotate(tensor, offsets, direction):
    quarter = tensor.shape[-1] // 4
    freqs = 10000.0 ** (-jnp.arange(quarter, dtype=jnp.float32) / quarter)
    angle = offsets[:, None] * freqs[None, :]
    cosine = jnp.cos(angle)[:, None, :]
    sine = direction * jnp.sin(angle)[:, None, :]
    front_half = tensor[..., :quarter]
    back_half = tensor[..., quarter : 2 * quarter]
    return jnp.concatenate(
        [
            front_half * cosine - back_half * sine,
            back_half * cosine + front_half * sine,
            tensor[..., 2 * quarter :],
        ],
        axis=-1,
    )


def model_sum(values):
    return lax.psum(values, "mp")


def inv_root(values):
    return lax.rsqrt(jnp.mean(values * values, axis=-1, keepdims=True) + EPS)


def norm_back(values, factor, gain, grad_norm):
    scaled = gain * grad_norm
    return factor * scaled - values * factor**3 * jnp.mean(scaled * values, axis=-1, keepdims=True)


def masked_scores(rot_query, rot_key, segment):
    length = segment.shape[0]
    index = jnp.arange(length, dtype=jnp.int32)
    allowed = (segment[:, None] == segment[None, :]) & (index[None, :] <= index[:, None])
    scores = jnp.einsum("thd,sd->hts", rot_query, rot_key, preferred_element_type=jnp.float32)
    return jnp.where(allowed[None], scores, -1e30)


def shards(
    inputs,
    gain_attn,
    w_query,
    w_keyval,
    w_output,
    gain_mlp,
    w_gate,
    b_gate,
    w_up,
    b_up,
    w_down,
    b_down,
    segment_ids,
    cotangent,
):
    micro = inputs.shape[0]
    length = inputs.shape[1]
    head_dim = w_keyval.shape[1] // 2
    local_heads = w_query.shape[1] // head_dim
    scale = head_dim ** (-0.5)
    ffn_total = None
    attn_total = None
    small = None
    outs_list = []
    grads_list = []
    for micro_idx in range(micro):
        wq_full, wkv_full, wg_full, wu_full, wo_full, wd_full = (
            lax.all_gather(w_query, "dp", axis=0, tiled=True),
            lax.all_gather(w_keyval, "dp", axis=0, tiled=True),
            lax.all_gather(w_gate, "dp", axis=0, tiled=True),
            lax.all_gather(w_up, "dp", axis=0, tiled=True),
            lax.all_gather(w_output, "dp", axis=1, tiled=True),
            lax.all_gather(w_down, "dp", axis=1, tiled=True),
        )
        segment = segment_ids[micro_idx, 0]
        offsets = positions(segment)
        hidden_x = inputs[micro_idx].astype(jnp.float32)
        factor_one = inv_root(hidden_x)
        normed = (hidden_x * factor_one * gain_attn).astype(jnp.bfloat16)
        queries = jnp.dot(normed, wq_full, preferred_element_type=jnp.float32)
        keyval = jnp.dot(normed, wkv_full, preferred_element_type=jnp.float32)
        rot_query = (
            rotate(queries.reshape(length, local_heads, head_dim), offsets, 1.0) * scale
        ).astype(jnp.bfloat16)
        rot_key = rotate(keyval[:, None, :head_dim], offsets, 1.0)[:, 0, :].astype(jnp.bfloat16)
        values_in = keyval[:, head_dim:].astype(jnp.bfloat16)
        scores = masked_scores(rot_query, rot_key, segment)
        row_max = jnp.max(scores, axis=-1, keepdims=True)
        expon = jnp.exp(scores - row_max)
        row_total = jnp.sum(expon, axis=-1, keepdims=True)
        log_total = row_max + jnp.log(row_total)
        probs_b = (expon / row_total).astype(jnp.bfloat16)
        mixed = jnp.einsum("hts,sd->thd", probs_b, values_in, preferred_element_type=jnp.float32)
        mixed_b = mixed.reshape(length, local_heads * head_dim).astype(jnp.bfloat16)
        attended = model_sum(jnp.dot(mixed_b, wo_full, preferred_element_type=jnp.float32))
        residual = hidden_x + attended
        factor_two = inv_root(residual)
        normed_two = (residual * factor_two * gain_mlp).astype(jnp.bfloat16)
        gate_pre = jnp.dot(normed_two, wg_full, preferred_element_type=jnp.float32) + b_gate
        up_pre = jnp.dot(normed_two, wu_full, preferred_element_type=jnp.float32) + b_up
        gelu_out, gelu_pull = jax.vjp(partial(jax.nn.gelu, approximate=True), gate_pre)
        inner_b = (gelu_out * up_pre).astype(jnp.bfloat16)
        branch = model_sum(jnp.dot(inner_b, wd_full, preferred_element_type=jnp.float32)) + b_down
        outs_list.append((residual + branch).astype(jnp.bfloat16))
        wq_full, wkv_full, wg_full, wu_full, wo_full, wd_full = (
            lax.all_gather(w_query, "dp", axis=0, tiled=True),
            lax.all_gather(w_keyval, "dp", axis=0, tiled=True),
            lax.all_gather(w_gate, "dp", axis=0, tiled=True),
            lax.all_gather(w_up, "dp", axis=0, tiled=True),
            lax.all_gather(w_output, "dp", axis=1, tiled=True),
            lax.all_gather(w_down, "dp", axis=1, tiled=True),
        )
        grad_out = cotangent[micro_idx].astype(jnp.float32)
        grad_branch = grad_out.astype(jnp.bfloat16)
        bias_down_term = jnp.sum(grad_branch.astype(jnp.float32), axis=0)
        down_term = jnp.einsum(
            "tf,td->fd", inner_b, grad_branch, preferred_element_type=jnp.float32
        )
        grad_inner = jnp.einsum(
            "td,fd->tf", grad_branch, wd_full, preferred_element_type=jnp.float32
        )
        grad_gate = gelu_pull(grad_inner * up_pre)[0].astype(jnp.bfloat16)
        grad_up = (grad_inner * gelu_out).astype(jnp.bfloat16)
        bias_gate_term = jnp.sum(grad_gate.astype(jnp.float32), axis=0)
        bias_up_term = jnp.sum(grad_up.astype(jnp.float32), axis=0)
        gate_term = jnp.einsum(
            "td,tf->df", normed_two, grad_gate, preferred_element_type=jnp.float32
        )
        up_term = jnp.einsum("td,tf->df", normed_two, grad_up, preferred_element_type=jnp.float32)
        ffn_terms = (gate_term, up_term, down_term)
        ffn_total = ffn_terms if ffn_total is None else jax.tree.map(jnp.add, ffn_total, ffn_terms)
        grad_norm_two = jnp.einsum(
            "tf,df->td", grad_gate, wg_full, preferred_element_type=jnp.float32
        )
        grad_norm_two = model_sum(
            grad_norm_two
            + jnp.einsum("tf,df->td", grad_up, wu_full, preferred_element_type=jnp.float32)
        )
        gain_mlp_term = jnp.sum(grad_norm_two * residual * factor_two, axis=0)
        grad_resid = grad_out + norm_back(residual, factor_two, gain_mlp, grad_norm_two)
        grad_resid_b = grad_resid.astype(jnp.bfloat16)
        output_term = jnp.einsum(
            "ta,td->ad", mixed_b, grad_resid_b, preferred_element_type=jnp.float32
        )
        grad_mixed = jnp.einsum(
            "td,ad->ta", grad_resid_b, wo_full, preferred_element_type=jnp.float32
        )
        grad_mixed = grad_mixed.astype(jnp.bfloat16).reshape(length, local_heads, head_dim)
        scores = masked_scores(rot_query, rot_key, segment)
        probs = jnp.exp(scores - log_total)
        probs_b = probs.astype(jnp.bfloat16)
        grad_values = jnp.einsum(
            "hts,thd->sd", probs_b, grad_mixed, preferred_element_type=jnp.float32
        )
        grad_probs = jnp.einsum(
            "thd,sd->hts", grad_mixed, values_in, preferred_element_type=jnp.float32
        )
        row_delta = jnp.sum(probs * grad_probs, axis=-1, keepdims=True)
        grad_scores = (probs * (grad_probs - row_delta)).astype(jnp.bfloat16)
        grad_rq = (
            jnp.einsum("hts,sd->thd", grad_scores, rot_key, preferred_element_type=jnp.float32)
            * scale
        )
        grad_query = (
            rotate(grad_rq, offsets, -1.0)
            .reshape(length, local_heads * head_dim)
            .astype(jnp.bfloat16)
        )
        grad_rk = jnp.einsum(
            "hts,thd->sd", grad_scores, rot_query, preferred_element_type=jnp.float32
        )
        grad_key = rotate(grad_rk[:, None, :], offsets, -1.0)[:, 0, :]
        query_part = jnp.einsum(
            "ta,da->td", grad_query, wq_full, preferred_element_type=jnp.float32
        )
        query_sum, grad_keyval = model_sum(
            (query_part, jnp.concatenate([grad_key, grad_values], axis=-1))
        )
        grad_keyval_b = grad_keyval.astype(jnp.bfloat16)
        grad_normed = query_sum + jnp.einsum(
            "tc,dc->td", grad_keyval_b, wkv_full, preferred_element_type=jnp.float32
        )
        query_term = jnp.einsum("td,ta->da", normed, grad_query, preferred_element_type=jnp.float32)
        keyval_term = jnp.einsum(
            "td,tc->dc", normed, grad_keyval_b, preferred_element_type=jnp.float32
        )
        gain_attn_term = jnp.sum(grad_normed * hidden_x * factor_one, axis=0)
        grad_input = grad_resid + norm_back(hidden_x, factor_one, gain_attn, grad_normed)
        grads_list.append(grad_input.astype(jnp.bfloat16))
        attn_terms = (query_term, keyval_term, output_term)
        attn_total = (
            attn_terms if attn_total is None else jax.tree.map(jnp.add, attn_total, attn_terms)
        )
        small_terms = (gain_attn_term, gain_mlp_term, bias_gate_term, bias_up_term, bias_down_term)
        small = small_terms if small is None else jax.tree.map(jnp.add, small, small_terms)
    shares = (
        lax.psum_scatter(attn_total[0], "dp", scatter_dimension=0, tiled=True),
        lax.psum_scatter(attn_total[1], "dp", scatter_dimension=0, tiled=True),
        lax.psum_scatter(ffn_total[0], "dp", scatter_dimension=0, tiled=True),
        lax.psum_scatter(ffn_total[1], "dp", scatter_dimension=0, tiled=True),
        lax.psum_scatter(attn_total[2], "dp", scatter_dimension=1, tiled=True),
        lax.psum_scatter(ffn_total[2], "dp", scatter_dimension=1, tiled=True),
    )
    attn_total = (shares[0], shares[1], shares[4])
    ffn_total = (shares[2], shares[3], shares[5])
    small = lax.psum((small[0], small[1], small[2], small[3], small[4]), "dp")
    outputs = jnp.stack(outs_list, axis=0)
    inputs_grad = jnp.stack(grads_list, axis=0)
    return (
        outputs,
        inputs_grad,
        small[0],
        attn_total[0],
        attn_total[1],
        attn_total[2],
        small[1],
        ffn_total[0],
        small[2],
        ffn_total[1],
        small[3],
        ffn_total[2],
        small[4],
    )


def solution(mesh):
    in_specs = (
        P(None, "dp", None),
        P(),
        P("dp", "mp"),
        P("dp", None),
        P("mp", "dp"),
        P(),
        P("dp", "mp"),
        P("mp"),
        P("dp", "mp"),
        P("mp"),
        P("mp", "dp"),
        P(),
        P(None, "dp", None),
        P(None, "dp", None),
    )
    out_specs = (
        P(None, "dp", None),
        P(None, "dp", None),
        P(),
        P("dp", "mp"),
        P("dp", None),
        P("mp", "dp"),
        P(),
        P("dp", "mp"),
        P("mp"),
        P("dp", "mp"),
        P("mp"),
        P("mp", "dp"),
        P(),
    )
    return jax.shard_map(shards, mesh=mesh, in_specs=in_specs, out_specs=out_specs, check_vma=False)
```

profile of v0, /device:TPU:0, one launch (start us, length us, event | category | flops | bytes accessed | tf_op | source)
XLA Modules:
  0.0 2419.6 jit_solution(9911652251985413412)
XLA Ops:
  16.0 40.3 %all-gather.7.cloned.1.call-done = bf16[2560,512]{1,0:T(8,128)(2,1)} async-done(((bf16[160,512]{1,0:T(8,128)(2,1)}), bf16[2560,512]{1,0:T(8,128)(2,1)}) %all-gather.7.cloned.1.call-update) | async-done | bytes 2621456 | tf_op jit(solution)/shard_map/all_gather | solution.py:87
  56.3 2.5 fusion.163
  58.8 2.5 fusion.169
  61.4 2.5 fusion.175
  64.4 56.2 %all-gather.9.cloned.1.call-done = bf16[2560,1280]{1,0:T(8,128)(2,1)} async-done(((bf16[160,1280]{1,0:T(8,128)(2,1)}), bf16[2560,1280]{1,0:T(8,128)(2,1)}) %all-gather.9.cloned.1.call-update) | async-done | bytes 6553616 | tf_op jit(solution)/shard_map/all_gather | solution.py:86
  120.7 9.5 copy.44
  130.2 5.1 fusion.104
  136.3 5.1 fusion.107
  145.5 39.4 %all-gather.11.cloned.1.call-done = bf16[1280,2560]{0,1:T(8,128)(2,1)} async-done(((bf16[1280,160]{0,1:T(8,128)(2,1)}), bf16[1280,2560]{0,1:T(8,128)(2,1)}) %all-gather.11.cloned.1.call-update) | async-done | bytes 6553616 | tf_op jit(solution)/shard_map/all_gather | solution.py:90
  184.9 5.9 fusion.268
  190.9 5.8 fusion.266
  196.7 2.9 fusion.264
  203.0 55.7 %all-reduce.14.cloned.1.call-done = (f32[64,2560]{1,0:T(8,128)}, f32[64,2560]{1,0:T(8,128)}, f32[64,2560]{1,0:T(8,128)}) async-done(((f32[64,2560]{1,0:T(8,128)}, f32[64,2560]{1,0:T(8,128)}, f32[64,2560]{1,0:T(8,128)}), (f32[64,2560]{1,0:T(8,128)}, f32[64,2560]{1,0:T(8,128)}, f32[64,2560]{1,0:T(8,128)})) %all-reduce.14.cloned.1.call-update) | async-done | bytes 1966096 | tf_op jit(solution)/shard_map/psum | solution.py:38
  262.8 100.2 %all-gather.13.cloned.1.call-done = bf16[2560,3840]{1,0:T(8,128)(2,1)} async-done(((bf16[160,3840]{1,0:T(8,128)(2,1)}), bf16[2560,3840]{1,0:T(8,128)(2,1)}) %all-gather.13.cloned.1.call-update) | async-done | bytes 19660816 | tf_op jit(solution)/shard_map/all_gather | solution.py:88
  363.0 11.2 convolution_add_fusion.5
  374.2 2.1 copy-done
  376.3 4.5 convolution_add_fusion.7
  380.8 86.4 %all-gather.15.cloned.1.call-done = bf16[2560,3840]{1,0:T(8,128)(2,1)} async-done(((bf16[160,3840]{1,0:T(8,128)(2,1)}), bf16[2560,3840]{1,0:T(8,128)(2,1)}) %all-gather.15.cloned.1.call-update) | async-done | bytes 19660816 | tf_op jit(solution)/shard_map/all_gather | solution.py:89
  467.2 11.2 convolution_add_fusion.4
  478.4 11.4 convolution_add_fusion.6
  489.9 4.9 convolution_add_fusion.9
  494.7 11.4 convolution_add_fusion.8
  506.2 65.4 %all-gather.17.cloned.1.call-done = bf16[3840,2560]{0,1:T(8,128)(2,1)} async-done(((bf16[3840,160]{0,1:T(8,128)(2,1)}), bf16[3840,2560]{0,1:T(8,128)(2,1)}) %all-gather.17.cloned.1.call-update) | async-done | bytes 19660816 | tf_op jit(solution)/shard_map/all_gather | solution.py:91
  571.6 12.4 convert_reduce_fusion
  584.8 13.4 fusion.274
  598.2 12.5 convert_reduce_fusion.1
  610.7 13.9 fusion.272
  624.6 12.7 convert_reduce_fusion.2
  637.3 13.6 fusion.270
  651.0 13.6 convolution_add_fusion.11
  664.5 13.8 convolution_add_fusion.13
  678.3 13.5 convolution_add_fusion.15
  691.9 14.1 fusion.269
  706.0 13.6 fusion.267
  719.6 13.5 fusion.265
  733.1 19.4 all-reduce.12.cloned.1.call-done
  752.5 3.3 multiply_reduce_fusion.2
  755.9 3.2 convert_add_fusion.2
  759.2 4.8 convolution_convert_fusion
  771.3 2.9 fusion.275
  774.3 2.9 fusion.273
  777.2 2.9 fusion.271
  784.6 23.4 all-reduce.15
  810.1 3.3 add_add_fusion.3
  817.6 6.8 convolution_add_fusion.2
  829.4 6.6 convolution_add_fusion
  837.1 17.3 fusion.276
  854.4 15.3 fusion.277
  869.7 39.9 %add_add_fusion.2 = f32[2560,3840]{1,0:T(8,128)} fusion(f32[2560,3840]{1,0:T(8,128)} %fusion.276, f32[2560,3840]{1,0:T(8,128)} %fusion.277, bf16[64,2560]{1,0:T(8,128)(2,1)S(1)} %copy-done.15, bf16[64,3840]{1,0:T(8,128)(2,1)S(1)} %copy-done.31), kind=kOutput, calls=%fused_computation.2 | convolution fusion | flops 1277952000 | bytes 118784000 | tf_op jit(solution)/shard_map/td,tf->df/dot_general | solution.py:144
  910.6 16.1 fusion.278
  926.8 15.3 fusion.279
  942.1 40.1 %add_add_fusion.1 = f32[2560,3840]{1,0:T(8,128)} fusion(f32[2560,3840]{1,0:T(8,128)} %fusion.278, f32[2560,3840]{1,0:T(8,128)} %fusion.279, bf16[64,2560]{1,0:T(8,128)(2,1)S(1)} %copy-done.15, bf16[64,3840]{1,0:T(8,128)(2,1)S(1)} %copy-done.33), kind=kOutput, calls=%fused_computation.1 | convolution fusion | flops 1277952000 | bytes 118784000 | tf_op jit(solution)/shard_map/td,tf->df/dot_general | solution.py:147
  983.5 21.1 fusion.100
  1004.6 16.3 fusion.96
  1020.9 39.9 %add_add_fusion = f32[3840,2560]{0,1:T(8,128)} fusion(f32[3840,2560]{0,1:T(8,128)} %fusion.100, f32[3840,2560]{0,1:T(8,128)} %fusion.96, bf16[64,3840]{1,0:T(8,128)(2,1)S(1)} %copy-done.25, bf16[3,64,2560]{2,1,0:T(8,128)(2,1)S(1)} %copy-done.5), kind=kOutput, calls=%fused_computation | convolution fusion | flops 1277952000 | bytes 118784000 | tf_op jit(solution)/shard_map/tf,td->fd/dot_general | solution.py:134
  1067.9 2.3 convolution_add_fusion.12
  1070.2 3.7 fusion.81
  1074.0 63.7 %all-reduce = (f32[2560]{0:T(1024)}, f32[2560]{0:T(1024)}, f32[3840]{0:T(1024)}, f32[3840]{0:T(1024)}, f32[2560]{0:T(1024)}) all-reduce(f32[2560]{0:T(1024)S(1)} %add_add_fusion.8, f32[2560]{0:T(1024)S(1)} %add_add_fusion.7, f32[3840]{0:T(1024)S(1)} %copy-done.132, ...), channel_id=1, replica_groups=mesh['dp'=16,'mp'=2] {'dp'}, use_global_device_ids=true, to_apply=%region_42.43 | all-reduce | flops 15360 | bytes 122880 | tf_op jit(solution)/shard_map/psum | solution.py:224
  1137.7 2.6 fusion.84
  1141.4 3.8 fusion.89
  1146.2 115.0 %reduce-scatter.11.cloned.1.call-done = f32[1280,160]{0,1:T(8,128)} async-done(((f32[1280,2560]{0,1:T(8,128)}), f32[1280,160]{0,1:T(8,128)}) %reduce-scatter.11.cloned.1.call-update) | async-done | bytes 819216 | tf_op jit(solution)/shard_map/reduce_scatter | solution.py:219
  1261.2 383.7 %reduce-scatter.13.cloned.1.call-done = f32[160,3840]{1,0:T(8,128)} async-done(((f32[2560,3840]{1,0:T(8,128)}), f32[160,3840]{1,0:T(8,128)}) %reduce-scatter.13.cloned.1.call-update) | async-done | bytes 2457616 | tf_op jit(solution)/shard_map/reduce_scatter | solution.py:217
  1644.9 384.1 %reduce-scatter.15.cloned.1.call-done = f32[160,3840]{1,0:T(8,128)} async-done(((f32[2560,3840]{1,0:T(8,128)}), f32[160,3840]{1,0:T(8,128)}) %reduce-scatter.15.cloned.1.call-update) | async-done | bytes 2457616 | tf_op jit(solution)/shard_map/reduce_scatter | solution.py:218
  2029.0 383.6 %reduce-scatter.17.cloned.1.call-done = f32[3840,160]{0,1:T(8,128)} async-done(((f32[3840,2560]{0,1:T(8,128)}), f32[3840,160]{0,1:T(8,128)}) %reduce-scatter.17.cloned.1.call-update) | async-done | bytes 2457616 | tf_op jit(solution)/shard_map/reduce_scatter | solution.py:220
  (479 shorter events, 56.8 us)
Async XLA Ops:
  7.2 123.0 %copy-start.3 = (bf16[3,64,2560]{2,1,0:T(8,128)(2,1)S(1)}, bf16[3,64,2560]{2,1,0:T(8,128)(2,1)}, u32[]{:S(2)}) copy-start(bf16[3,64,2560]{2,1,0:T(8,128)(2,1)} %param.14) | copy-start | bytes 2949124
  7.2 123.0 %copy-start.40 = (f32[2560]{0:T(1024)S(1)}, f32[2560]{0:T(1024)}, u32[]{:S(2)}) copy-start(f32[2560]{0:T(1024)} %param.15) | copy-start | bytes 30724
  7.2 49.1 %all-gather.7.cloned.1.call-start = ((), (), s32[]{:S(2)}) async-start(), calls=%async_computation.6 | async-start | bytes 2785280 | tf_op jit(solution)/shard_map/all_gather | solution.py:87
  7.9 112.7 %all-gather.9.cloned.1.call-start = ((), (), s32[]{:S(2)}) async-start(), calls=%async_computation.7 | async-start | bytes 6963200 | tf_op jit(solution)/shard_map/all_gather | solution.py:86
  8.7 176.2 %all-gather.11.cloned.1.call-start = ((), (), s32[]{:S(2)}) async-start(), calls=%async_computation.8 | async-start | bytes 6963200 | tf_op jit(solution)/shard_map/all_gather | solution.py:90
  9.4 249.3 %all-reduce.14.cloned.1.call-start = ((), (), s32[]{:S(2)}) async-start(), calls=%async_computation.20 | async-start | bytes 3932160 | tf_op jit(solution)/shard_map/psum | solution.py:38
  11.4 123.9 %copy-start.141 = (f32[64]{0:T(128)}, f32[64]{0:T(128)S(1)}, u32[]{:S(2)}) copy-start(f32[64]{0:T(128)S(1)} %multiply_power_fusion) | copy-start | bytes 772
  12.9 122.4 %copy-start.143 = (f32[64]{0:T(128)}, f32[64]{0:T(128)S(1)}, u32[]{:S(2)}) copy-start(f32[64]{0:T(128)S(1)} %subtract_convert_fusion.2) | copy-start | bytes 772
  12.9 122.4 %copy-start.145 = (f32[64]{0:T(128)}, f32[64]{0:T(128)S(1)}, u32[]{:S(2)}) copy-start(f32[64]{0:T(128)S(1)} %subtract_convert_fusion) | copy-start | bytes 772
  12.9 122.4 %copy-start.147 = (f32[64]{0:T(128)}, f32[64]{0:T(128)S(1)}, u32[]{:S(2)}) copy-start(f32[64]{0:T(128)S(1)} %subtract_convert_fusion.1) | copy-start | bytes 772
  13.5 129.0 %copy-start.139 = (f32[64]{0:T(128)}, f32[64]{0:T(128)S(1)}, u32[]{:S(2)}) copy-start(f32[64]{0:T(128)S(1)} %get-tuple-element.142) | copy-start | bytes 772
  14.8 120.6 %copy-start.134 = (f32[64]{0:T(128)}, f32[64]{0:T(128)S(1)}, u32[]{:S(2)}) copy-start(f32[64]{0:T(128)S(1)} %get-tuple-element.146) | copy-start | bytes 772
  14.8 121.6 %copy-start.137 = (f32[64]{0:T(128)}, f32[64]{0:T(128)S(1)}, u32[]{:S(2)}) copy-start(f32[64]{0:T(128)S(1)} %get-tuple-element.180) | copy-start | bytes 772
  16.0 119.4 %copy-start.92 = (f32[64,64]{1,0:T(8,128)}, f32[64,64]{1,0:T(8,128)S(1)}, u32[]{:S(2)}) copy-start(f32[64,64]{1,0:T(8,128)S(1)} %get-tuple-element.152) | copy-start | bytes 49156
  16.0 125.5 %copy-start.90 = (f32[64,64]{1,0:T(8,128)}, f32[64,64]{1,0:T(8,128)S(1)}, u32[]{:S(2)}) copy-start(f32[64,64]{1,0:T(8,128)S(1)} %get-tuple-element.155) | copy-start | bytes 49156
  58.7 77.1 %copy-start.88 = (f32[64,512]{1,0:T(8,128)}, f32[64,512]{1,0:T(8,128)S(1)}, u32[]{:S(2)}) copy-start(f32[64,512]{1,0:T(8,128)S(1)} %fusion.163) | copy-start | bytes 393220
  58.8 76.7 %copy-start.130 = (bf16[64,1,128]{2,0,1:T(8,128)(2,1)}, bf16[64,1,128]{2,0,1:T(8,128)(2,1)S(1)}, u32[]{:S(2)}) copy-start(bf16[64,1,128]{2,0,1:T(8,128)(2,1)S(1)} %slice.441) | copy-start | bytes 49156
  61.3 80.8 %copy-start.86 = (f32[64,512]{1,0:T(8,128)}, f32[64,512]{1,0:T(8,128)S(1)}, u32[]{:S(2)}) copy-start(f32[64,512]{1,0:T(8,128)S(1)} %fusion.169) | copy-start | bytes 393220
  61.3 80.3 %copy-start.128 = (bf16[64,1,128]{2,0,1:T(8,128)(2,1)}, bf16[64,1,128]{2,0,1:T(8,128)(2,1)S(1)}, u32[]{:S(2)}) copy-start(bf16[64,1,128]{2,0,1:T(8,128)(2,1)S(1)} %slice.442) | copy-start | bytes 49156
  63.9 81.4 %copy-start.84 = (f32[64,512]{1,0:T(8,128)}, f32[64,512]{1,0:T(8,128)S(1)}, u32[]{:S(2)}) copy-start(f32[64,512]{1,0:T(8,128)S(1)} %fusion.175) | copy-start | bytes 393220
  63.9 80.9 %copy-start.126 = (bf16[64,1,128]{2,0,1:T(8,128)(2,1)}, bf16[64,1,128]{2,0,1:T(8,128)(2,1)S(1)}, u32[]{:S(2)}) copy-start(bf16[64,1,128]{2,0,1:T(8,128)(2,1)S(1)} %slice.443) | copy-start | bytes 49156
  64.4 77.1 %copy-start.122 = (bf16[64,1,64]{2,0,1:T(8,128)(2,1)}, bf16[64,1,64]{2,0,1:T(8,128)(2,1)S(1)}, u32[]{:S(2)}) copy-start(bf16[64,1,64]{2,0,1:T(8,128)(2,1)S(1)} %get-tuple-element.163) | copy-start | bytes 24580
  64.4 77.1 %copy-start.124 = (bf16[64,1,64]{2,0,1:T(8,128)(2,1)}, bf16[64,1,64]{2,0,1:T(8,128)(2,1)S(1)}, u32[]{:S(2)}) copy-start(bf16[64,1,64]{2,0,1:T(8,128)(2,1)S(1)} %get-tuple-element.164) | copy-start | bytes 24580
  64.4 77.3 %copy-start.118 = (bf16[64,1,64]{2,0,1:T(8,128)(2,1)}, bf16[64,1,64]{2,0,1:T(8,128)(2,1)S(1)}, u32[]{:S(2)}) copy-start(bf16[64,1,64]{2,0,1:T(8,128)(2,1)S(1)} %get-tuple-element.165) | copy-start | bytes 24580
  64.4 77.3 %copy-start.120 = (bf16[64,1,64]{2,0,1:T(8,128)(2,1)}, bf16[64,1,64]{2,0,1:T(8,128)(2,1)S(1)}, u32[]{:S(2)}) copy-start(bf16[64,1,64]{2,0,1:T(8,128)(2,1)S(1)} %get-tuple-element.166) | copy-start | bytes 24580
  64.4 80.4 %copy-start.114 = (bf16[64,1,64]{2,0,1:T(8,128)(2,1)}, bf16[64,1,64]{2,0,1:T(8,128)(2,1)S(1)}, u32[]{:S(2)}) copy-start(bf16[64,1,64]{2,0,1:T(8,128)(2,1)S(1)} %get-tuple-element.110) | copy-start | bytes 24580
  64.4 80.4 %copy-start.116 = (bf16[64,1,64]{2,0,1:T(8,128)(2,1)}, bf16[64,1,64]{2,0,1:T(8,128)(2,1)S(1)}, u32[]{:S(2)}) copy-start(bf16[64,1,64]{2,0,1:T(8,128)(2,1)S(1)} %get-tuple-element.111) | copy-start | bytes 24580
  136.3 54.5 %copy-start.49 = (bf16[5,8,8,256]{3,2,0,1:T(8,128)(2,1)}, bf16[5,8,8,256]{3,2,0,1:T(8,128)(2,1)S(1)}, u32[]{:S(2)}) copy-start(bf16[5,8,8,256]{3,2,0,1:T(8,128)(2,1)S(1)} %copy.76) | copy-start | bytes 491524
  142.0 57.6 %copy-start.43 = (f32[5,64,64]{1,2,0:T(8,128)}, f32[5,64,64]{1,2,0:T(8,128)S(1)}, u32[]{:S(2)}) copy-start(f32[5,64,64]{1,2,0:T(8,128)S(1)} %get-tuple-element.170) | copy-start | bytes 245764
  142.5 57.0 %copy-start.51 = (bf16[5,8,8,256]{3,2,0,1:T(8,128)(2,1)}, bf16[5,8,8,256]{3,2,0,1:T(8,128)(2,1)S(1)}, u32[]{:S(2)}) copy-start(bf16[5,8,8,256]{3,2,0,1:T(8,128)(2,1)S(1)} %copy.75) | copy-start | bytes 491524
  144.7 54.9 %copy-start.73 = (f32[64,5,128]{2,0,1:T(8,128)}, f32[64,5,128]{2,0,1:T(8,128)S(1)}, u32[]{:S(2)}) copy-start(f32[64,5,128]{2,0,1:T(8,128)S(1)} %slice.253) | copy-start | bytes 491524
  144.8 55.4 %copy-start.82 = (f32[64,5,64]{2,0,1:T(8,128)}, f32[64,5,64]{2,0,1:T(8,128)S(1)}, u32[]{:S(2)}) copy-start(f32[64,5,64]{2,0,1:T(8,128)S(1)} %get-tuple-element.98) | copy-start | bytes 245764
  144.8 55.4 %copy-start.83 = (f32[64,5,64]{2,0,1:T(8,128)}, f32[64,5,64]{2,0,1:T(8,128)S(1)}, u32[]{:S(2)}) copy-start(f32[64,5,64]{2,0,1:T(8,128)S(1)} %get-tuple-element.99) | copy-start | bytes 245764
  145.2 55.1 %copy-start.46 = (f32[5,64,64]{1,2,0:T(8,128)}, f32[5,64,64]{1,2,0:T(8,128)S(1)}, u32[]{:S(2)}) copy-start(f32[5,64,64]{1,2,0:T(8,128)S(1)} %get-tuple-element.172) | copy-start | bytes 245764
  145.5 55.3 %copy-start.63 = (bf16[5,8,8,256]{3,2,0,1:T(8,128)(2,1)}, bf16[5,8,8,256]{3,2,0,1:T(8,128)(2,1)S(1)}, u32[]{:S(2)}) copy-start(bf16[5,8,8,256]{3,2,0,1:T(8,128)(2,1)S(1)} %copy.74) | copy-start | bytes 491524
  190.9 71.6 %copy-start.105 = (f32[2560]{0:T(1024)S(1)}, f32[2560]{0:T(1024)}, u32[]{:S(2)}) copy-start(f32[2560]{0:T(1024)} %param.19) | copy-start | bytes 30724
  190.9 172.1 %copy-start.100 = (f32[3840]{0:T(1024)S(1)}, f32[3840]{0:T(1024)}, u32[]{:S(2)}) copy-start(f32[3840]{0:T(1024)} %param.21) | copy-start | bytes 46084
  199.6 163.4 %all-gather.13.cloned.1.call-start = ((), (), s32[]{:S(2)}) async-start(), calls=%async_computation.9 | async-start | bytes 20889600 | tf_op jit(solution)/shard_map/all_gather | solution.py:88
  200.2 267.0 %all-gather.15.cloned.1.call-start = ((), (), s32[]{:S(2)}) async-start(), calls=%async_computation.10 | async-start | bytes 20889600 | tf_op jit(solution)/shard_map/all_gather | solution.py:89
  200.8 370.7 %all-gather.17.cloned.1.call-start = ((), (), s32[]{:S(2)}) async-start(), calls=%async_computation.11 | async-start | bytes 20889600 | tf_op jit(solution)/shard_map/all_gather | solution.py:91
  201.6 550.9 %all-reduce.12.cloned.1.call-start = ((), (), s32[]{:S(2)}) async-start(), calls=%async_computation.19 | async-start | bytes 3932160 | tf_op jit(solution)/shard_map/psum | solution.py:38
  261.3 112.9 %copy-start.149 = (f32[64]{0:T(128)}, f32[64]{0:T(128)S(1)}, u32[]{:S(2)}) copy-start(f32[64]{0:T(128)S(1)} %get-tuple-element.158) | copy-start | bytes 772
  261.9 112.3 %copy-start.150 = (f32[64]{0:T(128)}, f32[64]{0:T(128)S(1)}, u32[]{:S(2)}) copy-start(f32[64]{0:T(128)S(1)} %get-tuple-element.160) | copy-start | bytes 772
  262.5 111.7 %copy-start.151 = (f32[64]{0:T(128)}, f32[64]{0:T(128)S(1)}, u32[]{:S(2)}) copy-start(f32[64]{0:T(128)S(1)} %get-tuple-element.162) | copy-start | bytes 772
  262.7 204.5 %copy-start.14 = (bf16[64,2560]{1,0:T(8,128)(2,1)}, bf16[64,2560]{1,0:T(8,128)(2,1)S(1)}, u32[]{:S(2)}) copy-start(bf16[64,2560]{1,0:T(8,128)(2,1)S(1)} %get-tuple-element.125) | copy-start | bytes 983044
  262.8 215.7 %copy-start.10 = (bf16[64,2560]{1,0:T(8,128)(2,1)}, bf16[64,2560]{1,0:T(8,128)(2,1)S(1)}, u32[]{:S(2)}) copy-start(bf16[64,2560]{1,0:T(8,128)(2,1)S(1)} %get-tuple-element.124) | copy-start | bytes 983044
  262.8 232.0 %copy-start.12 = (bf16[64,2560]{1,0:T(8,128)(2,1)}, bf16[64,2560]{1,0:T(8,128)(2,1)S(1)}, u32[]{:S(2)}) copy-start(bf16[64,2560]{1,0:T(8,128)(2,1)S(1)} %get-tuple-element.123) | copy-start | bytes 983044
  376.3 90.9 %copy-start.101 = (f32[3840]{0:T(1024)S(1)}, f32[3840]{0:T(1024)}, u32[]{:S(2)}) copy-start(f32[3840]{0:T(1024)} %param.23) | copy-start | bytes 46084
  494.7 76.8 %copy-start.4 = (bf16[3,64,2560]{2,1,0:T(8,128)(2,1)S(1)}, bf16[3,64,2560]{2,1,0:T(8,128)(2,1)}, u32[]{:S(2)}) copy-start(bf16[3,64,2560]{2,1,0:T(8,128)(2,1)} %param.27) | copy-start | bytes 2949124
  584.0 107.9 %copy-start.24 = (bf16[64,3840]{1,0:T(8,128)(2,1)}, bf16[64,3840]{1,0:T(8,128)(2,1)S(1)}, u32[]{:S(2)}) copy-start(bf16[64,3840]{1,0:T(8,128)(2,1)S(1)} %get-tuple-element.81) | copy-start | bytes 1474564
  610.7 95.2 %copy-start.26 = (bf16[64,3840]{1,0:T(8,128)(2,1)}, bf16[64,3840]{1,0:T(8,128)(2,1)S(1)}, u32[]{:S(2)}) copy-start(bf16[64,3840]{1,0:T(8,128)(2,1)S(1)} %get-tuple-element.78) | copy-start | bytes 1474564
  691.9 374.0 %all-reduce.10.cloned.1.call-start = ((), (), s32[]{:S(2)}) async-start(), calls=%async_computation.18 | async-start | bytes 7864320 | tf_op jit(solution)/shard_map/psum | solution.py:38
  733.1 32.3 %slice-start.5 = ((s8[6553600]{0:T(1024)(128)(4,1)}), s8[2359296]{0:T(1024)(128)(4,1)S(1)}, s32[]{:S(2)}) async-start(s8[6553600]{0:T(1024)(128)(4,1)} %bitcast.415), calls=%async_computation.26 | async-start | bytes 4718592
  774.2 33.9 %copy-start.41 = (f32[2560]{0:T(1024)S(1)}, f32[2560]{0:T(1024)}, u32[]{:S(2)}) copy-start(f32[2560]{0:T(1024)} %param.15) | copy-start | bytes 30724
  774.2 33.9 %copy-start.140 = (f32[64]{0:T(128)S(1)}, f32[64]{0:T(128)}, u32[]{:S(2)}) copy-start(f32[64]{0:T(128)} %copy-done.139) | copy-start | bytes 772
  774.3 34.8 %copy-start.138 = (f32[64]{0:T(128)S(1)}, f32[64]{0:T(128)}, u32[]{:S(2)}) copy-start(f32[64]{0:T(128)} %copy-done.137) | copy-start | bytes 772
  777.2 32.9 %copy-start.135 = (f32[64]{0:T(128)S(1)}, f32[64]{0:T(128)}, u32[]{:S(2)}) copy-start(f32[64]{0:T(128)} %copy-done.134) | copy-start | bytes 772
  780.2 366.1 %reduce-scatter.9.cloned.1.call-start = ((), (), s32[]{:S(2)}) async-start(), calls=%async_computation.13 | async-start | bytes 5570560 | tf_op jit(solution)/shard_map/reduce_scatter | solution.py:216
  813.4 332.8 %reduce-scatter.7.cloned.1.call-start = ((), (), s32[]{:S(2)}) async-start(), calls=%async_computation.12 | async-start | bytes 13926400 | tf_op jit(solution)/shard_map/reduce_scatter | solution.py:215
  824.5 436.7 %reduce-scatter.11.cloned.1.call-start = ((), (), s32[]{:S(2)}) async-start(), calls=%async_computation.14 | async-start | bytes 13926400 | tf_op jit(solution)/shard_map/reduce_scatter | solution.py:219
  836.0 808.9 %reduce-scatter.13.cloned.1.call-start = ((), (), s32[]{:S(2)}) async-start(), calls=%async_computation.15 | async-start | bytes 41779200 | tf_op jit(solution)/shard_map/reduce_scatter | solution.py:217
  909.6 1119.4 %reduce-scatter.15.cloned.1.call-start = ((), (), s32[]{:S(2)}) async-start(), calls=%async_computation.16 | async-start | bytes 41779200 | tf_op jit(solution)/shard_map/reduce_scatter | solution.py:218
  982.2 1430.4 %reduce-scatter.17.cloned.1.call-start = ((), (), s32[]{:S(2)}) async-start(), calls=%async_computation.17 | async-start | bytes 41779200 | tf_op jit(solution)/shard_map/reduce_scatter | solution.py:220
  1060.9 76.8 %copy-start.7 = (f32[64,2560]{1,0:T(8,128)S(1)}, f32[64,2560]{1,0:T(8,128)}, u32[]{:S(2)}) copy-start(f32[64,2560]{1,0:T(8,128)} %copy-done.6) | copy-start | bytes 1966084
  (114 other events, 997.0 us)
Sparse Core Ops, SparseCore 0:
  10.3 45.8 all-gather.6
  58.5 62.0 all-gather.8
  122.9 61.9 all-gather.10
  199.7 58.9 all-reduce.13
  260.3 102.6 all-gather.12
  364.5 102.6 all-gather.14
  468.9 102.6 all-gather.16
  692.0 60.4 all-reduce.11
  780.3 112.2 all-reduce.9
  897.4 78.3 reduce-scatter.8
  981.1 137.8 reduce-scatter.6
  1123.4 137.6 reduce-scatter.10
  1266.6 378.2 reduce-scatter.12
  1650.2 378.7 reduce-scatter.14
  2034.3 378.2 reduce-scatter.16
where the time goes:
time: 2430 us; the launch traced here: 2420 us
  waiting for transfers between devices  1730 us (71%)
  matrix products  528 us (22%)
  blocking collectives  87.2 us (4%)
  other arithmetic  33 us (1%)
    reduce_scatter x1, waiting for transfers between devices, shards(): lax.psum_scatter(ffn_total[1], 'dp', scatter_dimension=0, tiled=True)  384 us
    reduce_scatter x1, waiting for transfers between devices, shards(): lax.psum_scatter(ffn_total[0], 'dp', scatter_dimension=0, tiled=True)  384 us
    reduce_scatter x1, waiting for transfers between devices, shards(): lax.psum_scatter(ffn_total[2], 'dp', scatter_dimension=1, tiled=True)  384 us
    reduce_scatter x1, waiting for transfers between devices, shards(): lax.psum_scatter(attn_total[2], 'dp', scatter_dimension=1, tiled=True)  115 us
    all_gather x1, waiting for transfers between devices, shards(): lax.all_gather(w_gate, 'dp', axis=0, tiled=True)  100 us
    all_gather x1, waiting for transfers between devices, shards(): lax.all_gather(w_up, 'dp', axis=0, tiled=True)  86.4 us
    dot_general x3, matrix products, shards(): jnp.einsum('tf,td->fd', inner_b, grad_branch, preferred_element_type=jnp....  77.3 us
    psum x3, waiting for transfers between devices, model_sum(): return lax.psum(values, 'mp')  75.1 us
  transfers between devices with their start and end apart: 15, of which 12 were waited for; matrix products, arithmetic and copies ran while one was open for 17% of the time, Pallas kernels for 0%

commit v1 on v0

v1 whole, which is shorter than its diff:
```python
from functools import partial

import jax
import jax.numpy as jnp
from jax import lax
from jax.sharding import PartitionSpec as P

EPS = 1e-06
F32 = jnp.float32
BF16 = jnp.bfloat16


def positions(segment):
    count = segment.shape[0]
    index = jnp.arange(count, dtype=jnp.int32)
    fresh = jnp.concatenate([jnp.ones((1,), jnp.bool_), segment[1:] != segment[:-1]])
    starts = lax.cummax(jnp.where(fresh, index, 0), axis=0)
    return (index - starts).astype(F32)


def rotate(tensor, cosine, sine):
    quarter = cosine.shape[-1]
    front_half = tensor[..., :quarter]
    back_half = tensor[..., quarter : 2 * quarter]
    return jnp.concatenate(
        [
            front_half * cosine - back_half * sine,
            back_half * cosine + front_half * sine,
            tensor[..., 2 * quarter :],
        ],
        axis=-1,
    )


def inv_root(values):
    return lax.rsqrt(jnp.mean(values * values, axis=-1, keepdims=True) + EPS)


def norm_back(values, factor, gain, grad_norm):
    scaled = gain * grad_norm
    return factor * scaled - values * factor**3 * jnp.mean(scaled * values, axis=-1, keepdims=True)


def mm(left, right):
    return jnp.dot(left, right, preferred_element_type=F32)


def mm_nt(left, right):
    return lax.dot_general(left, right, (((1,), (1,)), ((), ())), preferred_element_type=F32)


def mm_tn(left, right):
    return lax.dot_general(left, right, (((0,), (0,)), ((), ())), preferred_element_type=F32)


class Grid:
    def __init__(self, total):
        self.z_count = total // 4
        spots = [(z, y, c) for z in range(self.z_count) for y in range(2) for c in range(2)]
        at = lambda z, y, c: (z * 2 + y) * 2 + c
        self.swap_y = [(at(z, y, c), at(z, 1 - y, c)) for z, y, c in spots]
        self.swap_c = [(at(z, y, c), at(z, y, 1 - c)) for z, y, c in spots]
        self.ring = [(at(z, y, c), at((z + 1) % self.z_count, y, c)) for z, y, c in spots]
        self.flips = []
        step = 1
        while step < self.z_count:
            self.flips.append([(at(z, y, c), at(z ^ step, y, c)) for z, y, c in spots])
            step *= 2
        self.lines = [
            [at(z, y, c) for z in range(self.z_count)] for y in range(2) for c in range(2)
        ]
        self.sheets = [
            [at(z, y, c) for z in range(self.z_count) for c in range(2)] for y in range(2)
        ]
        index = lax.axis_index("dp")
        self.c = index % 2
        self.y = (index // 2) % 2
        self.z = index // 4
        self.x = lax.axis_index("mp")

    def over_y(self, value):
        return lax.ppermute(value, "dp", self.swap_y)

    def over_c(self, value):
        return lax.ppermute(value, "dp", self.swap_c)

    def over_x(self, value):
        return lax.ppermute(value, "mp", [(0, 1), (1, 0)])

    def next_z(self, value):
        return lax.ppermute(value, "dp", self.ring)

    def sum_dp(self, value):
        value = value + self.over_c(value)
        value = value + self.over_y(value)
        for flip in self.flips:
            value = value + lax.ppermute(value, "dp", flip)
        return value


def pair(index, mine, other, axis):
    return jnp.where(
        index == 0, jnp.stack([mine, other], axis=axis), jnp.stack([other, mine], axis=axis)
    )


def take(value, index, axis):
    return lax.dynamic_index_in_dim(value, index, axis, keepdims=False)


def gather_rows(grid, shard):
    rows, width = shard.shape
    count = grid.z_count
    whole = jnp.zeros((count, 4 * rows, width), shard.dtype)
    slot = shard
    for step in range(count):
        across = grid.over_y(slot)
        coming = grid.next_z(slot) if step + 1 < count else None
        lines = pair(grid.y, slot, across, 0)
        beside = grid.over_c(lines)
        block = pair(grid.c, lines, beside, 1).reshape(1, 4 * rows, width)
        place = lax.rem(grid.z - step + count, count)
        whole = lax.dynamic_update_slice(whole, block, (place, 0, 0))
        slot = coming
    return whole.reshape(count * 4 * rows, width)


def scatter_rows(grid, whole):
    count = grid.z_count
    rows = whole.shape[0] // (4 * count)
    width = whole.shape[1]
    parts = whole.reshape(count, 2, 2, rows, width)
    got = grid.over_c(take(parts, 1 - grid.c, 2).astype(BF16))
    parts = take(parts, grid.c, 2).astype(F32) + got.astype(F32)
    got = grid.over_y(take(parts, 1 - grid.y, 1).astype(BF16))
    parts = (take(parts, grid.y, 1) + got.astype(F32)).astype(BF16)
    got = lax.all_to_all(parts, "dp", 0, 0, axis_index_groups=grid.lines, tiled=True)
    return jnp.sum(got.astype(F32), axis=0)


def spread_columns(grid, shard):
    rows, width = shard.shape
    count = grid.z_count
    mine = lax.all_to_all(shard, "dp", 1, 0, axis_index_groups=grid.sheets, tiled=True)
    mine = mine.reshape(count, 2 * rows, width // (2 * count))
    other = grid.over_y(mine)
    return pair(grid.y, mine, other, 1).reshape(4 * count * rows, width // (2 * count))


def collect_columns(grid, whole):
    count = grid.z_count
    rows = whole.shape[0] // (4 * count)
    width = whole.shape[1]
    parts = whole.reshape(count, 2, 2 * rows, width)
    got = grid.over_y(take(parts, 1 - grid.y, 1).astype(BF16))
    parts = (take(parts, grid.y, 1).astype(F32) + got.astype(F32)).astype(BF16)
    parts = parts.reshape(2 * count * rows, width)
    return lax.all_to_all(parts, "dp", 0, 1, axis_index_groups=grid.sheets, tiled=True).astype(F32)


def gather_tokens(grid, half):
    count = grid.z_count
    whole = jnp.zeros((count, 2, 2) + half.shape, half.dtype)
    slot = half
    for step in range(count):
        across = grid.over_x(slot)
        coming = grid.next_z(slot) if step + 1 < count else None
        both = pair(grid.x, slot, across, 0)
        beside = grid.over_c(both)
        block = pair(grid.c, both, beside, 0)[None]
        place = lax.rem(grid.z - step + count, count)
        whole = lax.dynamic_update_slice(whole, block, (place,) + (0,) * (block.ndim - 1))
        slot = coming
    return whole.reshape(-1, half.shape[-1])


def scatter_tokens(grid, whole, tokens):
    count = grid.z_count
    parts = whole.reshape(count, 2, 2, tokens, whole.shape[-1])
    got = grid.over_c(take(parts, 1 - grid.c, 1))
    parts = take(parts, grid.c, 1).astype(F32) + got.astype(F32)
    got = grid.over_x(take(parts, 1 - grid.x, 1).astype(BF16))
    parts = (take(parts, grid.x, 1) + got.astype(F32)).astype(BF16)
    got = lax.all_to_all(parts, "dp", 0, 0, axis_index_groups=grid.lines, tiled=True)
    return jnp.sum(got.astype(F32), axis=0)


def shards(
    inputs,
    gain_attn,
    w_query,
    w_keyval,
    w_output,
    gain_mlp,
    w_gate,
    b_gate,
    w_up,
    b_up,
    w_down,
    b_down,
    segment_ids,
    cotangent,
    total,
):
    grid = Grid(total)
    count = grid.z_count
    micro, length, width = inputs.shape
    tokens = micro * length
    head_dim = w_keyval.shape[1] // 2
    heads = w_query.shape[1] // head_dim
    scale = head_dim ** (-0.5)

    def halves(value):
        value = value.reshape(micro, 2, length // 2, value.shape[-1])
        return tuple(take(value, i, 1).reshape(tokens // 2, -1) for i in (grid.x, 1 - grid.x))

    def join(mine, other):
        shape = (micro, length // 2, mine.shape[-1])
        return pair(grid.x, mine.reshape(shape), other.reshape(shape), 1).reshape(tokens, -1)

    keyval_half = lax.dynamic_slice_in_dim(w_keyval, grid.x * head_dim, head_dim, 1)
    w_qkv = gather_rows(grid, jnp.concatenate([w_query, keyval_half], axis=1))
    w_out = gather_rows(grid, w_output.T)
    wq, wkv = w_qkv[:, : heads * head_dim], w_qkv[:, heads * head_dim :]

    wg = spread_columns(grid, w_gate)
    wu = spread_columns(grid, w_up)
    wd = spread_columns(grid, w_down.T)
    hidden = wg.shape[1]
    place = (2 * grid.z + grid.c) * hidden
    bg = lax.dynamic_slice_in_dim(b_gate, place, hidden, 0)
    bu = lax.dynamic_slice_in_dim(b_up, place, hidden, 0)

    segment = segment_ids.reshape(micro, length)
    offsets = jax.vmap(positions)(segment).reshape(tokens)
    quarter = head_dim // 4
    freqs = 10000.0 ** (-jnp.arange(quarter, dtype=F32) / quarter)
    angle = offsets[:, None] * freqs[None, :]
    cosine, sine = jnp.cos(angle), jnp.sin(angle)
    index = jnp.arange(tokens, dtype=jnp.int32)
    seg = segment.reshape(tokens)
    allowed = (
        (seg[:, None] == seg[None, :])
        & (index[:, None] // length == index[None, :] // length)
        & (index[None, :] <= index[:, None])
    )
    hidden_x = inputs.reshape(tokens, width).astype(F32)
    factor_one = inv_root(hidden_x)
    normed = (hidden_x * factor_one * gain_attn).astype(BF16)
    queries = mm(normed, wq).reshape(tokens, heads, head_dim).transpose(1, 0, 2)
    rot_query = (rotate(queries, cosine, sine) * scale).astype(BF16)
    rot_query = rot_query.reshape(heads * tokens, head_dim)
    keyval = mm(normed, wkv)
    keyval = jnp.where(grid.x == 0, rotate(keyval, cosine, sine), keyval).astype(BF16)
    keyval_other = grid.over_x(keyval)
    rot_key = jnp.where(grid.x == 0, keyval, keyval_other)
    values_in = jnp.where(grid.x == 0, keyval_other, keyval)
    scores = mm_nt(rot_query, rot_key).reshape(heads, tokens, tokens)
    scores = jnp.where(allowed[None], scores, -1e30)
    row_max = jnp.max(scores, axis=-1, keepdims=True)
    expon = jnp.exp(scores - row_max)
    row_total = jnp.sum(expon, axis=-1, keepdims=True)
    probs = expon / row_total
    probs_b = probs.astype(BF16).reshape(heads * tokens, tokens)
    mixed = mm(probs_b, values_in).reshape(heads, tokens, head_dim)
    mixed_b = mixed.astype(BF16).transpose(1, 0, 2).reshape(tokens, heads * head_dim)
    attended = mm_nt(mixed_b, w_out)
    mine, other = halves(attended)
    attended = mine + grid.over_x(other.astype(BF16)).astype(F32)
    x_half = halves(hidden_x)[0]
    residual = x_half + attended
    factor_two = inv_root(residual)
    normed_two = (residual * factor_two * gain_mlp).astype(BF16)

    dy_half = halves(cotangent.reshape(tokens, width))[0]
    dy_all = gather_tokens(grid, dy_half)
    normed_all = gather_tokens(grid, normed_two)
    gate_pre = mm(normed_all, wg) + bg
    up_pre = mm(normed_all, wu) + bu
    gelu_out, gelu_pull = jax.vjp(partial(jax.nn.gelu, approximate=True), gate_pre)
    inner_b = (gelu_out * up_pre).astype(BF16)
    branch_all = mm_nt(inner_b, wd).astype(BF16)
    grad_inner = mm(dy_all, wd)
    grad_gate = gelu_pull(grad_inner * up_pre)[0].astype(BF16)
    grad_up = (grad_inner * gelu_out).astype(BF16)
    grad_norm_all = (mm_nt(grad_gate, wg) + mm_nt(grad_up, wu)).astype(BF16)
    grad_norm_two = scatter_tokens(grid, grad_norm_all, tokens // 2)
    branch = scatter_tokens(grid, branch_all, tokens // 2) + b_down
    outputs = (residual + branch).astype(BF16)
    outputs = join(outputs, grid.over_x(outputs))
    down_grad = collect_columns(grid, mm_tn(dy_all, inner_b)).T
    gate_grad = collect_columns(grid, mm_tn(normed_all, grad_gate))
    up_grad = collect_columns(grid, mm_tn(normed_all, grad_up))

    grad_out = dy_half.astype(F32)
    gain_mlp_term = jnp.sum(grad_norm_two * residual * factor_two, axis=0)
    grad_resid = grad_out + norm_back(residual, factor_two, gain_mlp, grad_norm_two)
    grad_resid_b = grad_resid.astype(BF16)
    grad_resid_b = join(grad_resid_b, grid.over_x(grad_resid_b))
    out_grad = scatter_rows(grid, mm_tn(grad_resid_b, mixed_b)).T
    grad_mixed = mm(grad_resid_b, w_out).astype(BF16)
    grad_mixed = grad_mixed.reshape(tokens, heads, head_dim).transpose(1, 0, 2)
    grad_mixed = grad_mixed.reshape(heads * tokens, head_dim)
    grad_values = mm_tn(probs_b, grad_mixed)
    grad_probs = mm_nt(grad_mixed, values_in).reshape(heads, tokens, tokens)
    row_delta = jnp.sum(probs * grad_probs, axis=-1, keepdims=True)
    grad_scores = (probs * (grad_probs - row_delta)).astype(BF16)
    grad_scores = grad_scores.reshape(heads * tokens, tokens)
    grad_rq = mm(grad_scores, rot_key).reshape(heads, tokens, head_dim) * scale
    grad_query = rotate(grad_rq, cosine, -sine).astype(BF16)
    grad_query = grad_query.transpose(1, 0, 2).reshape(tokens, heads * head_dim)
    grad_key = rotate(mm_tn(grad_scores, rot_query), cosine, -sine)
    grad_own = jnp.where(grid.x == 0, grad_key, grad_values)
    grad_other = jnp.where(grid.x == 0, grad_values, grad_key)
    grad_keyval = (grad_own + grid.over_x(grad_other)).astype(BF16)
    grad_qkv = jnp.concatenate([grad_query, grad_keyval], axis=1)
    qkv_grad = scatter_rows(grid, mm_tn(normed, grad_qkv))
    mine, other = halves(mm_nt(grad_qkv, w_qkv))
    grad_normed = mine + grid.over_x(other.astype(BF16)).astype(F32)
    factor_half = halves(factor_one)[0]
    gain_attn_term = jnp.sum(grad_normed * x_half * factor_half, axis=0)
    grad_input = grad_resid + norm_back(x_half, factor_half, gain_attn, grad_normed)
    grad_input = grad_input.astype(BF16)
    grad_input = join(grad_input, grid.over_x(grad_input))
    query_grad = qkv_grad[:, : heads * head_dim]
    keyval_grad = qkv_grad[:, heads * head_dim :]
    keyval_grad = pair(grid.x, keyval_grad, grid.over_x(keyval_grad), 1)
    keyval_grad = keyval_grad.reshape(keyval_grad.shape[0], 2 * head_dim)

    wide = jnp.zeros((2, b_gate.shape[0]), F32)
    bias = jnp.stack(
        [jnp.sum(grad_gate.astype(F32), axis=0), jnp.sum(grad_up.astype(F32), axis=0)]
    )
    wide = lax.dynamic_update_slice(wide, bias, (0, place)).reshape(-1)
    bias_down_term = jnp.sum(grad_out, axis=0)
    early = jnp.concatenate([gain_mlp_term, bias_down_term])
    early = jnp.concatenate([early + grid.over_x(early), wide])
    early = grid.sum_dp(early)
    gain_attn_grad = gain_attn_term + grid.over_x(gain_attn_term)
    gain_attn_grad = grid.sum_dp(gain_attn_grad)
    ffn = b_gate.shape[0]
    return (
        outputs.reshape(inputs.shape),
        grad_input.reshape(inputs.shape),
        gain_attn_grad,
        query_grad,
        keyval_grad,
        out_grad,
        early[:width],
        gate_grad,
        early[2 * width : 2 * width + ffn],
        up_grad,
        early[2 * width + ffn :],
        down_grad,
        early[width : 2 * width],
    )


def solution(mesh):
    in_specs = (
        P(None, "dp", None),
        P(),
        P("dp", "mp"),
        P("dp", None),
        P("mp", "dp"),
        P(),
        P("dp", "mp"),
        P("mp"),
        P("dp", "mp"),
        P("mp"),
        P("mp", "dp"),
        P(),
        P(None, "dp", None),
        P(None, "dp", None),
    )
    out_specs = (
        P(None, "dp", None),
        P(None, "dp", None),
        P(),
        P("dp", "mp"),
        P("dp", None),
        P("mp", "dp"),
        P(),
        P("dp", "mp"),
        P("mp"),
        P("dp", "mp"),
        P("mp"),
        P("mp", "dp"),
        P(),
    )
    body = partial(shards, total=mesh.shape["dp"])
    return jax.shard_map(body, mesh=mesh, in_specs=in_specs, out_specs=out_specs, check_vma=False)
```

time: 2430 us -> 890 us (0.37)
  waiting for transfers between devices: 1730 us -> 327 us
  matrix products: 528 us -> 105 us
  local copies, waits for them, and re-layouts: 19.7 us -> 161 us
  other arithmetic: 33 us -> 160 us
  starting transfers between devices: 1.45 us -> 124 us
  blocking collectives: 87.2 us -> 0 us
    reduce_scatter x6 -> x0, waiting for transfers between devices: 1270 us -> none  [the longest x1 384 us: shards(): lax.psum_scatter(ffn_total[1], 'dp', scatter_dimension=0, tiled=True)]
    dot_general x72 -> x21, matrix products: 528 us -> 103 us  [the longest x8 36.8 us: mm(): return jnp.dot(left, right, preferred_element_type=F32)]
    all_gather x6 -> x0, waiting for transfers between devices: 388 us -> none  [the longest x1 100 us: shards(): lax.all_gather(w_gate, 'dp', axis=0, tiled=True)]
    ppermute x0 -> x76, waiting for transfers between devices: none -> 279 us  [the longest x20 131 us: over_x(): return lax.ppermute(value, 'mp', [(0, 1), (1, 0)])]
    psum x2 -> x0, blocking collectives: 87.2 us -> none  [the longest x1 63.7 us: shards(): small = lax.psum((small[0], small[1], small[2], small[3], small[4]), 'dp')]
    ppermute x0 -> x76, starting transfers between devices: none -> 79.7 us  [the longest x20 22.2 us: over_x(): return lax.ppermute(value, 'mp', [(0, 1), (1, 0)])]
    psum x3 -> x0, waiting for transfers between devices: 75.1 us -> none  [model_sum(): return lax.psum(values, 'mp')]
    select_n x0 -> x39, other arithmetic: none -> 56 us  [the longest x37 56 us: pair(): jnp.where(index == 0, jnp.stack([mine, other], axis=axis), jnp.stack([oth...]
  transfers between devices with their start and end apart: 15 -> 86, of which waited for: 12 -> 32; matrix products, arithmetic and copies ran while one was open for 17% -> 39% of each run, Pallas kernels for 0% -> 0%
where the time goes in v1:
time: 890 us; the launch traced here: 879 us
  waiting for transfers between devices  327 us (37%)
  local copies, waits for them, and re-layouts  161 us (18%)
  other arithmetic  160 us (18%)
  starting transfers between devices  124 us (14%)
  matrix products  105 us (12%)
    ppermute x20, waiting for transfers between devices, over_x(): return lax.ppermute(value, 'mp', [(0, 1), (1, 0)])  131 us
    ppermute x18, waiting for transfers between devices, over_y(): return lax.ppermute(value, 'dp', self.swap_y)  75.5 us
    select_n x37, other arithmetic, pair(): jnp.where(index == 0, jnp.stack([mine, other], axis=axis), jnp.stack([oth...  56 us
    ppermute x12, waiting for transfers between devices, next_z(): return lax.ppermute(value, 'dp', self.ring)  48.2 us
    dot_general x8, matrix products, mm(): return jnp.dot(left, right, preferred_element_type=F32)  36.8 us
    dot_general x6, matrix products, mm_nt(): lax.dot_general(left, right, (((1,), (1,)), ((), ())), preferred_element_...  35.3 us
    dot_general x7, matrix products, mm_tn(): lax.dot_general(left, right, (((0,), (0,)), ((), ())), preferred_element_...  31.3 us
    all_to_all x2, waiting for transfers between devices, scatter_tokens(): lax.all_to_all(parts, 'dp', 0, 0, axis_index_groups=grid.lines, tiled=True)  27.2 us
  transfers between devices with their start and end apart: 86, of which 32 were waited for; matrix products, arithmetic and copies ran while one was open for 39% of the time, Pallas kernels for 0%

profile of v1, /device:TPU:0, one launch (start us, length us, event | category | flops | bytes accessed | tf_op | source)
XLA Modules:
  0.0 878.8 jit_solution(10446629381413619861)
XLA Ops:
  15.3 4.4 all-to-all-start
  52.6 10.9 %collective-permute-done.43 = bf16[96,2560]{1,0:T(8,128)(2,1)S(1)} collective-permute-done((bf16[96,2560]{1,0:T(8,128)(2,1)S(1)}, bf16[96,2560]{1,0:T(8,128)(2,1)S(1)}, u32[]{:S(2)}, u32[]{:S(2)}) %collective-permute-start.43) | collective-permute-done | bytes 491552 | tf_op jit(solution)/shard_map/ppermute | solution.py:91
  68.0 6.4 collective-permute-done.44
  75.5 5.4 collective-permute-start.5
  94.7 8.1 collective-permute-done.46
  106.4 10.3 %collective-permute-done.47 = bf16[96,2560]{1,0:T(8,128)(2,1)S(1)} collective-permute-done((bf16[96,2560]{1,0:T(8,128)(2,1)}, bf16[96,2560]{1,0:T(8,128)(2,1)S(1)}, u32[]{:S(2)}, u32[]{:S(2)}) %collective-permute-start.47) | collective-permute-done | bytes 491552 | tf_op jit(solution)/shard_map/ppermute | solution.py:88
  129.9 5.6 collective-permute-done.6
  142.6 3.9 broadcast.642.clone.1
  151.5 4.9 all-to-all-start.1
  174.8 5.9 collective-permute-done.50
  189.1 5.3 all-to-all-done.1
  194.5 4.0 all-to-all-start.2
  215.8 14.7 %all-to-all-done.2 = bf16[160,8,480]{2,0,1:T(8,128)(2,1)S(1)} async-done(((bf16[160,8,480]{2,0,1:T(8,128)(2,1)}), bf16[160,8,480]{2,0,1:T(8,128)(2,1)S(1)}, u32[]{:S(2)}, u32[]{:S(2)}) %all-to-all-start.2) | async-done | bytes 1228832 | tf_op jit(solution)/shard_map/all_to_all | solution.py:144
  241.2 6.0 slice_bitcast_fusion
  248.9 9.5 %copy.220 = bf16[1280,2560]{1,0:T(8,128)(2,1)} copy(bf16[1280,2560]{0,1:T(8,128)(2,1)} %slice_bitcast_fusion) | data formatting | bytes 13107200 | tf_op jit(solution)/shard_map/dot_general | solution.py:45
  258.4 5.1 convolution_bitcast_fusion
  274.7 5.3 fusion.120
  281.8 5.5 maximum_select_fusion
  287.7 6.9 collective-permute-done.37
  302.1 11.1 %collective-permute-done.26 = bf16[96,2560]{1,0:T(8,128)(2,1)S(1)} collective-permute-done((bf16[96,2560]{1,0:T(8,128)(2,1)S(1)}, bf16[96,2560]{1,0:T(8,128)(2,1)S(1)}, u32[]{:S(2)}, u32[]{:S(2)}) %collective-permute-start.26) | collective-permute-done | bytes 491552 | tf_op jit(solution)/shard_map/ppermute | solution.py:91
  315.1 11.9 %collective-permute-done.29 = bf16[96,2560]{1,0:T(8,128)(2,1)S(1)} collective-permute-done((bf16[96,2560]{1,0:T(8,128)(2,1)S(1)}, bf16[96,2560]{1,0:T(8,128)(2,1)S(1)}, u32[]{:S(2)}, u32[]{:S(2)}) %collective-permute-start.29) | collective-permute-done | bytes 491552 | tf_op jit(solution)/shard_map/ppermute | solution.py:91
  328.9 9.1 %collective-permute-done.30 = bf16[96,2560]{1,0:T(8,128)(2,1)S(1)} collective-permute-done((bf16[96,2560]{1,0:T(8,128)(2,1)S(1)}, bf16[96,2560]{1,0:T(8,128)(2,1)S(1)}, u32[]{:S(2)}, u32[]{:S(2)}) %collective-permute-start.30) | collective-permute-done | bytes 491552 | tf_op jit(solution)/shard_map/ppermute | solution.py:88
  339.1 5.0 collective-permute-done.32
  346.1 10.8 %collective-permute-done.33 = bf16[96,2560]{1,0:T(8,128)(2,1)S(1)} collective-permute-done((bf16[96,2560]{1,0:T(8,128)(2,1)S(1)}, bf16[96,2560]{1,0:T(8,128)(2,1)S(1)}, u32[]{:S(2)}, u32[]{:S(2)}) %collective-permute-start.33) | collective-permute-done | bytes 491552 | tf_op jit(solution)/shard_map/ppermute | solution.py:88
  360.5 5.9 convolution_add_fusion
  366.4 5.8 convolution_add_fusion.1
  372.2 11.2 %convert_reduce_fusion.4 = (f32[480]{0:T(512)}, bf16[1536,480]{0,1:T(8,128)(2,1)S(1)}, f32[480]{0:T(512)}, bf16[1536,480]{0,1:T(8,128)(2,1)S(1)}, bf16[1536,480]{0,1:T(8,128)(2,1)}) fusion(f32[1536,480]{0,1:T(8,128)} %convolution_add_fusion.1, f32[1536,480]{0,1:T(8,128)} %convolution_add_fusion, bf16[1536,2560]{1,0:T(8,128)(2,1)} %bitcast.156, ...), kind=kOutput, calls=%fused_computation.41 | convolution fusion | flops 3796990976 | bytes 20647680 | tf_op jit(solution)/shard_map/dot_general | solution.py:45
  383.4 7.9 fusion.121
  391.3 9.8 %add_convert_fusion = bf16[1536,2560]{1,0:T(8,128)(2,1)} fusion(f32[1536,2560]{1,0:T(8,128)} %fusion.121, bf16[1536,480]{0,1:T(8,128)(2,1)S(1)} %get-tuple-element.22, bf16[2560,480]{1,0:T(8,128)(2,1)S(1)} %bitcast.485), kind=kOutput, calls=%fused_computation.1 | convolution fusion | flops 3782737920 | bytes 27525120 | tf_op jit(solution)/shard_map/dot_general | solution.py:49
  401.2 4.4 dynamic-slice_bitcast_fusion
  406.1 5.1 convolution_convert_fusion
  415.5 4.6 convert_add_fusion
  422.6 6.2 convert_add_fusion.1
  428.9 36.8 %collective-permute-done.53 = bf16[4,96,2560]{2,1,0:T(8,128)(2,1)S(1)} collective-permute-done((bf16[4,96,2560]{2,1,0:T(8,128)(2,1)S(1)}, bf16[4,96,2560]{2,1,0:T(8,128)(2,1)S(1)}, u32[]{:S(2)}, u32[]{:S(2)}) %collective-permute-start.53) | collective-permute-done | bytes 1966112 | tf_op jit(solution)/shard_map/ppermute | solution.py:88
  474.0 43.9 %collective-permute-done.39 = bf16[4,96,2560]{2,1,0:T(8,128)(2,1)S(1)} collective-permute-done((bf16[4,96,2560]{2,1,0:T(8,128)(2,1)S(1)}, bf16[4,96,2560]{2,1,0:T(8,128)(2,1)S(1)}, u32[]{:S(2)}, u32[]{:S(2)}) %collective-permute-start.39) | collective-permute-done | bytes 1966112 | tf_op jit(solution)/shard_map/ppermute | solution.py:88
  517.9 4.0 fusion.4
  521.9 4.9 all-to-all-start.3
  530.0 10.7 %copy.264 = bf16[2560,1536]{1,0:T(8,128)(2,1)} copy(bf16[2560,1536]{0,1:T(8,128)(2,1)} %bitcast.223) | data formatting | bytes 15728640 | tf_op jit(solution)/shard_map/dot_general | solution.py:53
  544.0 27.2 %all-to-all-done.3 = bf16[4,96,2560]{2,1,0:T(8,128)(2,1)} async-done(((bf16[4,96,2560]{2,1,0:T(8,128)(2,1)}), bf16[4,96,2560]{2,1,0:T(8,128)(2,1)}, u32[]{:S(2)}, u32[]{:S(2)}) %all-to-all-start.3) | async-done | bytes 1966112 | tf_op jit(solution)/shard_map/all_to_all | solution.py:184
  575.6 5.7 fusion.31
  586.3 10.8 %copy.261 = bf16[2560,1536]{1,0:T(8,128)(2,1)} copy(bf16[2560,1536]{0,1:T(8,128)(2,1)} %bitcast.449) | data formatting | bytes 15728640 | tf_op jit(solution)/shard_map/dot_general | solution.py:53
  598.2 4.4 convolution_convert_fusion.1
  620.8 7.2 fusion.33
  629.9 3.9 fusion.14
  633.8 4.1 all-to-all-start.9
  637.9 10.3 %fusion.35 = f32[4,2,320,480]{3,2,1,0:T(8,128)} fusion(bf16[4,2,320,1536]{3,2,1,0:T(8,128)(2,1)} %bitcast.451, bf16[1536,480]{0,1:T(8,128)(2,1)} %copy-done.74), kind=kOutput, calls=%fused_computation.101 | convolution fusion | flops 3774873600 | bytes 14254080 | tf_op jit(solution)/shard_map/dot_general | solution.py:53
  648.3 12.3 %collective-permute-done.74 = bf16[4,320,480]{2,1,0:T(8,128)(2,1)} collective-permute-done((bf16[4,320,480]{2,1,0:T(8,128)(2,1)}, bf16[4,320,480]{2,1,0:T(8,128)(2,1)}, u32[]{:S(2)}, u32[]{:S(2)}) %collective-permute-start.74) | collective-permute-done | bytes 1228832 | tf_op jit(solution)/shard_map/ppermute | solution.py:82
  667.9 4.7 copy-done.3
  685.9 5.7 bitcast_add_fusion
  697.9 15.5 %collective-permute-done.73 = bf16[4,320,480]{2,1,0:T(8,128)(2,1)} collective-permute-done((bf16[4,320,480]{2,1,0:T(8,128)(2,1)}, bf16[4,320,480]{2,1,0:T(8,128)(2,1)}, u32[]{:S(2)}, u32[]{:S(2)}) %collective-permute-start.73) | collective-permute-done | bytes 1228832 | tf_op jit(solution)/shard_map/ppermute | solution.py:82
  717.0 5.1 all-to-all-start.7
  724.4 31.6 %collective-permute-done.70 = f32[12800]{0:T(1024)S(1)} collective-permute-done((f32[12800]{0:T(1024)S(1)}, f32[12800]{0:T(1024)S(1)}, u32[]{:S(2)}, u32[]{:S(2)}) %collective-permute-start.70) | collective-permute-done | bytes 51232 | tf_op jit(solution)/shard_map/ppermute | solution.py:82
  765.8 7.3 bitcast_add_fusion.1
  773.0 4.6 fusion.2
  777.6 4.6 all-to-all-start.5
  786.0 5.9 fusion.63
  799.7 4.1 reshape.2676
  806.8 4.1 reshape.2675
  814.0 4.1 reshape.2674
  821.9 3.9 fusion.6
  826.2 4.9 all-to-all-start.6
  840.2 16.6 %collective-permute-done.61 = f32[2560]{0:T(1024)S(1)} collective-permute-done((f32[2560]{0:T(1024)S(1)}, f32[2560]{0:T(1024)S(1)}, u32[]{:S(2)}, u32[]{:S(2)}) %collective-permute-start.61) | collective-permute-done | bytes 10272 | tf_op jit(solution)/shard_map/ppermute | solution.py:97
  856.8 4.7 collective-permute-start.62
  864.1 4.8 collective-permute-done.62
  (502 shorter events, 321.1 us)
Async XLA Ops:
  3.8 42.3 %collective-permute-start = (bf16[160,1536]{1,0:T(8,128)(2,1)}, bf16[160,1536]{1,0:T(8,128)(2,1)S(1)}, u32[]{:S(2)}, u32[]{:S(2)}) collective-permute-start(bf16[160,1536]{1,0:T(8,128)(2,1)} %get-tuple-element.39), channel_id=1, source_target_pairs={{0,4},{2,6},{4,0},{6,2},{8,12},{10,14},{12,8},{14,10},{16,20},{18,... | collective-permute-start | bytes 1474568 | tf_op jit(solution)/shard_map/ppermute | solution.py:82
  6.8 45.7 %collective-permute-start.2 = (bf16[160,1536]{1,0:T(8,128)(2,1)}, bf16[160,1536]{1,0:T(8,128)(2,1)}, u32[]{:S(2)}, u32[]{:S(2)}) collective-permute-start(bf16[160,1536]{1,0:T(8,128)(2,1)} %get-tuple-element.39), channel_id=1, source_target_pairs={{0,8},{2,10},{4,12},{6,14},{8,16},{10,18},{12,20},{14,22},{16,24},... | collective-permute-start | bytes 1474568 | tf_op jit(solution)/shard_map/ppermute | solution.py:91
  8.3 33.1 %collective-permute-start.12 = (bf16[160,1280]{1,0:T(8,128)(2,1)}, bf16[160,1280]{1,0:T(8,128)(2,1)}, u32[]{:S(2)}, u32[]{:S(2)}) collective-permute-start(bf16[160,1280]{1,0:T(8,128)(2,1)} %bitcast.524), channel_id=1, source_target_pairs={{0,4},{2,6},{4,0},{6,2},{8,12},{10,14},{12,8},{14,10},{16,20},{18,... | collective-permute-start | bytes 1228808 | tf_op jit(solution)/shard_map/ppermute | solution.py:82
  8.8 37.1 %collective-permute-start.14 = (bf16[160,1280]{1,0:T(8,128)(2,1)}, bf16[160,1280]{1,0:T(8,128)(2,1)}, u32[]{:S(2)}, u32[]{:S(2)}) collective-permute-start(bf16[160,1280]{1,0:T(8,128)(2,1)} %bitcast.525), channel_id=1, source_target_pairs={{0,8},{2,10},{4,12},{6,14},{8,16},{10,18},{12,20},{14,22},{16,24},... | collective-permute-start | bytes 1228808 | tf_op jit(solution)/shard_map/ppermute | solution.py:91
  15.3 136.2 %all-to-all-start = ((bf16[160,8,480]{2,0,1:T(8,128)(2,1)}), bf16[160,8,480]{2,0,1:T(8,128)(2,1)}, u32[]{:S(2)}, u32[]{:S(2)}) async-start(bf16[160,8,480]{2,0,1:T(8,128)(2,1)} %copy.230), calls=%async_computation | async-start | bytes 2621440 | tf_op jit(solution)/shard_map/all_to_all | solution.py:144
  20.4 27.4 %collective-permute-start.41 = (bf16[96,2560]{1,0:T(8,128)(2,1)S(1)}, bf16[96,2560]{1,0:T(8,128)(2,1)}, u32[]{:S(2)}, u32[]{:S(2)}) collective-permute-start(bf16[96,2560]{1,0:T(8,128)(2,1)S(1)} %bitcast.464), channel_id=1, source_target_pairs={{0,1},{1,0},{2,3},{3,2},{4,5},{5,4},{6,7},{7,6},{8,9},{9,8},{10,11... | collective-permute-start | bytes 1474568 | tf_op jit(solution)/shard_map/ppermute | solution.py:88
  41.5 22.0 %collective-permute-start.43 = (bf16[96,2560]{1,0:T(8,128)(2,1)S(1)}, bf16[96,2560]{1,0:T(8,128)(2,1)S(1)}, u32[]{:S(2)}, u32[]{:S(2)}) collective-permute-start(bf16[96,2560]{1,0:T(8,128)(2,1)S(1)} %bitcast.465), channel_id=1, source_target_pairs={{0,8},{2,10},{4,12},{6,14},{8,16},{10,18},{12,20},{14,22},{16,24},... | collective-permute-start | bytes 1474568 | tf_op jit(solution)/shard_map/ppermute | solution.py:91
  46.0 42.5 %collective-permute-start.13 = (bf16[2,160,1280]{2,1,0:T(8,128)(2,1)S(1)}, bf16[2,160,1280]{2,1,0:T(8,128)(2,1)S(1)}, u32[]{:S(2)}, u32[]{:S(2)}) collective-permute-start(bf16[2,160,1280]{2,1,0:T(8,128)(2,1)S(1)} %maximum_select_fusion.44), channel_id=1, source_target_pairs={{0,2},{2,0},{4,6},{6,4},{8,10},{10,8},{12,14},{14,12},{16,18},{18,... | collective-permute-start | bytes 2457608 | tf_op jit(solution)/shard_map/ppermute | solution.py:85
  46.1 17.7 %collective-permute-start.15 = (bf16[160,1280]{1,0:T(8,128)(2,1)}, bf16[160,1280]{1,0:T(8,128)(2,1)S(1)}, u32[]{:S(2)}, u32[]{:S(2)}) collective-permute-start(bf16[160,1280]{1,0:T(8,128)(2,1)} %collective-permute-done.14), channel_id=1, source_target_pairs={{0,4},{2,6},{4,0},{6,2},{8,12},{10,14},{12,8},{14,10},{16,20},{18,... | collective-permute-start | bytes 1228808 | tf_op jit(solution)/shard_map/ppermute | solution.py:82
  47.8 37.9 %collective-permute-start.17 = (bf16[160,1280]{1,0:T(8,128)(2,1)}, bf16[160,1280]{1,0:T(8,128)(2,1)S(1)}, u32[]{:S(2)}, u32[]{:S(2)}) collective-permute-start(bf16[160,1280]{1,0:T(8,128)(2,1)} %collective-permute-done.14), channel_id=1, source_target_pairs={{0,8},{2,10},{4,12},{6,14},{8,16},{10,18},{12,20},{14,22},{16,24},... | collective-permute-start | bytes 1228808 | tf_op jit(solution)/shard_map/ppermute | solution.py:91
  52.5 69.1 %collective-permute-start.1 = (bf16[2,160,1536]{2,1,0:T(8,128)(2,1)S(1)}, bf16[2,160,1536]{2,1,0:T(8,128)(2,1)S(1)}, u32[]{:S(2)}, u32[]{:S(2)}) collective-permute-start(bf16[2,160,1536]{2,1,0:T(8,128)(2,1)S(1)} %maximum_select_fusion.19), channel_id=1, source_target_pairs={{0,2},{2,0},{4,6},{6,4},{8,10},{10,8},{12,14},{14,12},{16,18},{18,... | collective-permute-start | bytes 2949128 | tf_op jit(solution)/shard_map/ppermute | solution.py:85
  74.4 65.7 %collective-permute-start.42 = (bf16[2,96,2560]{2,1,0:T(8,128)(2,1)S(1)}, bf16[2,96,2560]{2,1,0:T(8,128)(2,1)S(1)}, u32[]{:S(2)}, u32[]{:S(2)}) collective-permute-start(bf16[2,96,2560]{2,1,0:T(8,128)(2,1)S(1)} %maximum_select_fusion.35), channel_id=1, source_target_pairs={{0,2},{2,0},{4,6},{6,4},{8,10},{10,8},{12,14},{14,12},{16,18},{18,... | collective-permute-start | bytes 2949128 | tf_op jit(solution)/shard_map/ppermute | solution.py:85
  75.5 46.0 %collective-permute-start.5 = (bf16[160,1536]{1,0:T(8,128)(2,1)}, bf16[160,1536]{1,0:T(8,128)(2,1)}, u32[]{:S(2)}, u32[]{:S(2)}) collective-permute-start(bf16[160,1536]{1,0:T(8,128)(2,1)} %collective-permute-done.2), channel_id=1, source_target_pairs={{0,8},{2,10},{4,12},{6,14},{8,16},{10,18},{12,20},{14,22},{16,24},... | collective-permute-start | bytes 1474568 | tf_op jit(solution)/shard_map/ppermute | solution.py:91
  85.7 17.2 %collective-permute-start.46 = (bf16[96,2560]{1,0:T(8,128)(2,1)S(1)}, bf16[96,2560]{1,0:T(8,128)(2,1)}, u32[]{:S(2)}, u32[]{:S(2)}) collective-permute-start(bf16[96,2560]{1,0:T(8,128)(2,1)S(1)} %collective-permute-done.43), channel_id=1, source_target_pairs={{0,8},{2,10},{4,12},{6,14},{8,16},{10,18},{12,20},{14,22},{16,24},... | collective-permute-start | bytes 1474568 | tf_op jit(solution)/shard_map/ppermute | solution.py:91
  88.4 14.4 %collective-permute-start.18 = (bf16[160,1280]{1,0:T(8,128)(2,1)S(1)}, bf16[160,1280]{1,0:T(8,128)(2,1)S(1)}, u32[]{:S(2)}, u32[]{:S(2)}) collective-permute-start(bf16[160,1280]{1,0:T(8,128)(2,1)S(1)} %collective-permute-done.17), channel_id=1, source_target_pairs={{0,4},{2,6},{4,0},{6,2},{8,12},{10,14},{12,8},{14,10},{16,20},{18,... | collective-permute-start | bytes 1228808 | tf_op jit(solution)/shard_map/ppermute | solution.py:82
  102.9 45.4 %collective-permute-start.16 = (bf16[2,160,1280]{2,1,0:T(8,128)(2,1)S(1)}, bf16[2,160,1280]{2,1,0:T(8,128)(2,1)S(1)}, u32[]{:S(2)}, u32[]{:S(2)}) collective-permute-start(bf16[2,160,1280]{2,1,0:T(8,128)(2,1)S(1)} %maximum_select_fusion.46), channel_id=1, source_target_pairs={{0,2},{2,0},{4,6},{6,4},{8,10},{10,8},{12,14},{14,12},{16,18},{18,... | collective-permute-start | bytes 2457608 | tf_op jit(solution)/shard_map/ppermute | solution.py:85
  116.7 31.3 %collective-permute-start.20 = (bf16[160,1280]{1,0:T(8,128)(2,1)S(1)}, bf16[160,1280]{1,0:T(8,128)(2,1)S(1)}, u32[]{:S(2)}, u32[]{:S(2)}) collective-permute-start(bf16[160,1280]{1,0:T(8,128)(2,1)S(1)} %collective-permute-done.17), channel_id=1, source_target_pairs={{0,8},{2,10},{4,12},{6,14},{8,16},{10,18},{12,20},{14,22},{16,24},... | collective-permute-start | bytes 1228808 | tf_op jit(solution)/shard_map/ppermute | solution.py:91
  121.6 45.3 %collective-permute-start.4 = (bf16[2,160,1536]{2,1,0:T(8,128)(2,1)}, bf16[2,160,1536]{2,1,0:T(8,128)(2,1)}, u32[]{:S(2)}, u32[]{:S(2)}) collective-permute-start(bf16[2,160,1536]{2,1,0:T(8,128)(2,1)} %maximum_select_fusion.21), channel_id=1, source_target_pairs={{0,2},{2,0},{4,6},{6,4},{8,10},{10,8},{12,14},{14,12},{16,18},{18,... | collective-permute-start | bytes 2949128 | tf_op jit(solution)/shard_map/ppermute | solution.py:85
  135.5 47.6 %collective-permute-start.45 = (bf16[2,96,2560]{2,1,0:T(8,128)(2,1)}, bf16[2,96,2560]{2,1,0:T(8,128)(2,1)}, u32[]{:S(2)}, u32[]{:S(2)}) collective-permute-start(bf16[2,96,2560]{2,1,0:T(8,128)(2,1)} %maximum_select_fusion.37), channel_id=1, source_target_pairs={{0,2},{2,0},{4,6},{6,4},{8,10},{10,8},{12,14},{14,12},{16,18},{18,... | collective-permute-start | bytes 2949128 | tf_op jit(solution)/shard_map/ppermute | solution.py:85
  140.1 16.3 %collective-permute-start.8 = (bf16[160,1536]{1,0:T(8,128)(2,1)}, bf16[160,1536]{1,0:T(8,128)(2,1)}, u32[]{:S(2)}, u32[]{:S(2)}) collective-permute-start(bf16[160,1536]{1,0:T(8,128)(2,1)} %collective-permute-done.5), channel_id=1, source_target_pairs={{0,8},{2,10},{4,12},{6,14},{8,16},{10,18},{12,20},{14,22},{16,24},... | collective-permute-start | bytes 1474568 | tf_op jit(solution)/shard_map/ppermute | solution.py:91
  148.1 18.8 %collective-permute-start.49 = (bf16[96,2560]{1,0:T(8,128)(2,1)}, bf16[96,2560]{1,0:T(8,128)(2,1)}, u32[]{:S(2)}, u32[]{:S(2)}) collective-permute-start(bf16[96,2560]{1,0:T(8,128)(2,1)} %collective-permute-done.46), channel_id=1, source_target_pairs={{0,8},{2,10},{4,12},{6,14},{8,16},{10,18},{12,20},{14,22},{16,24},... | collective-permute-start | bytes 1474568 | tf_op jit(solution)/shard_map/ppermute | solution.py:91
  151.5 43.0 %all-to-all-start.1 = ((bf16[160,8,480]{2,0,1:T(8,128)(2,1)}), bf16[160,8,480]{2,0,1:T(8,128)(2,1)}, u32[]{:S(2)}, u32[]{:S(2)}) async-start(bf16[160,8,480]{2,0,1:T(8,128)(2,1)} %copy.232), calls=%async_computation.1 | async-start | bytes 2621440 | tf_op jit(solution)/shard_map/all_to_all | solution.py:144
  156.4 47.4 %collective-permute-start.19 = (bf16[2,160,1280]{2,1,0:T(8,128)(2,1)}, bf16[2,160,1280]{2,1,0:T(8,128)(2,1)}, u32[]{:S(2)}, u32[]{:S(2)}) collective-permute-start(bf16[2,160,1280]{2,1,0:T(8,128)(2,1)} %maximum_select_fusion.47), channel_id=1, source_target_pairs={{0,2},{2,0},{4,6},{6,4},{8,10},{10,8},{12,14},{14,12},{16,18},{18,... | collective-permute-start | bytes 2457608 | tf_op jit(solution)/shard_map/ppermute | solution.py:85
  166.9 45.1 %collective-permute-start.7 = (bf16[2,160,1536]{2,1,0:T(8,128)(2,1)}, bf16[2,160,1536]{2,1,0:T(8,128)(2,1)}, u32[]{:S(2)}, u32[]{:S(2)}) collective-permute-start(bf16[2,160,1536]{2,1,0:T(8,128)(2,1)} %maximum_select_fusion.22), channel_id=1, source_target_pairs={{0,2},{2,0},{4,6},{6,4},{8,10},{10,8},{12,14},{14,12},{16,18},{18,... | collective-permute-start | bytes 2949128 | tf_op jit(solution)/shard_map/ppermute | solution.py:85
  172.4 58.2 %collective-permute-start.48 = (bf16[2,96,2560]{2,1,0:T(8,128)(2,1)}, bf16[2,96,2560]{2,1,0:T(8,128)(2,1)}, u32[]{:S(2)}, u32[]{:S(2)}) collective-permute-start(bf16[2,96,2560]{2,1,0:T(8,128)(2,1)} %maximum_select_fusion.39), channel_id=1, source_target_pairs={{0,2},{2,0},{4,6},{6,4},{8,10},{10,8},{12,14},{14,12},{16,18},{18,... | collective-permute-start | bytes 2949128 | tf_op jit(solution)/shard_map/ppermute | solution.py:85
  180.7 26.6 %collective-permute-start.22 = (bf16[2,160,1280]{2,1,0:T(8,128)(2,1)}, bf16[2,160,1280]{2,1,0:T(8,128)(2,1)}, u32[]{:S(2)}, u32[]{:S(2)}) collective-permute-start(bf16[2,160,1280]{2,1,0:T(8,128)(2,1)} %maximum_select_fusion.49), channel_id=1, source_target_pairs={{0,2},{2,0},{4,6},{6,4},{8,10},{10,8},{12,14},{14,12},{16,18},{18,... | collective-permute-start | bytes 2457608 | tf_op jit(solution)/shard_map/ppermute | solution.py:85
  183.0 52.3 %collective-permute-start.10 = (bf16[2,160,1536]{2,1,0:T(8,128)(2,1)}, bf16[2,160,1536]{2,1,0:T(8,128)(2,1)}, u32[]{:S(2)}, u32[]{:S(2)}) collective-permute-start(bf16[2,160,1536]{2,1,0:T(8,128)(2,1)} %maximum_select_fusion.24), channel_id=1, source_target_pairs={{0,2},{2,0},{4,6},{6,4},{8,10},{10,8},{12,14},{14,12},{16,18},{18,... | collective-permute-start | bytes 2949128 | tf_op jit(solution)/shard_map/ppermute | solution.py:85
  194.5 36.1 %all-to-all-start.2 = ((bf16[160,8,480]{2,0,1:T(8,128)(2,1)}), bf16[160,8,480]{2,0,1:T(8,128)(2,1)S(1)}, u32[]{:S(2)}, u32[]{:S(2)}) async-start(bf16[160,8,480]{2,0,1:T(8,128)(2,1)} %copy.234), calls=%async_computation.2 | async-start | bytes 2621440 | tf_op jit(solution)/shard_map/all_to_all | solution.py:144
  203.8 60.0 %collective-permute-start.51 = (bf16[2,96,2560]{2,1,0:T(8,128)(2,1)}, bf16[2,96,2560]{2,1,0:T(8,128)(2,1)}, u32[]{:S(2)}, u32[]{:S(2)}) collective-permute-start(bf16[2,96,2560]{2,1,0:T(8,128)(2,1)} %maximum_select_fusion.41), channel_id=1, source_target_pairs={{0,2},{2,0},{4,6},{6,4},{8,10},{10,8},{12,14},{14,12},{16,18},{18,... | collective-permute-start | bytes 2949128 | tf_op jit(solution)/shard_map/ppermute | solution.py:85
  207.3 74.4 %collective-permute-start.35 = (bf16[4,320,480]{2,1,0:T(8,128)(2,1)}, bf16[4,320,480]{2,1,0:T(8,128)(2,1)}, u32[]{:S(2)}, u32[]{:S(2)}) collective-permute-start(bf16[4,320,480]{2,1,0:T(8,128)(2,1)} %bitcast.101), channel_id=1, source_target_pairs={{0,4},{2,6},{4,0},{6,2},{8,12},{10,14},{12,8},{14,10},{16,20},{18,... | collective-permute-start | bytes 3686408 | tf_op jit(solution)/shard_map/ppermute | solution.py:82
  212.0 69.8 %collective-permute-start.36 = (bf16[4,320,480]{2,1,0:T(8,128)(2,1)}, bf16[4,320,480]{2,1,0:T(8,128)(2,1)}, u32[]{:S(2)}, u32[]{:S(2)}) collective-permute-start(bf16[4,320,480]{2,1,0:T(8,128)(2,1)} %bitcast.107), channel_id=1, source_target_pairs={{0,4},{2,6},{4,0},{6,2},{8,12},{10,14},{12,8},{14,10},{16,20},{18,... | collective-permute-start | bytes 3686408 | tf_op jit(solution)/shard_map/ppermute | solution.py:82
  230.6 64.0 %collective-permute-start.37 = (bf16[4,320,480]{2,1,0:T(8,128)(2,1)S(1)}, bf16[4,320,480]{2,1,0:T(8,128)(2,1)}, u32[]{:S(2)}, u32[]{:S(2)}) collective-permute-start(bf16[4,320,480]{2,1,0:T(8,128)(2,1)S(1)} %bitcast.475), channel_id=1, source_target_pairs={{0,4},{2,6},{4,0},{6,2},{8,12},{10,14},{12,8},{14,10},{16,20},{18,... | collective-permute-start | bytes 3686408 | tf_op jit(solution)/shard_map/ppermute | solution.py:82
  247.3 20.9 %collective-permute-start.11 = (bf16[192,256]{1,0:T(8,128)(2,1)S(1)}, bf16[192,256]{1,0:T(8,128)(2,1)}, u32[]{:S(2)}, u32[]{:S(2)}) collective-permute-start(bf16[192,256]{1,0:T(8,128)(2,1)S(1)} %fusion.73), channel_id=1, source_target_pairs={{0,1},{1,0},{2,3},{3,2},{4,5},{5,4},{6,7},{7,6},{8,9},{9,8},{10,11... | collective-permute-start | bytes 294920 | tf_op jit(solution)/shard_map/ppermute | solution.py:88
  280.1 17.3 %collective-permute-start.23 = (bf16[96,2560]{1,0:T(8,128)(2,1)S(1)}, bf16[96,2560]{1,0:T(8,128)(2,1)S(1)}, u32[]{:S(2)}, u32[]{:S(2)}) collective-permute-start(bf16[96,2560]{1,0:T(8,128)(2,1)S(1)} %bitcast.550), channel_id=1, source_target_pairs={{0,1},{1,0},{2,3},{3,2},{4,5},{5,4},{6,7},{7,6},{8,9},{9,8},{10,11... | collective-permute-start | bytes 1474568 | tf_op jit(solution)/shard_map/ppermute | solution.py:88
  298.4 14.7 %collective-permute-start.26 = (bf16[96,2560]{1,0:T(8,128)(2,1)S(1)}, bf16[96,2560]{1,0:T(8,128)(2,1)S(1)}, u32[]{:S(2)}, u32[]{:S(2)}) collective-permute-start(bf16[96,2560]{1,0:T(8,128)(2,1)S(1)} %multiply_convert_fusion.4), channel_id=1, source_target_pairs={{0,8},{2,10},{4,12},{6,14},{8,16},{10,18},{12,20},{14,22},{16,24},... | collective-permute-start | bytes 1474568 | tf_op jit(solution)/shard_map/ppermute | solution.py:91
  313.1 15.3 %collective-permute-start.27 = (bf16[96,2560]{1,0:T(8,128)(2,1)S(1)}, bf16[96,2560]{1,0:T(8,128)(2,1)S(1)}, u32[]{:S(2)}, u32[]{:S(2)}) collective-permute-start(bf16[96,2560]{1,0:T(8,128)(2,1)S(1)} %collective-permute-done.26), channel_id=1, source_target_pairs={{0,1},{1,0},{2,3},{3,2},{4,5},{5,4},{6,7},{7,6},{8,9},{9,8},{10,11... | collective-permute-start | bytes 1474568 | tf_op jit(solution)/shard_map/ppermute | solution.py:88
  314.8 30.0 %collective-permute-start.25 = (bf16[2,96,2560]{2,1,0:T(8,128)(2,1)S(1)}, bf16[2,96,2560]{2,1,0:T(8,128)(2,1)S(1)}, u32[]{:S(2)}, u32[]{:S(2)}) collective-permute-start(bf16[2,96,2560]{2,1,0:T(8,128)(2,1)S(1)} %maximum_select_fusion.26), channel_id=1, source_target_pairs={{0,2},{2,0},{4,6},{6,4},{8,10},{10,8},{12,14},{14,12},{16,18},{18,... | collective-permute-start | bytes 2949128 | tf_op jit(solution)/shard_map/ppermute | solution.py:85
  328.6 28.7 %collective-permute-start.28 = (bf16[2,96,2560]{2,1,0:T(8,128)(2,1)S(1)}, bf16[2,96,2560]{2,1,0:T(8,128)(2,1)S(1)}, u32[]{:S(2)}, u32[]{:S(2)}) collective-permute-start(bf16[2,96,2560]{2,1,0:T(8,128)(2,1)S(1)} %maximum_select_fusion.28), channel_id=1, source_target_pairs={{0,2},{2,0},{4,6},{6,4},{8,10},{10,8},{12,14},{14,12},{16,18},{18,... | collective-permute-start | bytes 2949128 | tf_op jit(solution)/shard_map/ppermute | solution.py:85
  328.7 15.4 %collective-permute-start.32 = (bf16[96,2560]{1,0:T(8,128)(2,1)S(1)}, bf16[96,2560]{1,0:T(8,128)(2,1)S(1)}, u32[]{:S(2)}, u32[]{:S(2)}) collective-permute-start(bf16[96,2560]{1,0:T(8,128)(2,1)S(1)} %collective-permute-done.29), channel_id=1, source_target_pairs={{0,8},{2,10},{4,12},{6,14},{8,16},{10,18},{12,20},{14,22},{16,24},... | collective-permute-start | bytes 1474568 | tf_op jit(solution)/shard_map/ppermute | solution.py:91
  339.1 18.7 %collective-permute-start.31 = (bf16[2,96,2560]{2,1,0:T(8,128)(2,1)}, bf16[2,96,2560]{2,1,0:T(8,128)(2,1)}, u32[]{:S(2)}, u32[]{:S(2)}) collective-permute-start(bf16[2,96,2560]{2,1,0:T(8,128)(2,1)} %maximum_select_fusion.30), channel_id=1, source_target_pairs={{0,2},{2,0},{4,6},{6,4},{8,10},{10,8},{12,14},{14,12},{16,18},{18,... | collective-permute-start | bytes 2949128 | tf_op jit(solution)/shard_map/ppermute | solution.py:85
  420.4 45.3 %collective-permute-start.53 = (bf16[4,96,2560]{2,1,0:T(8,128)(2,1)S(1)}, bf16[4,96,2560]{2,1,0:T(8,128)(2,1)S(1)}, u32[]{:S(2)}, u32[]{:S(2)}) collective-permute-start(bf16[4,96,2560]{2,1,0:T(8,128)(2,1)S(1)} %fusion.18), channel_id=1, source_target_pairs={{0,1},{1,0},{2,3},{3,2},{4,5},{5,4},{6,7},{7,6},{8,9},{9,8},{10,11... | collective-permute-start | bytes 5898248 | tf_op jit(solution)/shard_map/ppermute | solution.py:88
  467.5 54.4 %all-to-all-start.4 = ((bf16[4,96,2560]{2,1,0:T(8,128)(2,1)}), bf16[4,96,2560]{2,1,0:T(8,128)(2,1)S(1)}, u32[]{:S(2)}, u32[]{:S(2)}) async-start(bf16[4,96,2560]{2,1,0:T(8,128)(2,1)} %fusion.3), calls=%async_computation.4 | async-start | bytes 3932160 | tf_op jit(solution)/shard_map/all_to_all | solution.py:184
  473.4 44.5 %collective-permute-start.39 = (bf16[4,96,2560]{2,1,0:T(8,128)(2,1)S(1)}, bf16[4,96,2560]{2,1,0:T(8,128)(2,1)S(1)}, u32[]{:S(2)}, u32[]{:S(2)}) collective-permute-start(bf16[4,96,2560]{2,1,0:T(8,128)(2,1)S(1)} %fusion.17), channel_id=1, source_target_pairs={{0,1},{1,0},{2,3},{3,2},{4,5},{5,4},{6,7},{7,6},{8,9},{9,8},{10,11... | collective-permute-start | bytes 5898248 | tf_op jit(solution)/shard_map/ppermute | solution.py:88
  521.9 49.3 %all-to-all-start.3 = ((bf16[4,96,2560]{2,1,0:T(8,128)(2,1)}), bf16[4,96,2560]{2,1,0:T(8,128)(2,1)}, u32[]{:S(2)}, u32[]{:S(2)}) async-start(bf16[4,96,2560]{2,1,0:T(8,128)(2,1)} %fusion.4), calls=%async_computation.3 | async-start | bytes 3932160 | tf_op jit(solution)/shard_map/all_to_all | solution.py:184
  575.0 22.1 %collective-permute-start.54 = (bf16[96,2560]{1,0:T(8,128)(2,1)S(1)}, bf16[96,2560]{1,0:T(8,128)(2,1)S(1)}, u32[]{:S(2)}, u32[]{:S(2)}) collective-permute-start(bf16[96,2560]{1,0:T(8,128)(2,1)S(1)} %get-tuple-element.23), channel_id=1, source_target_pairs={{0,1},{1,0},{2,3},{3,2},{4,5},{5,4},{6,7},{7,6},{8,9},{9,8},{10,11... | collective-permute-start | bytes 1474568 | tf_op jit(solution)/shard_map/ppermute | solution.py:88
  584.8 45.1 %collective-permute-start.75 = (bf16[4,320,480]{2,1,0:T(8,128)(2,1)}, bf16[4,320,480]{2,1,0:T(8,128)(2,1)}, u32[]{:S(2)}, u32[]{:S(2)}) collective-permute-start(bf16[4,320,480]{2,1,0:T(8,128)(2,1)} %fusion.41), channel_id=1, source_target_pairs={{0,4},{2,6},{4,0},{6,2},{8,12},{10,14},{12,8},{14,10},{16,20},{18,... | collective-permute-start | bytes 3686408 | tf_op jit(solution)/shard_map/ppermute | solution.py:82
  620.8 65.1 %collective-permute-start.63 = (bf16[4,2,160,1536]{3,2,1,0:T(8,128)(2,1)}, bf16[4,2,160,1536]{3,2,1,0:T(8,128)(2,1)}, u32[]{:S(2)}, u32[]{:S(2)}) collective-permute-start(bf16[4,2,160,1536]{3,2,1,0:T(8,128)(2,1)} %fusion.1), channel_id=1, source_target_pairs={{0,2},{2,0},{4,6},{6,4},{8,10},{10,8},{12,14},{14,12},{16,18},{18,... | collective-permute-start | bytes 11796488 | tf_op jit(solution)/shard_map/ppermute | solution.py:85
  629.4 31.2 %collective-permute-start.74 = (bf16[4,320,480]{2,1,0:T(8,128)(2,1)}, bf16[4,320,480]{2,1,0:T(8,128)(2,1)}, u32[]{:S(2)}, u32[]{:S(2)}) collective-permute-start(bf16[4,320,480]{2,1,0:T(8,128)(2,1)} %fusion.40), channel_id=1, source_target_pairs={{0,4},{2,6},{4,0},{6,2},{8,12},{10,14},{12,8},{14,10},{16,20},{18,... | collective-permute-start | bytes 3686408 | tf_op jit(solution)/shard_map/ppermute | solution.py:82
  633.8 40.9 %all-to-all-start.9 = ((bf16[8,160,480]{2,1,0:T(8,128)(2,1)}), bf16[8,160,480]{2,1,0:T(8,128)(2,1)S(1)}, u32[]{:S(2)}, u32[]{:S(2)}) async-start(bf16[8,160,480]{2,1,0:T(8,128)(2,1)} %bitcast.229), calls=%async_computation.9 | async-start | bytes 2621440 | tf_op jit(solution)/shard_map/all_to_all | solution.py:158
  674.7 91.0 %collective-permute-start.66 = (bf16[4,2,160,1280]{3,2,1,0:T(8,128)(2,1)}, bf16[4,2,160,1280]{3,2,1,0:T(8,128)(2,1)}, u32[]{:S(2)}, u32[]{:S(2)}) collective-permute-start(bf16[4,2,160,1280]{3,2,1,0:T(8,128)(2,1)} %fusion.5), channel_id=1, source_target_pairs={{0,2},{2,0},{4,6},{6,4},{8,10},{10,8},{12,14},{14,12},{16,18},{18,... | collective-permute-start | bytes 9830408 | tf_op jit(solution)/shard_map/ppermute | solution.py:85
  674.7 42.2 %all-to-all-start.8 = ((bf16[8,160,480]{2,1,0:T(8,128)(2,1)}), bf16[8,160,480]{2,1,0:T(8,128)(2,1)S(1)}, u32[]{:S(2)}, u32[]{:S(2)}) async-start(bf16[8,160,480]{2,1,0:T(8,128)(2,1)} %bitcast.477), calls=%async_computation.8 | async-start | bytes 2621440 | tf_op jit(solution)/shard_map/all_to_all | solution.py:158
  681.4 31.9 %collective-permute-start.73 = (bf16[4,320,480]{2,1,0:T(8,128)(2,1)}, bf16[4,320,480]{2,1,0:T(8,128)(2,1)}, u32[]{:S(2)}, u32[]{:S(2)}) collective-permute-start(bf16[4,320,480]{2,1,0:T(8,128)(2,1)} %fusion.39), channel_id=1, source_target_pairs={{0,4},{2,6},{4,0},{6,2},{8,12},{10,14},{12,8},{14,10},{16,20},{18,... | collective-permute-start | bytes 3686408 | tf_op jit(solution)/shard_map/ppermute | solution.py:82
  685.8 36.2 %collective-permute-start.69 = (f32[12800]{0:T(1024)S(1)}, f32[12800]{0:T(1024)S(1)}, u32[]{:S(2)}, u32[]{:S(2)}) collective-permute-start(f32[12800]{0:T(1024)S(1)} %pad_maximum_fusion.2), channel_id=1, source_target_pairs={{0,2},{2,0},{4,6},{6,4},{8,10},{10,8},{12,14},{14,12},{16,18},{18,... | collective-permute-start | bytes 153608 | tf_op jit(solution)/shard_map/ppermute | solution.py:85
  696.3 76.7 %collective-permute-start.64 = (bf16[4,160,1536]{2,1,0:T(8,128)(2,1)}, bf16[4,160,1536]{2,1,0:T(8,128)(2,1)}, u32[]{:S(2)}, u32[]{:S(2)}) collective-permute-start(bf16[4,160,1536]{2,1,0:T(8,128)(2,1)} %fusion.19), channel_id=1, source_target_pairs={{0,4},{2,6},{4,0},{6,2},{8,12},{10,14},{12,8},{14,10},{16,20},{18,... | collective-permute-start | bytes 5898248 | tf_op jit(solution)/shard_map/ppermute | solution.py:82
  717.0 60.7 %all-to-all-start.7 = ((bf16[8,160,480]{2,1,0:T(8,128)(2,1)}), bf16[8,160,480]{2,1,0:T(8,128)(2,1)}, u32[]{:S(2)}, u32[]{:S(2)}) async-start(bf16[8,160,480]{2,1,0:T(8,128)(2,1)} %bitcast.215), calls=%async_computation.7 | async-start | bytes 2621440 | tf_op jit(solution)/shard_map/all_to_all | solution.py:158
  722.1 34.0 %collective-permute-start.70 = (f32[12800]{0:T(1024)S(1)}, f32[12800]{0:T(1024)S(1)}, u32[]{:S(2)}, u32[]{:S(2)}) collective-permute-start(f32[12800]{0:T(1024)S(1)} %fusion.100), channel_id=1, source_target_pairs={{0,4},{2,6},{4,0},{6,2},{8,12},{10,14},{12,8},{14,10},{16,20},{18,... | collective-permute-start | bytes 153608 | tf_op jit(solution)/shard_map/ppermute | solution.py:82
  760.3 59.2 %collective-permute-start.72 = (f32[12800]{0:T(1024)S(1)}, f32[12800]{0:T(1024)S(1)}, u32[]{:S(2)}, u32[]{:S(2)}) collective-permute-start(f32[12800]{0:T(1024)S(1)} %add.367), channel_id=1, source_target_pairs={{0,16},{2,18},{4,20},{6,22},{8,24},{10,26},{12,28},{14,30},{16,0},... | collective-permute-start | bytes 153608 | tf_op jit(solution)/shard_map/ppermute | solution.py:97
  777.6 48.5 %all-to-all-start.5 = ((bf16[4,160,1536]{2,1,0:T(8,128)(2,1)}), bf16[4,160,1536]{2,1,0:T(8,128)(2,1)}, u32[]{:S(2)}, u32[]{:S(2)}) async-start(bf16[4,160,1536]{2,1,0:T(8,128)(2,1)} %fusion.2), calls=%async_computation.5 | async-start | bytes 3932160 | tf_op jit(solution)/shard_map/all_to_all | solution.py:137
  785.5 36.4 %collective-permute-start.67 = (bf16[4,160,1280]{2,1,0:T(8,128)(2,1)}, bf16[4,160,1280]{2,1,0:T(8,128)(2,1)}, u32[]{:S(2)}, u32[]{:S(2)}) collective-permute-start(bf16[4,160,1280]{2,1,0:T(8,128)(2,1)} %fusion.30), channel_id=1, source_target_pairs={{0,4},{2,6},{4,0},{6,2},{8,12},{10,14},{12,8},{14,10},{16,20},{18,... | collective-permute-start | bytes 4915208 | tf_op jit(solution)/shard_map/ppermute | solution.py:82
  792.9 27.9 %collective-permute-start.56 = (bf16[96,2560]{1,0:T(8,128)(2,1)}, bf16[96,2560]{1,0:T(8,128)(2,1)S(1)}, u32[]{:S(2)}, u32[]{:S(2)}) collective-permute-start(bf16[96,2560]{1,0:T(8,128)(2,1)} %bitcast.179), channel_id=1, source_target_pairs={{0,1},{1,0},{2,3},{3,2},{4,5},{5,4},{6,7},{7,6},{8,9},{9,8},{10,11... | collective-permute-start | bytes 1474568 | tf_op jit(solution)/shard_map/ppermute | solution.py:88
  818.1 43.5 %collective-permute-start.40 = (bf16[96,2560]{1,0:T(8,128)(2,1)}, bf16[96,2560]{1,0:T(8,128)(2,1)}, u32[]{:S(2)}, u32[]{:S(2)}) collective-permute-start(bf16[96,2560]{1,0:T(8,128)(2,1)} %get-tuple-element.36), channel_id=1, source_target_pairs={{0,1},{1,0},{2,3},{3,2},{4,5},{5,4},{6,7},{7,6},{8,9},{9,8},{10,11... | collective-permute-start | bytes 1474568 | tf_op jit(solution)/shard_map/ppermute | solution.py:88
  826.2 47.0 %all-to-all-start.6 = ((bf16[4,160,1280]{2,1,0:T(8,128)(2,1)}), bf16[4,160,1280]{2,1,0:T(8,128)(2,1)}, u32[]{:S(2)}, u32[]{:S(2)}) async-start(bf16[4,160,1280]{2,1,0:T(8,128)(2,1)} %fusion.6), calls=%async_computation.6 | async-start | bytes 3276800 | tf_op jit(solution)/shard_map/all_to_all | solution.py:137
  836.1 33.4 %collective-permute-start.57 = (bf16[96,2560]{1,0:T(8,128)(2,1)S(1)}, bf16[96,2560]{1,0:T(8,128)(2,1)S(1)}, u32[]{:S(2)}, u32[]{:S(2)}) collective-permute-start(bf16[96,2560]{1,0:T(8,128)(2,1)S(1)} %fusion.58), channel_id=1, source_target_pairs={{0,1},{1,0},{2,3},{3,2},{4,5},{5,4},{6,7},{7,6},{8,9},{9,8},{10,11... | collective-permute-start | bytes 1474568 | tf_op jit(solution)/shard_map/ppermute | solution.py:88
  837.6 19.2 %collective-permute-start.61 = (f32[2560]{0:T(1024)S(1)}, f32[2560]{0:T(1024)S(1)}, u32[]{:S(2)}, u32[]{:S(2)}) collective-permute-start(f32[2560]{0:T(1024)S(1)} %add.355), channel_id=1, source_target_pairs={{0,8},{2,10},{4,12},{6,14},{8,0},{10,2},{12,4},{14,6},{16,24},{18,... | collective-permute-start | bytes 30728 | tf_op jit(solution)/shard_map/ppermute | solution.py:97
  (103 other events, 1520.6 us)

commit v2 on v1

v2 whole, which is shorter than its diff:
```python
import math
from functools import partial

import jax
import jax.numpy as jnp
from jax import lax
from jax.experimental import pallas as pl
from jax.experimental.pallas import tpu as pltpu
from jax.sharding import PartitionSpec as P

EPS = 1e-06
F32 = jnp.float32
BF16 = jnp.bfloat16
DEPTH = {"x": 1, "y": 1, "z": 2}
VMEM = 48 * 2**20
GELU_A, GELU_B = math.sqrt(2.0 / math.pi), 0.044715


def positions(segment):
    count = segment.shape[0]
    index = jnp.arange(count, dtype=jnp.int32)
    fresh = jnp.concatenate([jnp.ones((1,), jnp.bool_), segment[1:] != segment[:-1]])
    starts = lax.cummax(jnp.where(fresh, index, 0), axis=0)
    return (index - starts).astype(F32)


def inv_root(values):
    return lax.rsqrt(jnp.mean(values * values, axis=-1, keepdims=True) + EPS)


def norm_back(values, factor, gain, grad_norm):
    scaled = gain * grad_norm
    return factor * scaled - values * factor**3 * jnp.mean(scaled * values, axis=-1, keepdims=True)


def mm(left, right):
    return jnp.dot(left, right, preferred_element_type=F32)


def mm_nt(left, right):
    return lax.dot_general(left, right, (((1,), (1,)), ((), ())), preferred_element_type=F32)


def mm_tn(left, right):
    return lax.dot_general(left, right, (((0,), (0,)), ((), ())), preferred_element_type=F32)


def after(value, *earlier):
    return lax.optimization_barrier((value,) + earlier)[0]


class Grid:
    def __init__(self, total):
        self.z_count = total // 4
        spots = [(z, y, c) for z in range(self.z_count) for y in range(2) for c in range(2)]
        at = lambda z, y, c: (z * 2 + y) * 2 + c
        self.swap_y = [(at(z, y, c), at(z, 1 - y, c)) for z, y, c in spots]
        self.swap_c = [(at(z, y, c), at(z, y, 1 - c)) for z, y, c in spots]
        self.ring = [(at(z, y, c), at((z + 1) % self.z_count, y, c)) for z, y, c in spots]
        self.flips = []
        step = 1
        while step < self.z_count:
            self.flips.append([(at(z, y, c), at(z ^ step, y, c)) for z, y, c in spots])
            step *= 2
        self.lines = [
            [at(z, y, c) for z in range(self.z_count)] for y in range(2) for c in range(2)
        ]
        index = lax.axis_index("dp")
        self.c = index % 2
        self.y = (index // 2) % 2
        self.z = index // 4
        self.x = lax.axis_index("mp")
        self.sent = {"x": [], "y": [], "z": []}

    def queue(self, link, value, send):
        ahead = self.sent[link][-DEPTH[link] :]
        if len(ahead) == DEPTH[link]:
            value = after(value, ahead[0])
        self.sent[link].append(send(value))
        return self.sent[link][-1]

    def over_y(self, value):
        return self.queue("y", value, lambda v: lax.ppermute(v, "dp", self.swap_y))

    def over_c(self, value):
        return lax.ppermute(value, "dp", self.swap_c)

    def over_x(self, value):
        return self.queue("x", value, lambda v: lax.ppermute(v, "mp", [(0, 1), (1, 0)]))

    def next_z(self, value):
        return self.queue("z", value, lambda v: lax.ppermute(v, "dp", self.ring))

    def along_z(self, value):
        send = lambda v: lax.all_to_all(v, "dp", 0, 0, axis_index_groups=self.lines, tiled=True)
        return self.queue("z", value, send)

    def behind(self, step):
        return lax.rem(self.z - step + 2 * self.z_count, self.z_count)

    def sum_dp(self, value):
        value = value + self.over_c(value)
        value = value + lax.ppermute(value, "dp", self.swap_y)
        for flip in self.flips:
            value = value + lax.ppermute(value, "dp", flip)
        return value


def pair(index, mine, other, axis):
    return jnp.where(
        index == 0, jnp.stack([mine, other], axis=axis), jnp.stack([other, mine], axis=axis)
    )


def take(value, index, axis):
    return lax.dynamic_index_in_dim(value, index, axis, keepdims=False)


def call(body, grid, in_specs, outs, out_specs, operands, scratch=(), aliases=None):
    return pl.pallas_call(
        body,
        out_shape=[jax.ShapeDtypeStruct(shape, dtype) for shape, dtype in outs],
        grid_spec=pltpu.PrefetchScalarGridSpec(
            num_scalar_prefetch=1,
            grid=grid,
            in_specs=in_specs,
            out_specs=out_specs,
            scratch_shapes=list(scratch),
        ),
        input_output_aliases=aliases or {},
        compiler_params=pltpu.CompilerParams(vmem_limit_bytes=VMEM),
    )(*operands)


def place_slot(ranks, pieces, wholes, z_count, cuts):
    rows, width = pieces[0].shape
    ends = list(cuts[1:]) + [width]
    given = len(wholes)

    def body(ranks_ref, *refs):
        sources, targets = refs[:4], refs[4 + given :]
        y, c = ranks_ref[1], ranks_ref[2]
        spots = [(y, c), (1 - y, c), (y, 1 - c), (1 - y, 1 - c)]
        for source, (at_y, at_c) in zip(sources, spots):
            for target, begin, end in zip(targets, cuts, ends):
                target[0, at_y, at_c] = source[:, begin:end]

    whole_spec = pl.BlockSpec(memory_space=pl.ANY)
    return call(
        body,
        (1,),
        [pl.BlockSpec((rows, width), lambda i, ranks: (0, 0))] * 4 + [whole_spec] * given,
        [((z_count, 2, 2, rows, end - begin), BF16) for begin, end in zip(cuts, ends)],
        [
            pl.BlockSpec((1, 2, 2, rows, end - begin), lambda i, ranks: (ranks[0], 0, 0, 0, 0))
            for begin, end in zip(cuts, ends)
        ],
        (ranks, *pieces, *wholes),
        aliases={5 + number: number for number in range(given)},
    )


def place_all(ranks, pieces):
    z_count, rows, width = pieces[0].shape

    def body(ranks_ref, own, side, core, both, target):
        y, c = ranks_ref[1], ranks_ref[2]
        target[0, y, c] = own[0]
        target[0, 1 - y, c] = side[0]
        target[0, y, 1 - c] = core[0]
        target[0, 1 - y, 1 - c] = both[0]

    whole = call(
        body,
        (z_count,),
        [pl.BlockSpec((1, rows, width), lambda i, ranks: (i, 0, 0))] * 4,
        [((z_count, 2, 2, rows, width), BF16)],
        [pl.BlockSpec((1, 2, 2, rows, width), lambda i, ranks: (i, 0, 0, 0, 0))],
        (ranks, *pieces),
    )[0]
    return whole.reshape(z_count * 4 * rows, width)


def product_rows(ranks, lefts, rights, z_count):
    features = lefts[0].shape[1]
    width = rights[0].shape[1]
    rows = features // (4 * z_count)
    block = math.lcm(4 * rows, 128)
    span = block // (4 * rows)

    def body(ranks_ref, *refs):
        left = [ref[...] for ref in refs[: len(lefts)]]
        right = [ref[...] for ref in refs[len(lefts) : -2]]
        keep, send = refs[-2:]
        left = left[0] if len(left) == 1 else jnp.concatenate(left, axis=0)
        right = right[0] if len(right) == 1 else jnp.concatenate(right, axis=0)
        whole = mm_tn(left, right)
        low = ranks_ref[2] == 0
        for place in range(span):
            for y in range(2):
                at = (place * 4 + y * 2) * rows
                first, second = whole[at : at + rows], whole[at + rows : at + 2 * rows]
                keep[place, y] = jnp.where(low, first, second).astype(BF16)
                send[place, y] = jnp.where(low, second, first).astype(BF16)

    out_spec = pl.BlockSpec((span, 2, rows, width), lambda i, ranks: (i, 0, 0, 0))
    return call(
        body,
        (features // block,),
        [pl.BlockSpec((left.shape[0], block), lambda i, ranks: (0, i)) for left in lefts]
        + [pl.BlockSpec(right.shape, lambda i, ranks: (0, 0)) for right in rights],
        [((z_count, 2, rows, width), BF16)] * 2,
        [out_spec] * 2,
        (ranks, *lefts, *rights),
    )


def reduce_rows(grid, ranks, lefts, rights):
    keep, send = product_rows(ranks, lefts, rights, grid.z_count)
    got = grid.over_c(send)
    pick = lambda value, y: take(value, y, 1).astype(F32)
    part = (pick(keep, 1 - grid.y) + pick(got, 1 - grid.y)).astype(BF16)
    across = grid.over_y(part)
    return (pick(keep, grid.y) + pick(got, grid.y) + across.astype(F32)).astype(BF16)


def mlp_slot(ranks, wg, wu, wd, bg, bu, own, other, dy_own, dy_other):
    features, hidden = wg.shape
    half = own.shape[0]
    block = features // 4 if (features // 4) % 128 == 0 else features

    def body(
        ranks_ref, wg_ref, wu_ref, wd_ref, bg_ref, bu_ref, own_ref, other_ref, dyo_ref, dyr_ref,
        hid_ref, dg_ref, du_ref, db_own, db_other, out_own, out_other, b_all, dy_all, sums,
    ):
        b_all[:half], b_all[half:] = own_ref[...], other_ref[...]
        dy_all[:half], dy_all[half:] = dyo_ref[...], dyr_ref[...]
        sums[...] = jnp.zeros_like(sums)

        @pl.loop(0, features // block)
        def _(step):
            at = pl.ds(pl.multiple_of(step * block, 128), block)
            sums[0] += mm(b_all[:, at], wg_ref[at, :])
            sums[1] += mm(b_all[:, at], wu_ref[at, :])
            sums[2] += mm(dy_all[:, at], wd_ref[at, :])

        gate, up, grad_inner = sums[0] + bg_ref[...], sums[1] + bu_ref[...], sums[2]
        inner = GELU_A * (gate + GELU_B * gate * gate * gate)
        bend = jnp.tanh(inner)
        gelu = 0.5 * gate * (1.0 + bend)
        slope = 0.5 * (1.0 + bend) + 0.5 * gate * (1.0 - bend * bend) * (
            GELU_A * (1.0 + 3.0 * GELU_B * gate * gate)
        )
        hid = (gelu * up).astype(BF16)
        grad_gate = (grad_inner * up * slope).astype(BF16)
        grad_up = (grad_inner * gelu).astype(BF16)
        hid_ref[...], dg_ref[...], du_ref[...] = hid, grad_gate, grad_up

        @pl.loop(0, features // block)
        def _(step):
            at = pl.ds(pl.multiple_of(step * block, 128), block)
            part = mm_nt(dg_ref[...], wg_ref[at, :]) + mm_nt(du_ref[...], wu_ref[at, :])
            db_own[:, at], db_other[:, at] = part[:half].astype(BF16), part[half:].astype(BF16)
            part = mm_nt(hid_ref[...], wd_ref[at, :])
            out_own[:, at], out_other[:, at] = part[:half].astype(BF16), part[half:].astype(BF16)

    full = lambda shape: pl.BlockSpec(shape, lambda i, ranks: (0, 0))
    operands = (wg, wu, wd, bg[None], bu[None], own, other, dy_own, dy_other)
    outs = [((2 * half, hidden), BF16)] * 3 + [((half, features), BF16)] * 4
    return call(
        body,
        (1,),
        [full(operand.shape) for operand in operands],
        outs,
        [full(shape) for shape, _ in outs],
        (ranks, *operands),
        scratch=[
            pltpu.VMEM((2 * half, features), BF16),
            pltpu.VMEM((2 * half, features), BF16),
            pltpu.VMEM((3, 2 * half, hidden), F32),
        ],
    )


def scatter_z(grid, parts):
    held = take(parts, grid.behind(1), 0)
    for step in range(2, grid.z_count + 1):
        got = grid.next_z(held)
        held = got.astype(F32) + take(parts, grid.behind(step), 0).astype(F32)
        held = held.astype(BF16) if step < grid.z_count else held
    return held


def split_columns(grid, shard):
    rows, width = shard.shape
    return shard.reshape(rows, grid.z_count, width // grid.z_count).transpose(1, 0, 2)


def collect_columns(grid, parts):
    parts = grid.along_z(parts)
    count, rows, width = parts.shape
    return parts.astype(F32).transpose(1, 0, 2).reshape(rows, count * width)


def turned(value, cosine, sine):
    first = value[:, : cosine.shape[1]]
    first = first * cosine + pltpu.roll(first, first.shape[1] // 2, 1) * sine
    return jnp.concatenate([first, value[:, cosine.shape[1] :]], axis=1)


def softmax(query, key, bias):
    scores = mm_nt(query, key) + bias
    expon = jnp.exp(scores - jnp.max(scores, axis=-1, keepdims=True))
    return expon / jnp.sum(expon, axis=-1, keepdims=True)


def attend(scale, q_ref, k_ref, v_ref, cos_ref, sin_ref, bias_ref, rq_ref, o_ref):
    size = k_ref.shape[1]
    for head in range(q_ref.shape[1] // size):
        at = pl.ds(head * size, size)
        query = (turned(q_ref[:, at], cos_ref[...], sin_ref[...]) * scale).astype(BF16)
        rq_ref[:, at] = query
        probs = softmax(query, k_ref[...], bias_ref[...]).astype(BF16)
        o_ref[:, at] = mm(probs, v_ref[...]).astype(BF16)


def attend_back(
    scale, do_ref, rq_ref, k_ref, v_ref, cos_ref, sin_ref, bias_ref, dq_ref, dk_ref, dv_ref
):
    size = k_ref.shape[1]
    cosine, sine = cos_ref[...], -sin_ref[...]
    grad_key = jnp.zeros(dk_ref.shape, F32)
    grad_value = jnp.zeros(dv_ref.shape, F32)
    for head in range(rq_ref.shape[1] // size):
        at = pl.ds(head * size, size)
        query, grad_out = rq_ref[:, at], do_ref[:, at]
        probs = softmax(query, k_ref[...], bias_ref[...])
        grad_value += mm_tn(probs.astype(BF16), grad_out)
        grad_probs = mm_nt(grad_out, v_ref[...])
        delta = jnp.sum(probs * grad_probs, axis=-1, keepdims=True)
        grad_scores = (probs * (grad_probs - delta)).astype(BF16)
        grad_query = mm(grad_scores, k_ref[...]) * scale
        dq_ref[:, at] = turned(grad_query, cosine, sine).astype(BF16)
        grad_key += mm_tn(grad_scores, query)
    dk_ref[...] = turned(grad_key, cosine, sine)
    dv_ref[...] = grad_value


def in_vmem(body, shapes, *operands):
    spec = pl.BlockSpec(memory_space=pltpu.VMEM)
    return pl.pallas_call(
        body,
        out_shape=[jax.ShapeDtypeStruct(shape, dtype) for shape, dtype in shapes],
        in_specs=[spec] * len(operands),
        out_specs=[spec] * len(shapes),
        compiler_params=pltpu.CompilerParams(vmem_limit_bytes=32 * 2**20),
    )(*operands)


def shards(
    inputs,
    gain_attn,
    w_query,
    w_keyval,
    w_output,
    gain_mlp,
    w_gate,
    b_gate,
    w_up,
    b_up,
    w_down,
    b_down,
    segment_ids,
    cotangent,
    total,
):
    grid = Grid(total)
    count = grid.z_count
    micro, length, width = inputs.shape
    tokens = micro * length
    head_dim = w_keyval.shape[1] // 2
    query_width = w_query.shape[1]
    scale = head_dim ** (-0.5)

    def halves(value):
        value = value.reshape(micro, 2, length // 2, value.shape[-1])
        return tuple(take(value, i, 1).reshape(tokens // 2, -1) for i in (grid.x, 1 - grid.x))

    def join(mine, other):
        shape = (micro, length // 2, mine.shape[-1])
        return pair(grid.x, mine.reshape(shape), other.reshape(shape), 1).reshape(tokens, -1)

    keyval_half = lax.dynamic_slice_in_dim(w_keyval, grid.x * head_dim, head_dim, 1)
    ranks = jnp.stack([grid.z, grid.y, grid.c]).astype(jnp.int32)
    slots = [jnp.concatenate([w_query, keyval_half, w_output.T], axis=1)]
    dy_half = halves(cotangent.reshape(tokens, width))[0]
    dy_slots, dy_others = [dy_half], []
    wholes = []
    for step in range(count):
        if step + 1 < count:
            slots.append(grid.next_z(slots[step]))
        across = grid.over_y(slots[step])
        if step + 1 < count:
            dy_slots.append(grid.next_z(dy_slots[step]))
        pieces = [slots[step], across, grid.over_c(slots[step]), grid.over_c(across)]
        spot = jnp.stack([grid.behind(step), grid.y, grid.c]).astype(jnp.int32)
        wholes = place_slot(spot, pieces, wholes, count, (0, query_width + head_dim))
        dy_others.append(grid.over_x(dy_slots[step]))
    w_qkv, w_out = [whole.reshape(width, -1) for whole in wholes]

    mlp = []
    for shard in (w_gate, w_up, w_down.T):
        mine = grid.along_z(split_columns(grid, shard))
        across = grid.over_y(mine)
        mlp.append(place_all(ranks, [mine, across, grid.over_c(mine), grid.over_c(across)]))
    wg, wu, wd = mlp
    hidden = wg.shape[1]
    place = grid.z * hidden
    bg = lax.dynamic_slice_in_dim(b_gate, place, hidden, 0)
    bu = lax.dynamic_slice_in_dim(b_up, place, hidden, 0)

    segment = segment_ids.reshape(micro, length)
    offsets = jax.vmap(positions)(segment).reshape(tokens)
    quarter = head_dim // 4
    freqs = 10000.0 ** (-jnp.arange(quarter, dtype=F32) / quarter)
    angle = offsets[:, None] * freqs[None, :]
    cosine, sine = jnp.cos(angle), jnp.sin(angle)
    cosine = jnp.concatenate([cosine, cosine], axis=1)
    sine = jnp.concatenate([-sine, sine], axis=1)
    index = jnp.arange(tokens, dtype=jnp.int32)
    seg = segment.reshape(tokens)
    allowed = (
        (seg[:, None] == seg[None, :])
        & (index[:, None] // length == index[None, :] // length)
        & (index[None, :] <= index[:, None])
    )
    bias = jnp.where(allowed, 0.0, -1e30).astype(F32)
    hidden_x = inputs.reshape(tokens, width).astype(F32)
    factor_one = inv_root(hidden_x)
    normed = (hidden_x * factor_one * gain_attn).astype(BF16)
    queries = mm(normed, w_qkv[:, :query_width])
    keyval = mm(normed, w_qkv[:, query_width:])
    front, back = keyval[:, :quarter], keyval[:, quarter : 2 * quarter]
    swapped = jnp.concatenate([back, front], axis=1)
    key = jnp.concatenate(
        [keyval[:, : 2 * quarter] * cosine + swapped * sine, keyval[:, 2 * quarter :]], axis=1
    )
    keyval = jnp.where(grid.x == 0, key, keyval).astype(BF16)
    keyval_other = grid.over_x(keyval)
    rot_key = jnp.where(grid.x == 0, keyval, keyval_other)
    values_in = jnp.where(grid.x == 0, keyval_other, keyval)
    shape = (tokens, query_width)
    rot_query, mixed_b = in_vmem(
        partial(attend, scale),
        [(shape, BF16), (shape, BF16)],
        *(queries, rot_key, values_in, cosine, sine, bias),
    )
    attended = mm_nt(mixed_b, w_out)
    mine, other = halves(attended)
    attended = mine + grid.over_x(other.astype(BF16)).astype(F32)
    x_half = halves(hidden_x)[0]
    residual = x_half + attended
    factor_two = inv_root(residual)
    normed_two = (residual * factor_two * gain_mlp).astype(BF16)

    b_slots, b_others, slot = [], [], normed_two
    for step in range(count):
        coming = grid.next_z(slot) if step + 1 < count else None
        b_slots.append(slot)
        b_others.append(grid.over_x(slot))
        slot = coming
    results = [
        mlp_slot(ranks, wg, wu, wd, bg, bu, *pieces)
        for pieces in zip(b_slots, b_others, dy_slots, dy_others)
    ]
    inner_slots, gate_slots, up_slots, db_own, db_other, out_own, out_other = zip(*results)

    def back_to_tokens(owns, others):
        held = None
        for step in list(range(1, count)) + [0]:
            part = owns[step].astype(F32) + grid.over_x(others[step]).astype(F32)
            held = part if held is None else part + held.astype(F32)
            if step > 0:
                held = grid.next_z(held.astype(BF16))
        return held

    grad_norm_two = back_to_tokens(db_own, db_other)
    grad_out = dy_half.astype(F32)
    gain_mlp_term = jnp.sum(grad_norm_two * residual * factor_two, axis=0)
    grad_resid = grad_out + norm_back(residual, factor_two, gain_mlp, grad_norm_two)
    grad_resid_b = grad_resid.astype(BF16)
    grad_resid_b = join(grad_resid_b, grid.over_x(grad_resid_b))

    dy_all = [piece for two in zip(dy_slots, dy_others) for piece in two]
    b_all = [piece for two in zip(b_slots, b_others) for piece in two]
    down_grad = collect_columns(grid, reduce_rows(grid, ranks, dy_all, inner_slots)).T
    gate_grad = collect_columns(grid, reduce_rows(grid, ranks, b_all, gate_slots))
    up_grad = collect_columns(grid, reduce_rows(grid, ranks, b_all, up_slots))

    out_grad = scatter_z(grid, reduce_rows(grid, ranks, [grad_resid_b], [mixed_b])).T
    grad_mixed = mm(grad_resid_b, w_out).astype(BF16)
    shape_kv = (tokens, head_dim)
    grad_query, grad_key, grad_values = in_vmem(
        partial(attend_back, scale),
        [(shape, BF16), (shape_kv, F32), (shape_kv, F32)],
        *(grad_mixed, rot_query, rot_key, values_in, cosine, sine, bias),
    )
    grad_own = jnp.where(grid.x == 0, grad_key, grad_values)
    grad_other = jnp.where(grid.x == 0, grad_values, grad_key)
    grad_keyval = (grad_own + grid.over_x(grad_other)).astype(BF16)
    grad_qkv = jnp.concatenate([grad_query, grad_keyval], axis=1)
    mine, other = halves(mm_nt(grad_qkv, w_qkv))
    grad_normed = mine + grid.over_x(other.astype(BF16)).astype(F32)
    factor_half = halves(factor_one)[0]
    gain_attn_term = jnp.sum(grad_normed * x_half * factor_half, axis=0)
    grad_input = grad_resid + norm_back(x_half, factor_half, gain_attn, grad_normed)
    grad_input = grad_input.astype(BF16)
    grad_input = join(grad_input, grid.over_x(grad_input))

    branch = back_to_tokens(out_own, out_other)
    outputs = (residual + branch + b_down).astype(BF16)
    outputs = join(outputs, grid.over_x(outputs))

    middle = (query_width + head_dim) // 2
    cuts = (grad_qkv[:, :middle], grad_qkv[:, middle:])
    cuts = [reduce_rows(grid, ranks, [normed], [cut]) for cut in cuts]
    qkv_grad = jnp.concatenate([scatter_z(grid, cut) for cut in cuts], axis=1)
    query_grad = qkv_grad[:, :query_width]
    keyval_grad = qkv_grad[:, query_width:]
    keyval_grad = pair(grid.x, keyval_grad, grid.over_x(keyval_grad), 1)
    keyval_grad = keyval_grad.reshape(keyval_grad.shape[0], 2 * head_dim)

    ffn = b_gate.shape[0]
    wide = jnp.zeros((2, ffn), F32)
    sums = [
        sum(jnp.sum(slot.astype(F32), axis=0) for slot in slots)
        for slots in (gate_slots, up_slots)
    ]
    wide = lax.dynamic_update_slice(wide, jnp.stack(sums), (0, place)).reshape(-1)
    narrow = jnp.stack([gain_attn_term, gain_mlp_term, jnp.sum(grad_out, axis=0)])
    narrow = (narrow + grid.over_x(narrow)).reshape(-1)
    small = grid.sum_dp(jnp.concatenate([narrow, wide]))
    return (
        outputs.reshape(inputs.shape),
        grad_input.reshape(inputs.shape),
        small[:width],
        query_grad,
        keyval_grad,
        out_grad,
        small[width : 2 * width],
        gate_grad,
        small[3 * width : 3 * width + ffn],
        up_grad,
        small[3 * width + ffn :],
        down_grad,
        small[2 * width : 3 * width],
    )


def solution(mesh):
    in_specs = (
        P(None, "dp", None),
        P(),
        P("dp", "mp"),
        P("dp", None),
        P("mp", "dp"),
        P(),
        P("dp", "mp"),
        P("mp"),
        P("dp", "mp"),
        P("mp"),
        P("mp", "dp"),
        P(),
        P(None, "dp", None),
        P(None, "dp", None),
    )
    out_specs = (
        P(None, "dp", None),
        P(None, "dp", None),
        P(),
        P("dp", "mp"),
        P("dp", None),
        P("mp", "dp"),
        P(),
        P("dp", "mp"),
        P("mp"),
        P("dp", "mp"),
        P("mp"),
        P("mp", "dp"),
        P(),
    )
    body = partial(shards, total=mesh.shape["dp"])
    return jax.shard_map(body, mesh=mesh, in_specs=in_specs, out_specs=out_specs, check_vma=False)
```

time: 890 us -> 743 us (0.83)
  Pallas kernels: 0 us -> 145 us
  matrix products: 105 us -> 20.1 us
  other arithmetic: 160 us -> 79.6 us
  local copies, waits for them, and re-layouts: 161 us -> 85.5 us
  starting transfers between devices: 124 us -> 91.8 us
  waiting for transfers between devices: 327 us -> 307 us
    pallas_call x0 -> x19, Pallas kernels: none -> 145 us  [the longest x17 142 us: call(): pl.pallas_call(body, out_shape=[jax.ShapeDtypeStruct(shape, dtype) for sh...]
    select_n x37 -> x3, other arithmetic: 56 us -> 3.21 us  [pair(): jnp.where(index == 0, jnp.stack([mine, other], axis=axis), jnp.stack([oth...]
    dot_general x7 -> x0, local copies, waits for them, and re-layouts: 42.2 us -> none  [the longest x4 25.4 us: mm_tn(): lax.dot_general(left, right, (((0,), (0,)), ((), ())), preferred_element_...]
    convert_element_type x16 -> x0, local copies, waits for them, and re-layouts: 34.6 us -> none  [the longest x4 14.2 us: collect_columns(): lax.all_to_all(parts, 'dp', 0, 1, axis_index_groups=grid.sheets, tiled=True)]
    dot_general x7 -> x0, matrix products: 31.3 us -> none  [mm_tn(): lax.dot_general(left, right, (((0,), (0,)), ((), ())), preferred_element_...]
    reshape x2 -> x12, local copies, waits for them, and re-layouts: 1.03 us -> 31.8 us  [the longest x6 21.5 us: split_columns(): shard.reshape(rows, grid.z_count, width // grid.z_count).transpose(1, 0, 2)]
    dot_general x8 -> x3, matrix products: 36.8 us -> 8.48 us  [mm(): return jnp.dot(left, right, preferred_element_type=F32)]
    dot_general x6 -> x2, matrix products: 35.3 us -> 11.6 us  [mm_nt(): lax.dot_general(left, right, (((1,), (1,)), ((), ())), preferred_element_...]
  transfers between devices with their start and end apart: 86 -> 92, of which waited for: 32 -> 37; matrix products, arithmetic and copies ran while one was open for 39% -> 20% of each run, Pallas kernels for 0% -> 20%
where the time goes in v2:
time: 743 us; the launch traced here: 732 us
  waiting for transfers between devices  307 us (41%)
  Pallas kernels  145 us (20%)
  starting transfers between devices  91.8 us (12%)
  local copies, waits for them, and re-layouts  85.5 us (12%)
  other arithmetic  79.6 us (11%)
  matrix products  20.1 us (3%)
    ppermute x24, waiting for transfers between devices, next_z(): return self.queue('z', value, lambda v: lax.ppermute(v, 'dp', self.ring))  175 us
    pallas_call x17, Pallas kernels, call(): pl.pallas_call(body, out_shape=[jax.ShapeDtypeStruct(shape, dtype) for sh...  142 us
    all_to_all x6, waiting for transfers between devices, along_z(): lax.all_to_all(v, 'dp', 0, 0, axis_index_groups=self.lines, tiled=True)  54.3 us
    ppermute x13, waiting for transfers between devices, over_y(): return self.queue('y', value, lambda v: lax.ppermute(v, 'dp', self.swap_y))  51.9 us
    ppermute x25, starting transfers between devices, over_x(): lax.ppermute(v, 'mp', [(0, 1), (1, 0)])  33.4 us
    unnamed x240, local copies, waits for them, and re-layouts  28.7 us
    all_to_all x6, starting transfers between devices, along_z(): lax.all_to_all(v, 'dp', 0, 0, axis_index_groups=self.lines, tiled=True)  26.2 us
    reshape x6, local copies, waits for them, and re-layouts, split_columns(): shard.reshape(rows, grid.z_count, width // grid.z_count).transpose(1, 0, 2)  21.5 us
  transfers between devices with their start and end apart: 92, of which 37 were waited for; matrix products, arithmetic and copies ran while one was open for 20% of the time, Pallas kernels for 20%

profile of v2, /device:TPU:0, one launch (start us, length us, event | category | flops | bytes accessed | tf_op | source)
XLA Modules:
  0.0 732.3 jit_solution(5423067693336866972)
XLA Ops:
  7.4 20.6 %collective-permute-done.refs_0_ = bf16[160,2816]{1,0:T(8,128)(2,1)} collective-permute-done((bf16[160,2816]{1,0:T(8,128)(2,1)S(1)}, bf16[160,2816]{1,0:T(8,128)(2,1)}, u32[]{:S(2)}, u32[]{:S(2)}) %collective-permute-start) | collective-permute-done | bytes 901152 | tf_op jit(solution)/shard_map/ppermute | solution.py:92
  31.0 22.1 %collective-permute-done.1.refs_0_ = bf16[160,2816]{1,0:T(8,128)(2,1)} collective-permute-done((bf16[160,2816]{1,0:T(8,128)(2,1)}, bf16[160,2816]{1,0:T(8,128)(2,1)}, u32[]{:S(2)}, u32[]{:S(2)}) %collective-permute-start.1) | collective-permute-done | bytes 901152 | tf_op jit(solution)/shard_map/ppermute | solution.py:92
  56.2 7.3 collective-permute-done.15.dyo_ref.refs_2_
  63.6 4.6 collective-permute-done.18.dyr_ref.refs_1_
  71.2 11.7 %collective-permute-done.2.refs_0_ = bf16[160,2816]{1,0:T(8,128)(2,1)} collective-permute-done((bf16[160,2816]{1,0:T(8,128)(2,1)}, bf16[160,2816]{1,0:T(8,128)(2,1)}, u32[]{:S(2)}, u32[]{:S(2)}) %collective-permute-start.2) | collective-permute-done | bytes 901152 | tf_op jit(solution)/shard_map/ppermute | solution.py:92
  83.4 8.2 %collective-permute-done.16.dyo_ref.refs_4_ = bf16[96,2560]{1,0:T(8,128)(2,1)S(1)} collective-permute-done((bf16[96,2560]{1,0:T(8,128)(2,1)S(1)}, bf16[96,2560]{1,0:T(8,128)(2,1)S(1)}, u32[]{:S(2)}, u32[]{:S(2)}) %collective-permute-start.16) | collective-permute-done | bytes 491552 | tf_op jit(solution)/shard_map/ppermute | solution.py:92
  95.5 4.4 reshape.436
  107.5 4.6 collective-permute-done.6.refs_1_
  113.7 3.6 all-to-all-start
  120.1 4.4 reshape.438
  128.6 4.3 shard_map.237
  133.8 4.5 shard_map.238
  138.3 4.6 shard_map.239
  143.0 4.6 shard_map.240
  152.2 5.3 fusion.q_ref
  158.3 5.3 all-to-all-start.1
  169.8 5.5 fusion.46
  179.3 4.4 reshape.440
  186.4 8.4 %all-to-all-done.1.own = bf16[4,160,960]{2,1,0:T(8,128)(2,1)} async-done(((bf16[4,160,960]{2,1,0:T(8,128)(2,1)}), bf16[4,160,960]{2,1,0:T(8,128)(2,1)}, u32[]{:S(2)}, u32[]{:S(2)}) %all-to-all-start.1) | async-done | bytes 1228832 | tf_op jit(solution)/shard_map/all_to_all | solution.py:95
  194.8 4.3 all-to-all-start.2
  205.6 35.0 %all-to-all-done.2.own = bf16[4,160,960]{2,1,0:T(8,128)(2,1)} async-done(((bf16[4,160,960]{2,1,0:T(8,128)(2,1)}), bf16[4,160,960]{2,1,0:T(8,128)(2,1)}, u32[]{:S(2)}, u32[]{:S(2)}) %all-to-all-start.2) | async-done | bytes 1228832 | tf_op jit(solution)/shard_map/all_to_all | solution.py:95
  243.2 12.3 %collective-permute-done.35.own_ref.refs_4_ = bf16[96,2560]{1,0:T(8,128)(2,1)S(1)} collective-permute-done((bf16[96,2560]{1,0:T(8,128)(2,1)}, bf16[96,2560]{1,0:T(8,128)(2,1)S(1)}, u32[]{:S(2)}, u32[]{:S(2)}) %collective-permute-start.35) | collective-permute-done | bytes 491552 | tf_op jit(solution)/shard_map/ppermute | solution.py:92
  259.1 9.3 %collective-permute-done.36.own_ref.refs_6_ = bf16[96,2560]{1,0:T(8,128)(2,1)} collective-permute-done((bf16[96,2560]{1,0:T(8,128)(2,1)S(1)}, bf16[96,2560]{1,0:T(8,128)(2,1)}, u32[]{:S(2)}, u32[]{:S(2)}) %collective-permute-start.36) | collective-permute-done | bytes 491552 | tf_op jit(solution)/shard_map/ppermute | solution.py:92
  275.6 5.1 shard_map.242
  280.8 5.9 shard_map.243
  286.7 5.8 shard_map.244
  292.5 18.2 %shard_map.248 = (bf16[192,960]{1,0:T(8,128)(2,1)S(1)}, bf16[192,960]{1,0:T(8,128)(2,1)S(1)}, bf16[192,960]{1,0:T(8,128)(2,1)S(1)}, bf16[96,2560]{1,0:T(8,128)(2...) custom-call(s32[3]{0:T(128)S(1)} %add_add_fusion.6.ranks_ref, ...), custom_call_target="tpu_custom_call" | custom-call | tf_op jit(solution)/shard_map/pallas_call | solution.py:120
  314.9 18.1 %shard_map.247 = (bf16[192,960]{1,0:T(8,128)(2,1)S(1)}, bf16[192,960]{1,0:T(8,128)(2,1)S(1)}, bf16[192,960]{1,0:T(8,128)(2,1)S(1)}, bf16[96,2560]{1,0:T(8,128)(2...) custom-call(s32[3]{0:T(128)S(1)} %add_add_fusion.6.ranks_ref, ...), custom_call_target="tpu_custom_call" | custom-call | tf_op jit(solution)/shard_map/pallas_call | solution.py:120
  339.7 18.2 %shard_map.246 = (bf16[192,960]{1,0:T(8,128)(2,1)S(1)}, bf16[192,960]{1,0:T(8,128)(2,1)S(1)}, bf16[192,960]{1,0:T(8,128)(2,1)S(1)}, bf16[96,2560]{1,0:T(8,128)(2...) custom-call(s32[3]{0:T(128)S(1)} %add_add_fusion.6.ranks_ref, ...), custom_call_target="tpu_custom_call" | custom-call | tf_op jit(solution)/shard_map/pallas_call | solution.py:120
  367.1 17.5 %shard_map.245 = (bf16[192,960]{1,0:T(8,128)(2,1)S(1)}, bf16[192,960]{1,0:T(8,128)(2,1)S(1)}, bf16[192,960]{1,0:T(8,128)(2,1)S(1)}, bf16[96,2560]{1,0:T(8,128)(2...) custom-call(s32[3]{0:T(128)S(1)} %add_add_fusion.6.ranks_ref, ...), custom_call_target="tpu_custom_call" | custom-call | tf_op jit(solution)/shard_map/pallas_call | solution.py:120
  385.5 8.1 %shard_map.251 = (bf16[4,2,160,960]{3,2,1,0:T(8,128)(2,1)}, bf16[4,2,160,960]{3,2,1,0:T(8,128)(2,1)}) custom-call(s32[3]{0:T(128)S(1)} %add_add_fusion.6.ranks_ref, bf16[96,2560]{1,0:T(8,128)(2,1)S(1)} %multiply_convert_fusion.own_ref.refs_0_, bf16[96,2560]{1,0:T(8,128)(2,1)} %collective-permute-done.33.other_ref.refs_1_, ...), custom_call_target="tpu_custom_call" | custom-call | tf_op jit(solution)/shard_map/pallas_call | solution.py:120
  393.8 8.4 %shard_map.252 = (bf16[4,2,160,960]{3,2,1,0:T(8,128)(2,1)}, bf16[4,2,160,960]{3,2,1,0:T(8,128)(2,1)}) custom-call(s32[3]{0:T(128)S(1)} %add_add_fusion.6.ranks_ref, bf16[96,2560]{1,0:T(8,128)(2,1)S(1)} %multiply_convert_fusion.own_ref.refs_0_, bf16[96,2560]{1,0:T(8,128)(2,1)} %collective-permute-done.33.other_ref.refs_1_, ...), custom_call_target="tpu_custom_call" | custom-call | tf_op jit(solution)/shard_map/pallas_call | solution.py:120
  402.7 7.8 %shard_map.253 = (bf16[4,2,160,960]{3,2,1,0:T(8,128)(2,1)}, bf16[4,2,160,960]{3,2,1,0:T(8,128)(2,1)}) custom-call(s32[3]{0:T(128)S(1)} %add_add_fusion.6.ranks_ref, bf16[96,2560]{1,0:T(8,128)(2,1)S(1)} %bitcast.206, bf16[96,2560]{1,0:T(8,128)(2,1)S(1)} %copy-done.18, bf16[96,2560]{1,0:T(8,128)(2,1)S(1)} %copy-done.15, bf16[96,2560]{1,0:T(8,128)(2,1)S(1)} %copy-done.24, ...), custom_call_target="tpu_custom_call" | custom-call | tf_op jit(solution)/shard_map/pallas_call | solution.py:120
  416.6 11.5 %collective-permute-done.46 = bf16[96,2560]{1,0:T(8,128)(2,1)S(1)} collective-permute-done((bf16[96,2560]{1,0:T(8,128)(2,1)S(1)}, bf16[96,2560]{1,0:T(8,128)(2,1)S(1)}, u32[]{:S(2)}, u32[]{:S(2)}) %collective-permute-start.46) | collective-permute-done | bytes 491552 | tf_op jit(solution)/shard_map/ppermute | solution.py:92
  432.2 11.3 %collective-permute-done.47 = bf16[96,2560]{1,0:T(8,128)(2,1)S(1)} collective-permute-done((bf16[96,2560]{1,0:T(8,128)(2,1)S(1)}, bf16[96,2560]{1,0:T(8,128)(2,1)S(1)}, u32[]{:S(2)}, u32[]{:S(2)}) %collective-permute-start.47) | collective-permute-done | bytes 491552 | tf_op jit(solution)/shard_map/ppermute | solution.py:89
  449.4 4.4 shard_map.250
  463.9 12.6 %collective-permute-done.59 = bf16[4,160,960]{2,1,0:T(8,128)(2,1)} collective-permute-done((bf16[4,160,960]{2,1,0:T(8,128)(2,1)S(1)}, bf16[4,160,960]{2,1,0:T(8,128)(2,1)}, u32[]{:S(2)}, u32[]{:S(2)}) %collective-permute-start.59) | collective-permute-done | bytes 1228832 | tf_op jit(solution)/shard_map/ppermute | solution.py:83
  480.8 4.3 all-to-all-start.4
  485.1 6.1 fusion.47
  491.2 14.3 %collective-permute-done.60 = bf16[4,160,960]{2,1,0:T(8,128)(2,1)} collective-permute-done((bf16[4,160,960]{2,1,0:T(8,128)(2,1)}, bf16[4,160,960]{2,1,0:T(8,128)(2,1)}, u32[]{:S(2)}, u32[]{:S(2)}) %collective-permute-start.60) | collective-permute-done | bytes 1228832 | tf_op jit(solution)/shard_map/ppermute | solution.py:83
  508.9 3.6 fusion.5
  514.6 4.5 all-to-all-start.3
  520.5 3.6 fusion.10
  524.0 10.4 %collective-permute-done.61 = bf16[4,160,960]{2,1,0:T(8,128)(2,1)} collective-permute-done((bf16[4,160,960]{2,1,0:T(8,128)(2,1)}, bf16[4,160,960]{2,1,0:T(8,128)(2,1)}, u32[]{:S(2)}, u32[]{:S(2)}) %collective-permute-start.61) | collective-permute-done | bytes 1228832 | tf_op jit(solution)/shard_map/ppermute | solution.py:83
  541.6 3.6 fusion.4
  545.2 4.8 all-to-all-done.3
  550.0 4.3 all-to-all-start.5
  554.4 3.7 shard_map.255
  559.7 9.0 %collective-permute-done.62 = bf16[4,160,1280]{2,1,0:T(8,128)(2,1)} collective-permute-done((bf16[4,160,1280]{2,1,0:T(8,128)(2,1)}, bf16[4,160,1280]{2,1,0:T(8,128)(2,1)}, u32[]{:S(2)}, u32[]{:S(2)}) %collective-permute-start.62) | collective-permute-done | bytes 1638432 | tf_op jit(solution)/shard_map/ppermute | solution.py:83
  579.2 8.8 %collective-permute-done.63 = bf16[160,1280]{1,0:T(8,128)(2,1)} collective-permute-done((bf16[160,1280]{1,0:T(8,128)(2,1)}, bf16[160,1280]{1,0:T(8,128)(2,1)}, u32[]{:S(2)}, u32[]{:S(2)}) %collective-permute-start.63) | collective-permute-done | bytes 409632 | tf_op jit(solution)/shard_map/ppermute | solution.py:92
  590.0 4.0 all-to-all-done.5
  597.4 9.0 %collective-permute-done.64 = bf16[160,1280]{1,0:T(8,128)(2,1)S(1)} collective-permute-done((bf16[160,1280]{1,0:T(8,128)(2,1)}, bf16[160,1280]{1,0:T(8,128)(2,1)S(1)}, u32[]{:S(2)}, u32[]{:S(2)}) %collective-permute-start.64) | collective-permute-done | bytes 409632 | tf_op jit(solution)/shard_map/ppermute | solution.py:92
  611.0 11.4 %collective-permute-done.65 = bf16[96,2560]{1,0:T(8,128)(2,1)S(1)} collective-permute-done((bf16[96,2560]{1,0:T(8,128)(2,1)S(1)}, bf16[96,2560]{1,0:T(8,128)(2,1)S(1)}, u32[]{:S(2)}, u32[]{:S(2)}) %collective-permute-start.65) | collective-permute-done | bytes 491552 | tf_op jit(solution)/shard_map/ppermute | solution.py:92
  623.6 4.6 collective-permute-done.66
  633.2 7.2 collective-permute-done.67
  644.7 12.5 %collective-permute-done.74 = bf16[160,768]{1,0:T(8,128)(2,1)S(1)} collective-permute-done((bf16[160,768]{1,0:T(8,128)(2,1)S(1)}, bf16[160,768]{1,0:T(8,128)(2,1)S(1)}, u32[]{:S(2)}, u32[]{:S(2)}) %collective-permute-start.74) | collective-permute-done | bytes 245792 | tf_op jit(solution)/shard_map/ppermute | solution.py:92
  659.7 6.7 collective-permute-done.75
  669.0 3.2 copy.75
  672.2 4.4 reshape.467
  682.7 6.7 collective-permute-done.78
  692.9 3.4 reshape.462
  704.0 3.4 reshape.464
  721.8 3.3 collective-permute-done.84
  727.1 3.5 collective-permute-done.85
  (522 shorter events, 213.2 us)
Async XLA Ops:
  2.8 25.2 %collective-permute-start = (bf16[160,2816]{1,0:T(8,128)(2,1)S(1)}, bf16[160,2816]{1,0:T(8,128)(2,1)}, u32[]{:S(2)}, u32[]{:S(2)}) collective-permute-start(bf16[160,2816]{1,0:T(8,128)(2,1)S(1)} %pad_maximum_fusion.refs_0_), channel_id=1, source_target_pairs={{0,8},{2,10},{4,12},{6,14},{8,16},{10,18},{12,20},{14,22},{16,24},... | collective-permute-start | bytes 2703368 | tf_op jit(solution)/shard_map/ppermute | solution.py:92
  5.9 22.1 %collective-permute-start.3 = (bf16[160,2816]{1,0:T(8,128)(2,1)S(1)}, bf16[160,2816]{1,0:T(8,128)(2,1)}, u32[]{:S(2)}, u32[]{:S(2)}) collective-permute-start(bf16[160,2816]{1,0:T(8,128)(2,1)S(1)} %pad_maximum_fusion.refs_0_), channel_id=1, source_target_pairs={{0,4},{2,6},{4,0},{6,2},{8,12},{10,14},{12,8},{14,10},{16,20},{18,... | collective-permute-start | bytes 2703368 | tf_op jit(solution)/shard_map/ppermute | solution.py:83
  28.0 25.0 %collective-permute-start.1 = (bf16[160,2816]{1,0:T(8,128)(2,1)}, bf16[160,2816]{1,0:T(8,128)(2,1)}, u32[]{:S(2)}, u32[]{:S(2)}) collective-permute-start(bf16[160,2816]{1,0:T(8,128)(2,1)} %collective-permute-done.refs_0_), channel_id=1, source_target_pairs={{0,8},{2,10},{4,12},{6,14},{8,16},{10,18},{12,20},{14,22},{16,24},... | collective-permute-start | bytes 2703368 | tf_op jit(solution)/shard_map/ppermute | solution.py:92
  28.0 25.0 %collective-permute-start.4 = (bf16[160,2816]{1,0:T(8,128)(2,1)}, bf16[160,2816]{1,0:T(8,128)(2,1)}, u32[]{:S(2)}, u32[]{:S(2)}) collective-permute-start(bf16[160,2816]{1,0:T(8,128)(2,1)} %collective-permute-done.refs_0_), channel_id=1, source_target_pairs={{0,4},{2,6},{4,0},{6,2},{8,12},{10,14},{12,8},{14,10},{16,20},{18,... | collective-permute-start | bytes 2703368 | tf_op jit(solution)/shard_map/ppermute | solution.py:83
  29.6 33.8 %collective-permute-start.15 = (bf16[96,2560]{1,0:T(8,128)(2,1)S(1)}, bf16[96,2560]{1,0:T(8,128)(2,1)S(1)}, u32[]{:S(2)}, u32[]{:S(2)}) collective-permute-start(bf16[96,2560]{1,0:T(8,128)(2,1)S(1)} %bitcast.203), channel_id=1, source_target_pairs={{0,8},{2,10},{4,12},{6,14},{8,16},{10,18},{12,20},{14,22},{16,24},... | collective-permute-start | bytes 1474568 | tf_op jit(solution)/shard_map/ppermute | solution.py:92
  53.0 29.8 %collective-permute-start.2 = (bf16[160,2816]{1,0:T(8,128)(2,1)}, bf16[160,2816]{1,0:T(8,128)(2,1)}, u32[]{:S(2)}, u32[]{:S(2)}) collective-permute-start(bf16[160,2816]{1,0:T(8,128)(2,1)} %collective-permute-done.1.refs_0_), channel_id=1, source_target_pairs={{0,8},{2,10},{4,12},{6,14},{8,16},{10,18},{12,20},{14,22},{16,24},... | collective-permute-start | bytes 2703368 | tf_op jit(solution)/shard_map/ppermute | solution.py:92
  53.0 29.8 %collective-permute-start.5 = (bf16[160,2816]{1,0:T(8,128)(2,1)}, bf16[160,2816]{1,0:T(8,128)(2,1)}, u32[]{:S(2)}, u32[]{:S(2)}) collective-permute-start(bf16[160,2816]{1,0:T(8,128)(2,1)} %collective-permute-done.1.refs_0_), channel_id=1, source_target_pairs={{0,4},{2,6},{4,0},{6,2},{8,12},{10,14},{12,8},{14,10},{16,20},{18,... | collective-permute-start | bytes 2703368 | tf_op jit(solution)/shard_map/ppermute | solution.py:83
  54.6 39.2 %collective-permute-start.13 = (bf16[160,2816]{1,0:T(8,128)(2,1)S(1)}, bf16[160,2816]{1,0:T(8,128)(2,1)}, u32[]{:S(2)}, u32[]{:S(2)}) collective-permute-start(bf16[160,2816]{1,0:T(8,128)(2,1)S(1)} %pad_maximum_fusion.refs_0_), channel_id=1, source_target_pairs={{0,2},{2,0},{4,6},{6,4},{8,10},{10,8},{12,14},{14,12},{16,18},{18,... | collective-permute-start | bytes 2703368 | tf_op jit(solution)/shard_map/ppermute | solution.py:86
  63.5 28.1 %collective-permute-start.16 = (bf16[96,2560]{1,0:T(8,128)(2,1)S(1)}, bf16[96,2560]{1,0:T(8,128)(2,1)S(1)}, u32[]{:S(2)}, u32[]{:S(2)}) collective-permute-start(bf16[96,2560]{1,0:T(8,128)(2,1)S(1)} %collective-permute-done.15.dyo_ref.refs_2_), channel_id=1, source_target_pairs={{0,8},{2,10},{4,12},{6,14},{8,16},{10,18},{12,20},{14,22},{16,24},... | collective-permute-start | bytes 1474568 | tf_op jit(solution)/shard_map/ppermute | solution.py:92
  68.2 24.7 %collective-permute-start.19 = (bf16[96,2560]{1,0:T(8,128)(2,1)S(1)}, bf16[96,2560]{1,0:T(8,128)(2,1)S(1)}, u32[]{:S(2)}, u32[]{:S(2)}) collective-permute-start(bf16[96,2560]{1,0:T(8,128)(2,1)S(1)} %collective-permute-done.15.dyo_ref.refs_2_), channel_id=1, source_target_pairs={{0,1},{1,0},{2,3},{3,2},{4,5},{5,4},{6,7},{7,6},{8,9},{9,8},{10,11... | collective-permute-start | bytes 1474568 | tf_op jit(solution)/shard_map/ppermute | solution.py:89
  82.9 24.1 %collective-permute-start.11 = (bf16[160,2816]{1,0:T(8,128)(2,1)}, bf16[160,2816]{1,0:T(8,128)(2,1)}, u32[]{:S(2)}, u32[]{:S(2)}) collective-permute-start(bf16[160,2816]{1,0:T(8,128)(2,1)} %collective-permute-done.refs_0_), channel_id=1, source_target_pairs={{0,2},{2,0},{4,6},{6,4},{8,10},{10,8},{12,14},{14,12},{16,18},{18,... | collective-permute-start | bytes 2703368 | tf_op jit(solution)/shard_map/ppermute | solution.py:86
  82.9 24.2 %collective-permute-start.14 = (bf16[160,2816]{1,0:T(8,128)(2,1)}, bf16[160,2816]{1,0:T(8,128)(2,1)}, u32[]{:S(2)}, u32[]{:S(2)}) collective-permute-start(bf16[160,2816]{1,0:T(8,128)(2,1)} %collective-permute-done.3.refs_1_), channel_id=1, source_target_pairs={{0,2},{2,0},{4,6},{6,4},{8,10},{10,8},{12,14},{14,12},{16,18},{18,... | collective-permute-start | bytes 2703368 | tf_op jit(solution)/shard_map/ppermute | solution.py:86
  91.6 20.6 %collective-permute-start.6 = (bf16[160,2816]{1,0:T(8,128)(2,1)}, bf16[160,2816]{1,0:T(8,128)(2,1)}, u32[]{:S(2)}, u32[]{:S(2)}) collective-permute-start(bf16[160,2816]{1,0:T(8,128)(2,1)} %collective-permute-done.2.refs_0_), channel_id=1, source_target_pairs={{0,4},{2,6},{4,0},{6,2},{8,12},{10,14},{12,8},{14,10},{16,20},{18,... | collective-permute-start | bytes 2703368 | tf_op jit(solution)/shard_map/ppermute | solution.py:83
  106.5 31.8 %collective-permute-start.9 = (bf16[160,2816]{1,0:T(8,128)(2,1)}, bf16[160,2816]{1,0:T(8,128)(2,1)}, u32[]{:S(2)}, u32[]{:S(2)}) collective-permute-start(bf16[160,2816]{1,0:T(8,128)(2,1)} %collective-permute-done.1.refs_0_), channel_id=1, source_target_pairs={{0,2},{2,0},{4,6},{6,4},{8,10},{10,8},{12,14},{14,12},{16,18},{18,... | collective-permute-start | bytes 2703368 | tf_op jit(solution)/shard_map/ppermute | solution.py:86
  106.5 26.3 %collective-permute-start.12 = (bf16[160,2816]{1,0:T(8,128)(2,1)}, bf16[160,2816]{1,0:T(8,128)(2,1)}, u32[]{:S(2)}, u32[]{:S(2)}) collective-permute-start(bf16[160,2816]{1,0:T(8,128)(2,1)} %collective-permute-done.4.refs_1_), channel_id=1, source_target_pairs={{0,2},{2,0},{4,6},{6,4},{8,10},{10,8},{12,14},{14,12},{16,18},{18,... | collective-permute-start | bytes 2703368 | tf_op jit(solution)/shard_map/ppermute | solution.py:86
  107.0 36.0 %collective-permute-start.7 = (bf16[160,2816]{1,0:T(8,128)(2,1)}, bf16[160,2816]{1,0:T(8,128)(2,1)}, u32[]{:S(2)}, u32[]{:S(2)}) collective-permute-start(bf16[160,2816]{1,0:T(8,128)(2,1)} %collective-permute-done.2.refs_0_), channel_id=1, source_target_pairs={{0,2},{2,0},{4,6},{6,4},{8,10},{10,8},{12,14},{14,12},{16,18},{18,... | collective-permute-start | bytes 2703368 | tf_op jit(solution)/shard_map/ppermute | solution.py:86
  107.1 31.3 %collective-permute-start.10 = (bf16[160,2816]{1,0:T(8,128)(2,1)}, bf16[160,2816]{1,0:T(8,128)(2,1)}, u32[]{:S(2)}, u32[]{:S(2)}) collective-permute-start(bf16[160,2816]{1,0:T(8,128)(2,1)} %collective-permute-done.5.refs_1_), channel_id=1, source_target_pairs={{0,2},{2,0},{4,6},{6,4},{8,10},{10,8},{12,14},{14,12},{16,18},{18,... | collective-permute-start | bytes 2703368 | tf_op jit(solution)/shard_map/ppermute | solution.py:86
  112.1 30.9 %collective-permute-start.8 = (bf16[160,2816]{1,0:T(8,128)(2,1)}, bf16[160,2816]{1,0:T(8,128)(2,1)}, u32[]{:S(2)}, u32[]{:S(2)}) collective-permute-start(bf16[160,2816]{1,0:T(8,128)(2,1)} %collective-permute-done.6.refs_1_), channel_id=1, source_target_pairs={{0,2},{2,0},{4,6},{6,4},{8,10},{10,8},{12,14},{14,12},{16,18},{18,... | collective-permute-start | bytes 2703368 | tf_op jit(solution)/shard_map/ppermute | solution.py:86
  113.7 44.6 %all-to-all-start = ((bf16[4,160,960]{2,1,0:T(8,128)(2,1)}), bf16[4,160,960]{2,1,0:T(8,128)(2,1)S(1)}, u32[]{:S(2)}, u32[]{:S(2)}) async-start(bf16[4,160,960]{2,1,0:T(8,128)(2,1)} %bitcast.238), calls=%async_computation | async-start | bytes 2621440 | tf_op jit(solution)/shard_map/all_to_all | solution.py:95
  132.8 18.4 %collective-permute-start.21 = (bf16[96,2560]{1,0:T(8,128)(2,1)S(1)}, bf16[96,2560]{1,0:T(8,128)(2,1)S(1)}, u32[]{:S(2)}, u32[]{:S(2)}) collective-permute-start(bf16[96,2560]{1,0:T(8,128)(2,1)S(1)} %copy-done.26), channel_id=1, source_target_pairs={{0,1},{1,0},{2,3},{3,2},{4,5},{5,4},{6,7},{7,6},{8,9},{9,8},{10,11... | collective-permute-start | bytes 1474568 | tf_op jit(solution)/shard_map/ppermute | solution.py:89
  158.3 36.5 %all-to-all-start.1 = ((bf16[4,160,960]{2,1,0:T(8,128)(2,1)}), bf16[4,160,960]{2,1,0:T(8,128)(2,1)}, u32[]{:S(2)}, u32[]{:S(2)}) async-start(bf16[4,160,960]{2,1,0:T(8,128)(2,1)} %bitcast.239), calls=%async_computation.1 | async-start | bytes 2621440 | tf_op jit(solution)/shard_map/all_to_all | solution.py:95
  163.5 37.0 %collective-permute-start.24 = (bf16[4,160,960]{2,1,0:T(8,128)(2,1)S(1)}, bf16[4,160,960]{2,1,0:T(8,128)(2,1)}, u32[]{:S(2)}, u32[]{:S(2)}) collective-permute-start(bf16[4,160,960]{2,1,0:T(8,128)(2,1)S(1)} %all-to-all-done.own), channel_id=1, source_target_pairs={{0,4},{2,6},{4,0},{6,2},{8,12},{10,14},{12,8},{14,10},{16,20},{18,... | collective-permute-start | bytes 3686408 | tf_op jit(solution)/shard_map/ppermute | solution.py:83
  176.8 24.8 %collective-permute-start.23 = (bf16[96,2560]{1,0:T(8,128)(2,1)}, bf16[96,2560]{1,0:T(8,128)(2,1)S(1)}, u32[]{:S(2)}, u32[]{:S(2)}) collective-permute-start(bf16[96,2560]{1,0:T(8,128)(2,1)} %bitcast.18), channel_id=1, source_target_pairs={{0,1},{1,0},{2,3},{3,2},{4,5},{5,4},{6,7},{7,6},{8,9},{9,8},{10,11... | collective-permute-start | bytes 1474568 | tf_op jit(solution)/shard_map/ppermute | solution.py:89
  194.8 45.8 %all-to-all-start.2 = ((bf16[4,160,960]{2,1,0:T(8,128)(2,1)}), bf16[4,160,960]{2,1,0:T(8,128)(2,1)}, u32[]{:S(2)}, u32[]{:S(2)}) async-start(bf16[4,160,960]{2,1,0:T(8,128)(2,1)} %bitcast.240), calls=%async_computation.2 | async-start | bytes 2621440 | tf_op jit(solution)/shard_map/all_to_all | solution.py:95
  200.5 40.0 %collective-permute-start.27 = (bf16[4,160,960]{2,1,0:T(8,128)(2,1)}, bf16[4,160,960]{2,1,0:T(8,128)(2,1)}, u32[]{:S(2)}, u32[]{:S(2)}) collective-permute-start(bf16[4,160,960]{2,1,0:T(8,128)(2,1)} %all-to-all-done.1.own), channel_id=1, source_target_pairs={{0,4},{2,6},{4,0},{6,2},{8,12},{10,14},{12,8},{14,10},{16,20},{18,... | collective-permute-start | bytes 3686408 | tf_op jit(solution)/shard_map/ppermute | solution.py:83
  202.1 39.5 %collective-permute-start.34 = (bf16[96,2560]{1,0:T(8,128)(2,1)S(1)}, bf16[96,2560]{1,0:T(8,128)(2,1)}, u32[]{:S(2)}, u32[]{:S(2)}) collective-permute-start(bf16[96,2560]{1,0:T(8,128)(2,1)S(1)} %multiply_convert_fusion.own_ref.refs_0_), channel_id=1, source_target_pairs={{0,8},{2,10},{4,12},{6,14},{8,16},{10,18},{12,20},{14,22},{16,24},... | collective-permute-start | bytes 1474568 | tf_op jit(solution)/shard_map/ppermute | solution.py:92
  204.1 37.5 %collective-permute-start.33 = (bf16[96,2560]{1,0:T(8,128)(2,1)S(1)}, bf16[96,2560]{1,0:T(8,128)(2,1)}, u32[]{:S(2)}, u32[]{:S(2)}) collective-permute-start(bf16[96,2560]{1,0:T(8,128)(2,1)S(1)} %multiply_convert_fusion.own_ref.refs_0_), channel_id=1, source_target_pairs={{0,1},{1,0},{2,3},{3,2},{4,5},{5,4},{6,7},{7,6},{8,9},{9,8},{10,11... | collective-permute-start | bytes 1474568 | tf_op jit(solution)/shard_map/ppermute | solution.py:89
  205.6 53.0 %collective-permute-start.25 = (bf16[4,160,960]{2,1,0:T(8,128)(2,1)S(1)}, bf16[4,160,960]{2,1,0:T(8,128)(2,1)}, u32[]{:S(2)}, u32[]{:S(2)}) collective-permute-start(bf16[4,160,960]{2,1,0:T(8,128)(2,1)S(1)} %all-to-all-done.own), channel_id=1, source_target_pairs={{0,2},{2,0},{4,6},{6,4},{8,10},{10,8},{12,14},{14,12},{16,18},{18,... | collective-permute-start | bytes 3686408 | tf_op jit(solution)/shard_map/ppermute | solution.py:86
  240.6 30.0 %collective-permute-start.30 = (bf16[4,160,960]{2,1,0:T(8,128)(2,1)}, bf16[4,160,960]{2,1,0:T(8,128)(2,1)}, u32[]{:S(2)}, u32[]{:S(2)}) collective-permute-start(bf16[4,160,960]{2,1,0:T(8,128)(2,1)} %all-to-all-done.2.own), channel_id=1, source_target_pairs={{0,4},{2,6},{4,0},{6,2},{8,12},{10,14},{12,8},{14,10},{16,20},{18,... | collective-permute-start | bytes 3686408 | tf_op jit(solution)/shard_map/ppermute | solution.py:83
  258.6 22.2 %collective-permute-start.28 = (bf16[4,160,960]{2,1,0:T(8,128)(2,1)}, bf16[4,160,960]{2,1,0:T(8,128)(2,1)}, u32[]{:S(2)}, u32[]{:S(2)}) collective-permute-start(bf16[4,160,960]{2,1,0:T(8,128)(2,1)} %all-to-all-done.1.own), channel_id=1, source_target_pairs={{0,2},{2,0},{4,6},{6,4},{8,10},{10,8},{12,14},{14,12},{16,18},{18,... | collective-permute-start | bytes 3686408 | tf_op jit(solution)/shard_map/ppermute | solution.py:86
  269.2 17.5 %collective-permute-start.31 = (bf16[4,160,960]{2,1,0:T(8,128)(2,1)}, bf16[4,160,960]{2,1,0:T(8,128)(2,1)}, u32[]{:S(2)}, u32[]{:S(2)}) collective-permute-start(bf16[4,160,960]{2,1,0:T(8,128)(2,1)} %all-to-all-done.2.own), channel_id=1, source_target_pairs={{0,2},{2,0},{4,6},{6,4},{8,10},{10,8},{12,14},{14,12},{16,18},{18,... | collective-permute-start | bytes 3686408 | tf_op jit(solution)/shard_map/ppermute | solution.py:86
  270.6 16.1 %collective-permute-start.32 = (bf16[4,160,960]{2,1,0:T(8,128)(2,1)}, bf16[4,160,960]{2,1,0:T(8,128)(2,1)}, u32[]{:S(2)}, u32[]{:S(2)}) collective-permute-start(bf16[4,160,960]{2,1,0:T(8,128)(2,1)} %collective-permute-done.30.side), channel_id=1, source_target_pairs={{0,2},{2,0},{4,6},{6,4},{8,10},{10,8},{12,14},{14,12},{16,18},{18,... | collective-permute-start | bytes 3686408 | tf_op jit(solution)/shard_map/ppermute | solution.py:86
  271.7 42.1 %collective-permute-start.39 = (bf16[96,2560]{1,0:T(8,128)(2,1)}, bf16[96,2560]{1,0:T(8,128)(2,1)}, u32[]{:S(2)}, u32[]{:S(2)}) collective-permute-start(bf16[96,2560]{1,0:T(8,128)(2,1)} %collective-permute-done.36.own_ref.refs_6_), channel_id=1, source_target_pairs={{0,1},{1,0},{2,3},{3,2},{4,5},{5,4},{6,7},{7,6},{8,9},{9,8},{10,11... | collective-permute-start | bytes 1474568 | tf_op jit(solution)/shard_map/ppermute | solution.py:89
  313.8 21.4 %collective-permute-start.40 = (bf16[96,2560]{1,0:T(8,128)(2,1)S(1)}, bf16[96,2560]{1,0:T(8,128)(2,1)S(1)}, u32[]{:S(2)}, u32[]{:S(2)}) collective-permute-start(bf16[96,2560]{1,0:T(8,128)(2,1)S(1)} %get-tuple-element.174), channel_id=1, source_target_pairs={{0,1},{1,0},{2,3},{3,2},{4,5},{5,4},{6,7},{7,6},{8,9},{9,8},{10,11... | collective-permute-start | bytes 1474568 | tf_op jit(solution)/shard_map/ppermute | solution.py:89
  336.2 24.8 %collective-permute-start.44 = (bf16[96,2560]{1,0:T(8,128)(2,1)}, bf16[96,2560]{1,0:T(8,128)(2,1)}, u32[]{:S(2)}, u32[]{:S(2)}) collective-permute-start(bf16[96,2560]{1,0:T(8,128)(2,1)} %add_convert_fusion.12), channel_id=1, source_target_pairs={{0,8},{2,10},{4,12},{6,14},{8,16},{10,18},{12,20},{14,22},{16,24},... | collective-permute-start | bytes 1474568 | tf_op jit(solution)/shard_map/ppermute | solution.py:92
  336.4 24.6 %collective-permute-start.41 = (bf16[96,2560]{1,0:T(8,128)(2,1)}, bf16[96,2560]{1,0:T(8,128)(2,1)}, u32[]{:S(2)}, u32[]{:S(2)}) collective-permute-start(bf16[96,2560]{1,0:T(8,128)(2,1)} %get-tuple-element.175), channel_id=1, source_target_pairs={{0,1},{1,0},{2,3},{3,2},{4,5},{5,4},{6,7},{7,6},{8,9},{9,8},{10,11... | collective-permute-start | bytes 1474568 | tf_op jit(solution)/shard_map/ppermute | solution.py:89
  363.5 47.3 %collective-permute-start.45 = (bf16[96,2560]{1,0:T(8,128)(2,1)}, bf16[96,2560]{1,0:T(8,128)(2,1)}, u32[]{:S(2)}, u32[]{:S(2)}) collective-permute-start(bf16[96,2560]{1,0:T(8,128)(2,1)} %add_convert_fusion.11), channel_id=1, source_target_pairs={{0,8},{2,10},{4,12},{6,14},{8,16},{10,18},{12,20},{14,22},{16,24},... | collective-permute-start | bytes 1474568 | tf_op jit(solution)/shard_map/ppermute | solution.py:92
  363.9 46.9 %collective-permute-start.42 = (bf16[96,2560]{1,0:T(8,128)(2,1)}, bf16[96,2560]{1,0:T(8,128)(2,1)}, u32[]{:S(2)}, u32[]{:S(2)}) collective-permute-start(bf16[96,2560]{1,0:T(8,128)(2,1)} %get-tuple-element.176), channel_id=1, source_target_pairs={{0,1},{1,0},{2,3},{3,2},{4,5},{5,4},{6,7},{7,6},{8,9},{9,8},{10,11... | collective-permute-start | bytes 1474568 | tf_op jit(solution)/shard_map/ppermute | solution.py:89
  393.6 64.1 %collective-permute-start.56 = (bf16[4,2,160,960]{3,2,1,0:T(8,128)(2,1)}, bf16[4,2,160,960]{3,2,1,0:T(8,128)(2,1)}, u32[]{:S(2)}, u32[]{:S(2)}) collective-permute-start(bf16[4,2,160,960]{3,2,1,0:T(8,128)(2,1)} %get-tuple-element.206), channel_id=1, source_target_pairs={{0,2},{2,0},{4,6},{6,4},{8,10},{10,8},{12,14},{14,12},{16,18},{18,... | collective-permute-start | bytes 7372808 | tf_op jit(solution)/shard_map/ppermute | solution.py:86
  402.2 58.6 %collective-permute-start.57 = (bf16[4,2,160,960]{3,2,1,0:T(8,128)(2,1)}, bf16[4,2,160,960]{3,2,1,0:T(8,128)(2,1)}, u32[]{:S(2)}, u32[]{:S(2)}) collective-permute-start(bf16[4,2,160,960]{3,2,1,0:T(8,128)(2,1)} %get-tuple-element.212), channel_id=1, source_target_pairs={{0,2},{2,0},{4,6},{6,4},{8,10},{10,8},{12,14},{14,12},{16,18},{18,... | collective-permute-start | bytes 7372808 | tf_op jit(solution)/shard_map/ppermute | solution.py:86
  410.6 33.2 %collective-permute-start.58 = (bf16[4,2,160,960]{3,2,1,0:T(8,128)(2,1)}, bf16[4,2,160,960]{3,2,1,0:T(8,128)(2,1)S(1)}, u32[]{:S(2)}, u32[]{:S(2)}) collective-permute-start(bf16[4,2,160,960]{3,2,1,0:T(8,128)(2,1)} %get-tuple-element.218), channel_id=1, source_target_pairs={{0,2},{2,0},{4,6},{6,4},{8,10},{10,8},{12,14},{14,12},{16,18},{18,... | collective-permute-start | bytes 7372808 | tf_op jit(solution)/shard_map/ppermute | solution.py:86
  446.8 29.8 %collective-permute-start.59 = (bf16[4,160,960]{2,1,0:T(8,128)(2,1)S(1)}, bf16[4,160,960]{2,1,0:T(8,128)(2,1)}, u32[]{:S(2)}, u32[]{:S(2)}) collective-permute-start(bf16[4,160,960]{2,1,0:T(8,128)(2,1)S(1)} %fusion.13), channel_id=1, source_target_pairs={{0,4},{2,6},{4,0},{6,2},{8,12},{10,14},{12,8},{14,10},{16,20},{18,... | collective-permute-start | bytes 3686408 | tf_op jit(solution)/shard_map/ppermute | solution.py:83
  457.7 62.7 %collective-permute-start.55 = (bf16[4,2,160,1280]{3,2,1,0:T(8,128)(2,1)}, bf16[4,2,160,1280]{3,2,1,0:T(8,128)(2,1)}, u32[]{:S(2)}, u32[]{:S(2)}) collective-permute-start(bf16[4,2,160,1280]{3,2,1,0:T(8,128)(2,1)} %get-tuple-element.200), channel_id=1, source_target_pairs={{0,2},{2,0},{4,6},{6,4},{8,10},{10,8},{12,14},{14,12},{16,18},{18,... | collective-permute-start | bytes 9830408 | tf_op jit(solution)/shard_map/ppermute | solution.py:86
  476.5 29.0 %collective-permute-start.60 = (bf16[4,160,960]{2,1,0:T(8,128)(2,1)}, bf16[4,160,960]{2,1,0:T(8,128)(2,1)}, u32[]{:S(2)}, u32[]{:S(2)}) collective-permute-start(bf16[4,160,960]{2,1,0:T(8,128)(2,1)} %fusion.12), channel_id=1, source_target_pairs={{0,4},{2,6},{4,0},{6,2},{8,12},{10,14},{12,8},{14,10},{16,20},{18,... | collective-permute-start | bytes 3686408 | tf_op jit(solution)/shard_map/ppermute | solution.py:83
  480.8 33.9 %all-to-all-start.4 = ((bf16[4,160,960]{2,1,0:T(8,128)(2,1)}), bf16[4,160,960]{2,1,0:T(8,128)(2,1)}, u32[]{:S(2)}, u32[]{:S(2)}) async-start(bf16[4,160,960]{2,1,0:T(8,128)(2,1)} %fusion.3), calls=%async_computation.4 | async-start | bytes 2621440 | tf_op jit(solution)/shard_map/all_to_all | solution.py:95
  505.5 28.9 %collective-permute-start.61 = (bf16[4,160,960]{2,1,0:T(8,128)(2,1)}, bf16[4,160,960]{2,1,0:T(8,128)(2,1)}, u32[]{:S(2)}, u32[]{:S(2)}) collective-permute-start(bf16[4,160,960]{2,1,0:T(8,128)(2,1)} %fusion.11), channel_id=1, source_target_pairs={{0,4},{2,6},{4,0},{6,2},{8,12},{10,14},{12,8},{14,10},{16,20},{18,... | collective-permute-start | bytes 3686408 | tf_op jit(solution)/shard_map/ppermute | solution.py:83
  507.4 28.1 %collective-permute-start.49 = (bf16[96,2560]{1,0:T(8,128)(2,1)}, bf16[96,2560]{1,0:T(8,128)(2,1)}, u32[]{:S(2)}, u32[]{:S(2)}) collective-permute-start(bf16[96,2560]{1,0:T(8,128)(2,1)} %bitcast.36), channel_id=1, source_target_pairs={{0,1},{1,0},{2,3},{3,2},{4,5},{5,4},{6,7},{7,6},{8,9},{9,8},{10,11... | collective-permute-start | bytes 1474568 | tf_op jit(solution)/shard_map/ppermute | solution.py:89
  514.6 35.4 %all-to-all-start.3 = ((bf16[4,160,960]{2,1,0:T(8,128)(2,1)}), bf16[4,160,960]{2,1,0:T(8,128)(2,1)}, u32[]{:S(2)}, u32[]{:S(2)}) async-start(bf16[4,160,960]{2,1,0:T(8,128)(2,1)} %fusion.5), calls=%async_computation.3 | async-start | bytes 2621440 | tf_op jit(solution)/shard_map/all_to_all | solution.py:95
  534.4 34.3 %collective-permute-start.62 = (bf16[4,160,1280]{2,1,0:T(8,128)(2,1)}, bf16[4,160,1280]{2,1,0:T(8,128)(2,1)}, u32[]{:S(2)}, u32[]{:S(2)}) collective-permute-start(bf16[4,160,1280]{2,1,0:T(8,128)(2,1)} %fusion.10), channel_id=1, source_target_pairs={{0,4},{2,6},{4,0},{6,2},{8,12},{10,14},{12,8},{14,10},{16,20},{18,... | collective-permute-start | bytes 4915208 | tf_op jit(solution)/shard_map/ppermute | solution.py:83
  540.1 18.0 %collective-permute-start.50 = (bf16[96,2560]{1,0:T(8,128)(2,1)}, bf16[96,2560]{1,0:T(8,128)(2,1)S(1)}, u32[]{:S(2)}, u32[]{:S(2)}) collective-permute-start(bf16[96,2560]{1,0:T(8,128)(2,1)} %fusion.21), channel_id=1, source_target_pairs={{0,1},{1,0},{2,3},{3,2},{4,5},{5,4},{6,7},{7,6},{8,9},{9,8},{10,11... | collective-permute-start | bytes 1474568 | tf_op jit(solution)/shard_map/ppermute | solution.py:89
  550.0 44.0 %all-to-all-start.5 = ((bf16[4,160,960]{2,1,0:T(8,128)(2,1)}), bf16[4,160,960]{2,1,0:T(8,128)(2,1)}, u32[]{:S(2)}, u32[]{:S(2)}) async-start(bf16[4,160,960]{2,1,0:T(8,128)(2,1)} %fusion.4), calls=%async_computation.5 | async-start | bytes 2621440 | tf_op jit(solution)/shard_map/all_to_all | solution.py:95
  558.1 48.4 %collective-permute-start.71 = (bf16[4,2,160,768]{3,2,1,0:T(8,128)(2,1)}, bf16[4,2,160,768]{3,2,1,0:T(8,128)(2,1)}, u32[]{:S(2)}, u32[]{:S(2)}) collective-permute-start(bf16[4,2,160,768]{3,2,1,0:T(8,128)(2,1)} %get-tuple-element.236), channel_id=1, source_target_pairs={{0,2},{2,0},{4,6},{6,4},{8,10},{10,8},{12,14},{14,12},{16,18},{18,... | collective-permute-start | bytes 5898248 | tf_op jit(solution)/shard_map/ppermute | solution.py:86
  558.1 20.1 %collective-permute-start.51 = (bf16[96,2560]{1,0:T(8,128)(2,1)}, bf16[96,2560]{1,0:T(8,128)(2,1)}, u32[]{:S(2)}, u32[]{:S(2)}) collective-permute-start(bf16[96,2560]{1,0:T(8,128)(2,1)} %get-tuple-element.192), channel_id=1, source_target_pairs={{0,1},{1,0},{2,3},{3,2},{4,5},{5,4},{6,7},{7,6},{8,9},{9,8},{10,11... | collective-permute-start | bytes 1474568 | tf_op jit(solution)/shard_map/ppermute | solution.py:89
  578.1 50.2 %collective-permute-start.70 = (bf16[4,2,160,768]{3,2,0,1:T(8,128)(2,1)}, bf16[4,2,160,768]{3,2,0,1:T(8,128)(2,1)}, u32[]{:S(2)}, u32[]{:S(2)}) collective-permute-start(bf16[4,2,160,768]{3,2,0,1:T(8,128)(2,1)} %copy.68), channel_id=1, source_target_pairs={{0,2},{2,0},{4,6},{6,4},{8,10},{10,8},{12,14},{14,12},{16,18},{18,... | collective-permute-start | bytes 5898248 | tf_op jit(solution)/shard_map/ppermute | solution.py:86
  578.2 17.7 %collective-permute-start.52 = (bf16[96,2560]{1,0:T(8,128)(2,1)S(1)}, bf16[96,2560]{1,0:T(8,128)(2,1)}, u32[]{:S(2)}, u32[]{:S(2)}) collective-permute-start(bf16[96,2560]{1,0:T(8,128)(2,1)S(1)} %copy-done.84), channel_id=1, source_target_pairs={{0,1},{1,0},{2,3},{3,2},{4,5},{5,4},{6,7},{7,6},{8,9},{9,8},{10,11... | collective-permute-start | bytes 1474568 | tf_op jit(solution)/shard_map/ppermute | solution.py:89
  595.9 37.3 %collective-permute-start.53 = (bf16[96,2560]{1,0:T(8,128)(2,1)S(1)}, bf16[96,2560]{1,0:T(8,128)(2,1)S(1)}, u32[]{:S(2)}, u32[]{:S(2)}) collective-permute-start(bf16[96,2560]{1,0:T(8,128)(2,1)S(1)} %copy-done.82), channel_id=1, source_target_pairs={{0,1},{1,0},{2,3},{3,2},{4,5},{5,4},{6,7},{7,6},{8,9},{9,8},{10,11... | collective-permute-start | bytes 1474568 | tf_op jit(solution)/shard_map/ppermute | solution.py:89
  606.4 16.0 %collective-permute-start.65 = (bf16[96,2560]{1,0:T(8,128)(2,1)S(1)}, bf16[96,2560]{1,0:T(8,128)(2,1)S(1)}, u32[]{:S(2)}, u32[]{:S(2)}) collective-permute-start(bf16[96,2560]{1,0:T(8,128)(2,1)S(1)} %add_convert_fusion.9), channel_id=1, source_target_pairs={{0,8},{2,10},{4,12},{6,14},{8,16},{10,18},{12,20},{14,22},{16,24},... | collective-permute-start | bytes 1474568 | tf_op jit(solution)/shard_map/ppermute | solution.py:92
  608.3 22.2 %collective-permute-start.72 = (bf16[4,160,768]{2,1,0:T(8,128)(2,1)S(1)}, bf16[4,160,768]{2,1,0:T(8,128)(2,1)S(1)}, u32[]{:S(2)}, u32[]{:S(2)}) collective-permute-start(bf16[4,160,768]{2,1,0:T(8,128)(2,1)S(1)} %fusion.17), channel_id=1, source_target_pairs={{0,4},{2,6},{4,0},{6,2},{8,12},{10,14},{12,8},{14,10},{16,20},{18,... | collective-permute-start | bytes 2949128 | tf_op jit(solution)/shard_map/ppermute | solution.py:83
  610.4 17.9 %collective-permute-start.66 = (bf16[160,1280]{1,0:T(8,128)(2,1)S(1)}, bf16[160,1280]{1,0:T(8,128)(2,1)S(1)}, u32[]{:S(2)}, u32[]{:S(2)}) collective-permute-start(bf16[160,1280]{1,0:T(8,128)(2,1)S(1)} %fusion.26), channel_id=1, source_target_pairs={{0,8},{2,10},{4,12},{6,14},{8,16},{10,18},{12,20},{14,22},{16,24},... | collective-permute-start | bytes 1228808 | tf_op jit(solution)/shard_map/ppermute | solution.py:92
  630.5 26.8 %collective-permute-start.73 = (bf16[4,160,768]{2,1,0:T(8,128)(2,1)S(1)}, bf16[4,160,768]{2,1,0:T(8,128)(2,1)S(1)}, u32[]{:S(2)}, u32[]{:S(2)}) collective-permute-start(bf16[4,160,768]{2,1,0:T(8,128)(2,1)S(1)} %fusion.16), channel_id=1, source_target_pairs={{0,4},{2,6},{4,0},{6,2},{8,12},{10,14},{12,8},{14,10},{16,20},{18,... | collective-permute-start | bytes 2949128 | tf_op jit(solution)/shard_map/ppermute | solution.py:83
  640.6 16.6 %collective-permute-start.68 = (bf16[96,2560]{1,0:T(8,128)(2,1)S(1)}, bf16[96,2560]{1,0:T(8,128)(2,1)S(1)}, u32[]{:S(2)}, u32[]{:S(2)}) collective-permute-start(bf16[96,2560]{1,0:T(8,128)(2,1)S(1)} %add_convert_fusion.7), channel_id=1, source_target_pairs={{0,8},{2,10},{4,12},{6,14},{8,16},{10,18},{12,20},{14,22},{16,24},... | collective-permute-start | bytes 1474568 | tf_op jit(solution)/shard_map/ppermute | solution.py:92
  640.7 16.5 %collective-permute-start.74 = (bf16[160,768]{1,0:T(8,128)(2,1)S(1)}, bf16[160,768]{1,0:T(8,128)(2,1)S(1)}, u32[]{:S(2)}, u32[]{:S(2)}) collective-permute-start(bf16[160,768]{1,0:T(8,128)(2,1)S(1)} %dynamic-slice_bitcast_fusion.1), channel_id=1, source_target_pairs={{0,8},{2,10},{4,12},{6,14},{8,16},{10,18},{12,20},{14,22},{16,24},... | collective-permute-start | bytes 737288 | tf_op jit(solution)/shard_map/ppermute | solution.py:92
  643.2 35.9 %collective-permute-start.54 = (bf16[96,2560]{1,0:T(8,128)(2,1)S(1)}, bf16[96,2560]{1,0:T(8,128)(2,1)}, u32[]{:S(2)}, u32[]{:S(2)}) collective-permute-start(bf16[96,2560]{1,0:T(8,128)(2,1)S(1)} %copy-done.80), channel_id=1, source_target_pairs={{0,1},{1,0},{2,3},{3,2},{4,5},{5,4},{6,7},{7,6},{8,9},{9,8},{10,11... | collective-permute-start | bytes 1474568 | tf_op jit(solution)/shard_map/ppermute | solution.py:89
  681.2 18.0 %collective-permute-start.69 = (bf16[96,2560]{1,0:T(8,128)(2,1)}, bf16[96,2560]{1,0:T(8,128)(2,1)}, u32[]{:S(2)}, u32[]{:S(2)}) collective-permute-start(bf16[96,2560]{1,0:T(8,128)(2,1)} %add_convert_fusion.6), channel_id=1, source_target_pairs={{0,1},{1,0},{2,3},{3,2},{4,5},{5,4},{6,7},{7,6},{8,9},{9,8},{10,11... | collective-permute-start | bytes 1474568 | tf_op jit(solution)/shard_map/ppermute | solution.py:89
  (147 other events, 1382.0 us)

commit v3 on v2

v3 whole, which is shorter than its diff:
```python
import math
from functools import partial

import jax
import jax.numpy as jnp
from jax import lax
from jax.experimental import pallas as pl
from jax.experimental.pallas import tpu as pltpu
from jax.sharding import PartitionSpec as P

EPS = 1e-06
F32 = jnp.float32
BF16 = jnp.bfloat16
VMEM = 24 * 2**20
SCALE = 4.0
GELU_A, GELU_B = math.sqrt(2.0 / math.pi), 0.044715


def positions(segment):
    count = segment.shape[0]
    index = jnp.arange(count, dtype=jnp.int32)
    fresh = jnp.concatenate([jnp.ones((1,), jnp.bool_), segment[1:] != segment[:-1]])
    starts = lax.cummax(jnp.where(fresh, index, 0), axis=0)
    return (index - starts).astype(F32)


def inv_root(values):
    return lax.rsqrt(jnp.mean(values * values, axis=-1, keepdims=True) + EPS)


def norm_back(values, factor, gain, grad_norm):
    scaled = gain * grad_norm
    return factor * scaled - values * factor**3 * jnp.mean(scaled * values, axis=-1, keepdims=True)


def mm(left, right):
    return jnp.dot(left, right, preferred_element_type=F32)


def mm_nt(left, right):
    return lax.dot_general(left, right, (((1,), (1,)), ((), ())), preferred_element_type=F32)


def mm_tn(left, right):
    return lax.dot_general(left, right, (((0,), (0,)), ((), ())), preferred_element_type=F32)


class Grid:
    def __init__(self, total):
        self.z_count = total // 4
        spots = [(z, y, c) for z in range(self.z_count) for y in range(2) for c in range(2)]
        at = lambda z, y, c: (z * 2 + y) * 2 + c
        self.swap_y = [(at(z, y, c), at(z, 1 - y, c)) for z, y, c in spots]
        self.swap_c = [(at(z, y, c), at(z, y, 1 - c)) for z, y, c in spots]
        self.ring = lambda step: [
            (at(z, y, c), at((z + step) % self.z_count, y, c)) for z, y, c in spots
        ]
        self.flips = []
        step = 1
        while step < self.z_count:
            self.flips.append([(at(z, y, c), at(z ^ step, y, c)) for z, y, c in spots])
            step *= 2
        self.lines = [
            [at(z, y, c) for z in range(self.z_count)] for y in range(2) for c in range(2)
        ]
        index = lax.axis_index("dp")
        self.c = index % 2
        self.y = (index // 2) % 2
        self.z = index // 4
        self.x = lax.axis_index("mp")
        self.token = jnp.zeros((), F32)

    def wait(self, *values):
        self.token = lax.optimization_barrier((self.token, values))[0]

    def gate(self, value):
        return lax.optimization_barrier((value, self.token))[0]

    def over_y(self, value):
        return lax.ppermute(self.gate(value), "dp", self.swap_y)

    def over_c(self, value):
        return lax.ppermute(self.gate(value), "dp", self.swap_c)

    def over_x(self, value):
        return lax.ppermute(self.gate(value), "mp", [(0, 1), (1, 0)])

    def next_z(self, value, step=1):
        return lax.ppermute(self.gate(value), "dp", self.ring(step))

    def along_z(self, value):
        value = self.gate(value)
        return lax.all_to_all(value, "dp", 0, 0, axis_index_groups=self.lines, tiled=True)

    def behind(self, step):
        return lax.rem(self.z - step + 2 * self.z_count, self.z_count)


def pair(index, mine, other, axis):
    return jnp.where(
        index == 0, jnp.stack([mine, other], axis=axis), jnp.stack([other, mine], axis=axis)
    )


def take(value, index, axis):
    return lax.dynamic_index_in_dim(value, index, axis, keepdims=False)


def cost(micros):
    micros = micros / SCALE
    flops, moved = int(micros * 1.15e9), int(micros * 3.69e6)
    return pl.CostEstimate(flops=flops, bytes_accessed=moved, transcendentals=0)


def call(body, micros, grid, in_specs, outs, out_specs, operands, aliases=None, limit=VMEM):
    return pl.pallas_call(
        body,
        out_shape=[jax.ShapeDtypeStruct(shape, dtype) for shape, dtype in outs],
        grid_spec=pltpu.PrefetchScalarGridSpec(
            num_scalar_prefetch=1,
            grid=grid,
            in_specs=in_specs,
            out_specs=out_specs,
        ),
        input_output_aliases=aliases or {},
        cost_estimate=cost(micros),
        compiler_params=pltpu.CompilerParams(vmem_limit_bytes=limit),
    )(*operands)


def place_slot(ranks, pieces, wholes, z_count, cuts):
    rows, width = pieces[0].shape
    ends = list(cuts[1:]) + [width]
    given = len(wholes)

    def body(ranks_ref, *refs):
        sources, targets = refs[:4], refs[4 + given :]
        y, c = ranks_ref[1], ranks_ref[2]
        spots = [(y, c), (1 - y, c), (y, 1 - c), (1 - y, 1 - c)]
        for source, (at_y, at_c) in zip(sources, spots):
            for target, begin, end in zip(targets, cuts, ends):
                target[0, at_y, at_c] = source[:, begin:end]

    whole_spec = pl.BlockSpec(memory_space=pl.ANY)
    return call(
        body,
        4.0,
        (1,),
        [pl.BlockSpec((rows, width), lambda i, ranks: (0, 0))] * 4 + [whole_spec] * given,
        [((z_count, 2, 2, rows, end - begin), BF16) for begin, end in zip(cuts, ends)],
        [
            pl.BlockSpec((1, 2, 2, rows, end - begin), lambda i, ranks: (ranks[0], 0, 0, 0, 0))
            for begin, end in zip(cuts, ends)
        ],
        (ranks, *pieces, *wholes),
        aliases={5 + number: number for number in range(given)},
        limit=2 * VMEM,
    )


def place_all(ranks, pieces):
    z_count, rows, width = pieces[0].shape

    def body(ranks_ref, own, side, core, both, target):
        y, c = ranks_ref[1], ranks_ref[2]
        target[0, y, c] = own[0]
        target[0, 1 - y, c] = side[0]
        target[0, y, 1 - c] = core[0]
        target[0, 1 - y, 1 - c] = both[0]

    whole = call(
        body,
        4.0,
        (z_count,),
        [pl.BlockSpec((1, rows, width), lambda i, ranks: (i, 0, 0))] * 4,
        [((z_count, 2, 2, rows, width), BF16)],
        [pl.BlockSpec((1, 2, 2, rows, width), lambda i, ranks: (i, 0, 0, 0, 0))],
        (ranks, *pieces),
    )[0]
    return whole.reshape(z_count * 4 * rows, width)


def product(left, right, dtype):
    rows, depth = left.shape
    width = right.shape[1]
    block = 256 if width % 256 == 0 else width

    def body(ranks_ref, left_ref, right_ref, out_ref):
        out_ref[...] = mm(left_ref[...], right_ref[...]).astype(dtype)

    return call(
        body,
        4.5,
        (width // block,),
        [
            pl.BlockSpec((rows, depth), lambda i, ranks: (0, 0)),
            pl.BlockSpec((depth, block), lambda i, ranks: (0, i)),
        ],
        [((rows, width), dtype)],
        [pl.BlockSpec((rows, block), lambda i, ranks: (0, i))],
        (jnp.zeros((1,), jnp.int32), left, right),
    )[0]


def product_nt(ranks, left, right, groups):
    rows, depth = left.shape
    width = right.shape[0]
    block = 512 if width % 512 == 0 else width
    half = rows // groups // 2

    def body(ranks_ref, left_ref, right_ref, own_ref, other_ref):
        whole = mm_nt(left_ref[...], right_ref[...])
        low = ranks_ref[3] == 0
        for group in range(groups):
            at = group * 2 * half
            first, second = whole[at : at + half], whole[at + half : at + 2 * half]
            to = pl.ds(group * half, half)
            own_ref[to, :] = jnp.where(low, first, second)
            other_ref[to, :] = jnp.where(low, second, first).astype(BF16)

    out_spec = pl.BlockSpec((rows // 2, block), lambda i, ranks: (0, i))
    return call(
        body,
        4.0,
        (width // block,),
        [
            pl.BlockSpec((rows, depth), lambda i, ranks: (0, 0)),
            pl.BlockSpec((block, depth), lambda i, ranks: (i, 0)),
        ],
        [((rows // 2, width), F32), ((rows // 2, width), BF16)],
        [out_spec] * 2,
        (ranks, left, right),
    )


def second_norm(x_ref, mine_ref, got_ref, gain_ref, residual_ref, factor_ref, normed_ref):
    residual = x_ref[...].astype(F32) + mine_ref[...] + got_ref[...].astype(F32)
    factor = inv_root(residual)
    residual_ref[...], factor_ref[...] = residual, factor
    normed_ref[...] = (residual * factor * gain_ref[...]).astype(BF16)


def second_norm_back(
    own_ref, got_ref, held_ref, residual_ref, factor_ref, gain_ref, dy_ref,
    grad_ref, grad_b_ref, term_ref,
):
    grad = own_ref[...].astype(F32) + got_ref[...].astype(F32) + held_ref[...].astype(F32)
    residual, factor = residual_ref[...], factor_ref[...]
    term_ref[...] = jnp.sum(grad * residual * factor, axis=0, keepdims=True)
    grad = dy_ref[...].astype(F32) + norm_back(residual, factor, gain_ref[...], grad)
    grad_ref[...], grad_b_ref[...] = grad, grad.astype(BF16)


def first_norm_back(mine_ref, got_ref, x_ref, factor_ref, gain_ref, grad_ref, out_ref, term_ref):
    grad = mine_ref[...] + got_ref[...].astype(F32)
    values, factor = x_ref[...].astype(F32), factor_ref[...]
    term_ref[...] = jnp.sum(grad * values * factor, axis=0, keepdims=True)
    out_ref[...] = (grad_ref[...] + norm_back(values, factor, gain_ref[...], grad)).astype(BF16)


def product_rows(ranks, lefts, groups, z_count):
    features = lefts[0].shape[1]
    width = groups[0][0].shape[1]
    rows = features // (4 * z_count)
    block = math.lcm(4 * rows, 128)
    span = block // (4 * rows)
    rights = [right for group in groups for right in group]
    each = len(groups[0])
    join = lambda parts: parts[0] if len(parts) == 1 else jnp.concatenate(parts, axis=0)

    def body(ranks_ref, *refs):
        left = join([ref[...] for ref in refs[: len(lefts)]])
        right_refs, out_refs = refs[len(lefts) : -outs], refs[-outs:]
        low = ranks_ref[2] == 0
        here = pl.program_id(0)
        for number in range(len(groups)):
            right = join([ref[...] for ref in right_refs[number * each : (number + 1) * each]])
            keep, sends = out_refs[number], out_refs[len(groups) + number * z_count :]
            whole = mm_tn(left, right)
            for place in range(span):
                for y in range(2):
                    at = (place * 4 + y * 2) * rows
                    first, second = whole[at : at + rows], whole[at + rows : at + 2 * rows]
                    keep[place, y] = jnp.where(low, first, second).astype(BF16)
                    other = jnp.where(low, second, first).astype(BF16)
                    for z in range(place, z_count, span):

                        @pl.when(here == z // span)
                        def _(target=sends[z], y=y, other=other):
                            target[y] = other

    outs = len(groups) * (1 + z_count)
    keep_spec = pl.BlockSpec((span, 2, rows, width), lambda i, ranks: (i, 0, 0, 0))
    send_spec = pl.BlockSpec((2, rows, width), lambda i, ranks: (0, 0, 0))
    out = call(
        body,
        (7.0 if len(lefts) > 1 else 3.0) * len(groups),
        (features // block,),
        [pl.BlockSpec((left.shape[0], block), lambda i, ranks: (0, i)) for left in lefts]
        + [pl.BlockSpec(right.shape, lambda i, ranks: (0, 0)) for right in rights],
        [((z_count, 2, rows, width), BF16)] * len(groups)
        + [((2, rows, width), BF16)] * (len(groups) * z_count),
        [keep_spec] * len(groups) + [send_spec] * (len(groups) * z_count),
        (ranks, *lefts, *rights),
    )
    sends = out[len(groups) :]
    return [
        (out[number], sends[number * z_count : (number + 1) * z_count])
        for number in range(len(groups))
    ]


def mlp_slot(wg, wu, wd, bg, bu, own, other, dy_own, dy_other):
    features, hidden = wg.shape
    half = own.shape[0]
    block = features // 4 if (features // 4) % 128 == 0 else features

    def body(
        wg_ref, wu_ref, wd_ref, bg_ref, bu_ref, own_ref, other_ref, dyo_ref, dyr_ref,
        hid_ref, dg_ref, du_ref, db_own, db_other, out_own, out_other, b_all, dy_all,
    ):
        b_all[:half], b_all[half:] = own_ref[...], other_ref[...]
        dy_all[:half], dy_all[half:] = dyo_ref[...], dyr_ref[...]
        gate = mm(b_all[...], wg_ref[...]) + bg_ref[...]
        up = mm(b_all[...], wu_ref[...]) + bu_ref[...]
        grad_inner = mm(dy_all[...], wd_ref[...])
        bend = jnp.tanh(GELU_A * (gate + GELU_B * gate * gate * gate))
        gelu = 0.5 * gate * (1.0 + bend)
        slope = 0.5 * (1.0 + bend) + 0.5 * gate * (1.0 - bend * bend) * (
            GELU_A * (1.0 + 3.0 * GELU_B * gate * gate)
        )
        hid_ref[...] = (gelu * up).astype(BF16)
        dg_ref[...] = (grad_inner * up * slope).astype(BF16)
        du_ref[...] = (grad_inner * gelu).astype(BF16)
        for step in range(features // block):
            at = pl.ds(step * block, block)
            part = mm_nt(dg_ref[...], wg_ref[at, :]) + mm_nt(du_ref[...], wu_ref[at, :])
            db_own[:, at], db_other[:, at] = part[:half].astype(BF16), part[half:].astype(BF16)
            part = mm_nt(hid_ref[...], wd_ref[at, :])
            out_own[:, at], out_other[:, at] = part[:half].astype(BF16), part[half:].astype(BF16)

    weights = [pltpu.with_memory_space_constraint(w, pltpu.VMEM) for w in (wg, wu, wd)]
    return in_vmem(
        body,
        10.0,
        [((2 * half, hidden), BF16)] * 3 + [((half, features), BF16)] * 4,
        *(*weights, bg[None], bu[None], own, other, dy_own, dy_other),
        scratch=[pltpu.VMEM((2 * half, features), BF16)] * 2,
    )


def split_columns(grid, shard):
    rows, width = shard.shape
    return shard.reshape(rows, grid.z_count, width // grid.z_count).transpose(1, 0, 2)


def own_rows(ranks, keep, got):
    z_count, _, rows, width = keep.shape

    def body(ranks_ref, keep_ref, *refs):
        away_ref, stay_ref = refs[-2:]
        y = ranks_ref[1]
        for z in range(z_count):

            @pl.when(pl.program_id(0) == z)
            def _(got_ref=refs[z]):
                for at, target in ((1 - y, away_ref), (y, stay_ref)):
                    part = keep_ref[0, at].astype(F32) + got_ref[at].astype(F32)
                    target[0] = part.astype(BF16)

    block = pl.BlockSpec((1, 2, rows, width), lambda i, ranks: (i, 0, 0, 0))
    whole = pl.BlockSpec((2, rows, width), lambda i, ranks: (0, 0, 0))
    half = pl.BlockSpec((1, rows, width), lambda i, ranks: (i, 0, 0))
    shape = ((z_count, rows, width), BF16)
    specs = [block] + [whole] * z_count
    return call(body, 2.0, (z_count,), specs, [shape] * 2, [half] * 2, (ranks, keep, *got))


def plus(left, right):
    z_count, rows, width = left.shape

    def body(ranks_ref, left_ref, right_ref, out_ref):
        out_ref[...] = (left_ref[...].astype(F32) + right_ref[...].astype(F32)).astype(BF16)

    block = pl.BlockSpec((1, rows, width), lambda i, ranks: (i, 0, 0))
    operands = (jnp.zeros((1,), jnp.int32), left, right)
    return call(body, 2.0, (z_count,), [block] * 2, [(left.shape, BF16)], [block], operands)[0]


def ring_sum(grid, parts, held, step):
    _, rows, width = parts.shape
    dtype = BF16 if step < grid.z_count else F32
    given = [] if held is None else [held]

    def body(ranks_ref, part_ref, *refs):
        part = part_ref[0].astype(F32)
        refs[-1][...] = (part + refs[0][...].astype(F32) if given else part).astype(dtype)

    full = pl.BlockSpec((rows, width), lambda i, ranks: (0, 0))
    spot = grid.behind(step).astype(jnp.int32)[None]
    return call(
        body,
        1.0,
        (1,),
        [pl.BlockSpec((1, rows, width), lambda i, ranks: (ranks[0], 0, 0))] + [full] * len(given),
        [((rows, width), dtype)],
        [full],
        (spot, parts, *given),
    )[0]


def add(*values):
    def body(*refs):
        total = refs[0][...].astype(F32)
        for ref in refs[1:-1]:
            total += ref[...].astype(F32)
        refs[-1][...] = total.astype(BF16)

    values = [value for value in values if value is not None]
    return in_vmem(body, 1.0, [(values[0].shape, BF16)], *values)[0]


def collect_columns(parts, turn=False):
    count, rows, width = parts.shape

    def body(parts_ref, out_ref):
        if turn:
            for step in range(count):
                out_ref[step * width : (step + 1) * width, :] = parts_ref[step].astype(F32).T
        else:
            pieces = [parts_ref[step].astype(F32) for step in range(count)]
            out_ref[...] = jnp.concatenate(pieces, axis=1)

    shape = (count * width, rows) if turn else (rows, count * width)
    return in_vmem(body, 3.0, [(shape, F32)], parts)[0]


def turned(value, cosine, sine):
    first = value[:, : cosine.shape[1]]
    first = first * cosine + pltpu.roll(first, first.shape[1] // 2, 1) * sine
    return jnp.concatenate([first, value[:, cosine.shape[1] :]], axis=1)


def softmax(query, key, bias):
    scores = mm_nt(query, key) + bias
    expon = jnp.exp(scores - jnp.max(scores, axis=-1, keepdims=True))
    return expon / jnp.sum(expon, axis=-1, keepdims=True)


def attend(scale, q_ref, k_ref, v_ref, cos_ref, sin_ref, bias_ref, rq_ref, o_ref):
    size = k_ref.shape[1]
    for head in range(rq_ref.shape[1] // size):
        at = pl.ds(head * size, size)
        query = (turned(q_ref[:, at], cos_ref[...], sin_ref[...]) * scale).astype(BF16)
        rq_ref[:, at] = query
        probs = softmax(query, k_ref[...], bias_ref[...]).astype(BF16)
        o_ref[:, at] = mm(probs, v_ref[...]).astype(BF16)


def attend_back(
    scale, do_ref, rq_ref, k_ref, v_ref, cos_ref, sin_ref, bias_ref, dq_ref, dk_ref, dv_ref
):
    size = k_ref.shape[1]
    cosine, sine = cos_ref[...], -sin_ref[...]
    grad_key = jnp.zeros(dk_ref.shape, F32)
    grad_value = jnp.zeros(dv_ref.shape, F32)
    for head in range(rq_ref.shape[1] // size):
        at = pl.ds(head * size, size)
        query, grad_out = rq_ref[:, at], do_ref[:, at]
        probs = softmax(query, k_ref[...], bias_ref[...])
        grad_value += mm_tn(probs.astype(BF16), grad_out)
        grad_probs = mm_nt(grad_out, v_ref[...])
        delta = jnp.sum(probs * grad_probs, axis=-1, keepdims=True)
        grad_scores = (probs * (grad_probs - delta)).astype(BF16)
        grad_query = mm(grad_scores, k_ref[...]) * scale
        dq_ref[:, at] = turned(grad_query, cosine, sine).astype(BF16)
        grad_key += mm_tn(grad_scores, query)
    dk_ref[...] = turned(grad_key, cosine, sine)
    dv_ref[...] = grad_value


def in_vmem(body, micros, shapes, *operands, scratch=()):
    spec = pl.BlockSpec(memory_space=pltpu.VMEM)
    return pl.pallas_call(
        body,
        out_shape=[jax.ShapeDtypeStruct(shape, dtype) for shape, dtype in shapes],
        in_specs=[spec] * len(operands),
        out_specs=[spec] * len(shapes),
        scratch_shapes=list(scratch),
        cost_estimate=cost(micros),
        compiler_params=pltpu.CompilerParams(vmem_limit_bytes=VMEM),
    )(*operands)


def shards(
    inputs,
    gain_attn,
    w_query,
    w_keyval,
    w_output,
    gain_mlp,
    w_gate,
    b_gate,
    w_up,
    b_up,
    w_down,
    b_down,
    segment_ids,
    cotangent,
    total,
):
    grid = Grid(total)
    count = grid.z_count
    micro, length, width = inputs.shape
    tokens = micro * length
    head_dim = w_keyval.shape[1] // 2
    query_width = w_query.shape[1]
    scale = head_dim ** (-0.5)

    def halves(value):
        value = value.reshape(micro, 2, length // 2, value.shape[-1])
        return tuple(take(value, i, 1).reshape(tokens // 2, -1) for i in (grid.x, 1 - grid.x))

    def join(mine, other):
        shape = (micro, length // 2, mine.shape[-1])
        return pair(grid.x, mine.reshape(shape), other.reshape(shape), 1).reshape(tokens, -1)

    ranks = jnp.stack([grid.z, grid.y, grid.c, grid.x]).astype(jnp.int32)
    keyval_half = lax.dynamic_slice_in_dim(w_keyval, grid.x * head_dim, head_dim, 1)
    shards_of = [split_columns(grid, shard) for shard in (w_gate, w_up, w_down.T)]
    dy_half = halves(cotangent.reshape(tokens, width))[0]
    segment = segment_ids.reshape(micro, length)
    offsets = jax.vmap(positions)(segment).reshape(tokens)
    quarter = head_dim // 4
    freqs = 10000.0 ** (-jnp.arange(quarter, dtype=F32) / quarter)
    angle = offsets[:, None] * freqs[None, :]
    cosine, sine = jnp.cos(angle), jnp.sin(angle)
    cosine = jnp.concatenate([cosine, cosine], axis=1)
    sine = jnp.concatenate([-sine, sine], axis=1)
    index = jnp.arange(tokens, dtype=jnp.int32)
    seg = segment.reshape(tokens)
    allowed = (
        (seg[:, None] == seg[None, :])
        & (index[:, None] // length == index[None, :] // length)
        & (index[None, :] <= index[:, None])
    )
    bias = jnp.where(allowed, 0.0, -1e30).astype(F32)
    hidden_x = inputs.reshape(tokens, width).astype(F32)
    factor_one = inv_root(hidden_x)
    normed = (hidden_x * factor_one * gain_attn).astype(BF16)
    x_half, factor_half = halves(inputs.reshape(tokens, width))[0], halves(factor_one)[0]
    half_shape = (tokens // 2, width)

    def mlp(step):
        pieces = (b_slots[step], b_others[step], dy_slots[step], dy_others[step])
        results.append(mlp_slot(wg, wu, wd, bg, bu, *grid.gate(pieces)))
        grid.wait(*results[-1])

    slots = [jnp.concatenate([w_query, keyval_half, w_output.T], axis=1)]
    across, beside, both, wholes = [], [], [], []
    dy_slots, dy_others = [dy_half], []

    def place(step):
        pieces = [slots[step], across[step], beside[step], both[step]]
        spot = jnp.stack([grid.behind(step), grid.y, grid.c]).astype(jnp.int32)
        return place_slot(spot, pieces, wholes, count, (0, query_width + head_dim))

    for step in range(count):
        if step + 1 < count:
            slots.append(grid.next_z(slots[step]))
        else:
            gate_mine = grid.along_z(shards_of[0])
        if step > 0:
            grid.wait(across[step - 1])
        across.append(grid.over_y(slots[step]))
        beside.append(grid.over_c(slots[step]))
        if step == 0:
            dy_others.append(grid.over_x(dy_half))
            grid.wait(shards_of[0])
        else:
            both.append(grid.over_c(across[step - 1]))
            wholes = place(step - 1)
            grid.wait(*wholes, beside[step])
        if step == 1:
            grid.wait(shards_of[1], normed, x_half, dy_others[0])
        if step == 2:
            grid.wait(shards_of[2], cosine, sine, bias)
        if step + 1 < count:
            grid.wait(slots[step + 1])
    grid.wait(across[-1])
    grid.wait(gate_mine)

    up_mine = grid.along_z(shards_of[1])
    gate_across, gate_beside = grid.over_y(gate_mine), grid.over_c(gate_mine)
    both.append(grid.over_c(across[-1]))
    wholes = place(count - 1)
    w_qkv, w_out = [whole.reshape(width, -1) for whole in wholes]
    queries = product(normed, w_qkv, F32)
    keyval = queries[:, query_width:]
    front, back = keyval[:, :quarter], keyval[:, quarter : 2 * quarter]
    swapped = jnp.concatenate([back, front], axis=1)
    key = jnp.concatenate(
        [keyval[:, : 2 * quarter] * cosine + swapped * sine, keyval[:, 2 * quarter :]], axis=1
    )
    keyval = jnp.where(grid.x == 0, key, keyval).astype(BF16)
    keyval_other = grid.over_x(keyval)
    grid.wait(keyval_other)
    rot_key = jnp.where(grid.x == 0, keyval, keyval_other)
    values_in = jnp.where(grid.x == 0, keyval_other, keyval)
    shape = (tokens, query_width)
    rot_query, mixed_b = in_vmem(
        partial(attend, scale),
        1.2,
        [(shape, BF16), (shape, BF16)],
        *(queries, rot_key, values_in, cosine, sine, bias),
    )
    mine, other = product_nt(ranks, mixed_b, w_out, micro)
    grid.wait(mine)
    attended = grid.over_x(other)
    grid.wait(up_mine)
    down_mine = grid.along_z(shards_of[2])
    grid.wait(gate_across)
    up_across, up_beside = grid.over_y(up_mine), grid.over_c(up_mine)
    gate_both = grid.over_c(gate_across)
    grid.wait(attended)
    residual, factor_two, normed_two = in_vmem(
        second_norm,
        2.0,
        [(half_shape, F32), ((tokens // 2, 1), F32), (half_shape, BF16)],
        *(x_half, mine, attended, gain_mlp[None]),
    )
    grid.wait(normed_two)
    b_slots, b_others = [normed_two], [grid.over_x(normed_two)]
    b_slots.append(grid.next_z(normed_two))
    dy_slots.append(grid.next_z(dy_half))
    wg = place_all(ranks, [gate_mine, gate_across, gate_beside, gate_both])
    grid.wait(wg, b_others[0])
    grid.wait(down_mine)

    grid.wait(up_across)
    down_across, down_beside = grid.over_y(down_mine), grid.over_c(down_mine)
    grid.wait(b_slots[1], dy_slots[1])
    for step in range(1, count - 1):
        b_slots.append(grid.next_z(b_slots[step]))
        dy_slots.append(grid.next_z(dy_slots[step]))
        b_others.append(grid.over_x(b_slots[step]))
        dy_others.append(grid.over_x(dy_slots[step]))
        if step == 1:
            up_both = grid.over_c(up_across)
            wu = place_all(ranks, [up_mine, up_across, up_beside, up_both])
            grid.wait(wu)
        if step == 2:
            grid.wait(down_across)
            down_both = grid.over_c(down_across)
            wd = place_all(ranks, [down_mine, down_across, down_beside, down_both])
            hidden = wg.shape[1]
            spot = grid.z * hidden
            bg = lax.dynamic_slice_in_dim(b_gate, spot, hidden, 0)
            bu = lax.dynamic_slice_in_dim(b_up, spot, hidden, 0)
            grid.wait(wd, bg, bu)
            results = []
            mlp(0)
        grid.wait(b_slots[step + 1], dy_slots[step + 1])
        grid.wait(b_others[step], dy_others[step])
    b_others.append(grid.over_x(b_slots[-1]))
    dy_others.append(grid.over_x(dy_slots[-1]))
    mlp(1)

    db_got = [None, grid.over_x(results[1][4])]
    db_next = None
    for step in range(2, count):
        mlp(step)
        if step == 2:
            grid.wait(b_others[-1], dy_others[-1])
        grid.wait(db_got[step - 1], *([] if db_next is None else [db_next]))
        db_held = add(results[step - 1][3], db_got[step - 1], db_next)
        grid.wait(db_held)
        db_next = grid.next_z(db_held)
        db_got.append(grid.over_x(results[step][4]))
    inner_slots, gate_slots, up_slots, db_own, db_other, out_own, out_other = zip(*results)
    dy_all = [piece for two in zip(dy_slots, dy_others) for piece in two]
    b_all = [piece for two in zip(b_slots, b_others) for piece in two]
    down_keep, down_send = product_rows(ranks, grid.gate(dy_all), [inner_slots], count)[0]
    grid.wait(down_keep)
    down_got = [grid.over_c(send) for send in down_send]
    grid.wait(db_next, db_got[-1])
    db_held = add(db_own[-1], db_got[-1], db_next)
    grid.wait(db_held)
    db_next = grid.next_z(db_held)
    db_got[0] = grid.over_x(db_other[0])
    grid.wait(*down_got)
    down_away, down_stay = own_rows(ranks, down_keep, down_got)
    grid.wait(down_away)
    down_back = grid.over_y(down_away)
    out_got = [None] * count
    grid.wait(db_got[0], db_next)
    grad_resid, grad_resid_b, gain_mlp_term = in_vmem(
        second_norm_back,
        3.0,
        [(half_shape, F32), (half_shape, BF16), ((1, width), F32)],
        *(db_own[0], db_got[0], db_next, residual, factor_two, gain_mlp[None], dy_half),
    )
    grid.wait(grad_resid_b)
    grad_resid_other = grid.over_x(grad_resid_b)
    out_got[1] = grid.over_x(out_other[1])
    (gate_keep, gate_send), (up_keep, up_send) = product_rows(
        ranks, grid.gate(b_all), [gate_slots, up_slots], count
    )
    grid.wait(gate_keep)
    gate_got = [grid.over_c(send) for send in gate_send]
    up_got = [grid.over_c(send) for send in up_send]
    grid.wait(*gate_got, grad_resid_other)
    gate_away, gate_stay = own_rows(ranks, gate_keep, gate_got)
    grid.wait(gate_away)
    grid.wait(down_back)
    gate_back = grid.over_y(gate_away)

    grad_resid_b = join(grad_resid_b, grad_resid_other)
    grad_mixed = product(grid.gate(grad_resid_b), w_out, BF16)
    shape_kv = (tokens, head_dim)
    grad_query, grad_key, grad_values = in_vmem(
        partial(attend_back, scale),
        2.3,
        [(shape, BF16), (shape_kv, F32), (shape_kv, F32)],
        *(grad_mixed, rot_query, rot_key, values_in, cosine, sine, bias),
    )
    grid.wait(grad_query)
    grad_own = jnp.where(grid.x == 0, grad_key, grad_values)
    grad_other = grid.over_x(jnp.where(grid.x == 0, grad_values, grad_key))
    down_rows = plus(down_stay, down_back)
    grid.wait(down_rows)
    down_parts = grid.along_z(down_rows)
    grid.wait(grad_other, out_got[1])
    branch = add(out_own[1], out_got[1])
    grad_keyval = (grad_own + grad_other).astype(BF16)
    grad_qkv = jnp.concatenate([grad_query, grad_keyval], axis=1)
    mine, other = product_nt(ranks, grid.gate(grad_qkv), w_qkv, micro)
    grid.wait(mine, branch)
    grad_normed = grid.over_x(other)
    branch = grid.next_z(branch)
    out_keep, out_send = product_rows(ranks, [grid.gate(grad_resid_b)], [[mixed_b]], count)[0]
    grid.wait(out_keep)
    out_got_c = [grid.over_c(send) for send in out_send]
    grid.wait(*up_got)
    up_away, up_stay = own_rows(ranks, up_keep, up_got)
    grid.wait(up_away)
    grid.wait(gate_back, grad_normed)
    up_back = grid.over_y(up_away)
    out_got[2] = grid.over_x(out_other[2])
    gate_rows = plus(gate_stay, gate_back)
    grid.wait(gate_rows)
    grid.wait(down_parts, branch)
    gate_parts = grid.along_z(gate_rows)
    grad_input, gain_attn_term = in_vmem(
        first_norm_back,
        3.0,
        [(half_shape, BF16), ((1, width), F32)],
        *(mine, grad_normed, x_half, factor_half, gain_attn[None], grad_resid),
    )
    grid.wait(grad_input, *out_got_c)
    out_away, out_stay = own_rows(ranks, out_keep, out_got_c)
    middle = (query_width + head_dim) // 2
    cuts = (grad_qkv[:, :middle], grad_qkv[:, middle:])
    products = [product_rows(ranks, [grid.gate(normed)], [[cut]], count)[0] for cut in cuts]
    qkv_keep, qkv_send = zip(*products)
    grid.wait(out_away, *qkv_keep)
    qkv_got = [[grid.over_c(send) for send in sends] for sends in qkv_send]
    grid.wait(up_back, out_got[2])
    out_back = grid.over_y(out_away)
    out_got[3] = grid.over_x(out_other[3])
    branch = add(out_own[2], out_got[2], branch)
    grid.wait(branch)
    branch = grid.next_z(branch)
    up_rows = plus(up_stay, up_back)
    grid.wait(up_rows)
    narrow = jnp.concatenate(
        [gain_attn_term, gain_mlp_term, jnp.sum(dy_half.astype(F32), axis=0)[None]]
    )
    grid.wait(*qkv_got[0], *qkv_got[1])
    qkv_away, qkv_stay = zip(
        *[own_rows(ranks, keep, got) for keep, got in zip(qkv_keep, qkv_got)]
    )
    grid.wait(*qkv_away)
    grid.wait(gate_parts, branch, out_got[3])
    up_parts = grid.along_z(up_rows)
    branch = add(out_own[3], out_got[3], branch)
    grid.wait(branch)
    branch = grid.next_z(branch)
    for step in range(4, count):
        out_got[step] = grid.over_x(out_other[step])
        branch = grid.next_z(add(out_own[step], out_got[step], branch))
    out_got[0] = grid.over_x(out_other[0])
    down_grad = collect_columns(down_parts, True)
    gate_grad = collect_columns(gate_parts)
    grid.wait(down_grad, gate_grad)
    grid.wait(out_back, out_got[0])
    qkv_back = [grid.over_y(qkv_away[0])]
    narrow_other = grid.over_x(narrow)
    out_rows = plus(out_stay, out_back)
    out_held = ring_sum(grid, out_rows, None, 1)
    grid.wait(out_held)
    out_held = grid.next_z(out_held)
    grid.wait(branch, narrow_other)
    outputs = (residual + add(out_own[0], out_got[0], branch).astype(F32) + b_down).astype(BF16)
    grid.wait(outputs)
    outputs_other = grid.over_x(outputs)
    grid.wait(out_held)
    out_held = ring_sum(grid, out_rows, out_held, 2)
    grid.wait(out_held)
    out_held = grid.next_z(out_held)

    ffn = b_gate.shape[0]
    wide = jnp.zeros((2, ffn), F32)
    sums = [
        sum(jnp.sum(slot.astype(F32), axis=0) for slot in slots)
        for slots in (gate_slots, up_slots)
    ]
    wide = lax.dynamic_update_slice(wide, jnp.stack(sums), (0, spot)).reshape(-1)
    small = jnp.concatenate([(narrow + narrow_other).reshape(-1), wide])
    small_other = grid.over_c(small)
    grid.wait(small_other, outputs_other)
    small = small + small_other
    grad_input_other = grid.over_x(grad_input)
    grid.wait(qkv_back[0])
    qkv_back.append(grid.over_y(qkv_away[1]))
    small_other = grid.over_y(small)
    qkv_rows = [plus(qkv_stay[0], qkv_back[0])]
    qkv_held = ring_sum(grid, qkv_rows[0], None, 1)
    grid.wait(qkv_held)
    qkv_held = [grid.next_z(qkv_held), None]
    for step in range(3, count):
        grid.wait(out_held)
        out_held = ring_sum(grid, out_rows, out_held, step)
        grid.wait(out_held)
        out_held = grid.next_z(out_held)
    grid.wait(qkv_held[0], small_other)
    small = small + small_other
    qkv_held[0] = ring_sum(grid, qkv_rows[0], qkv_held[0], 2)
    grid.wait(qkv_held[0])
    qkv_held[0] = grid.next_z(qkv_held[0])
    grid.wait(up_parts, out_held)
    up_grad = collect_columns(up_parts)
    out_grad = ring_sum(grid, out_rows, out_held, count).T
    grid.wait(up_grad, out_grad)
    grid.wait(qkv_back[1])
    qkv_rows.append(plus(qkv_stay[1], qkv_back[1]))
    qkv_held[1] = ring_sum(grid, qkv_rows[1], None, 1)
    grid.wait(qkv_held[1])
    qkv_held[1] = grid.next_z(qkv_held[1])
    for step in range(3, count + 1):
        if step - 3 < len(grid.flips):
            small_other = lax.ppermute(grid.gate(small), "dp", grid.flips[step - 3])
        grid.wait(*qkv_held)
        qkv_held[1] = grid.next_z(ring_sum(grid, qkv_rows[1], qkv_held[1], step - 1))
        if step < count:
            qkv_held[0] = grid.next_z(ring_sum(grid, qkv_rows[0], qkv_held[0], step))
        if step - 3 < len(grid.flips):
            grid.wait(small_other)
            small = small + small_other
    grid.wait(grad_input_other)
    qkv_held = [ring_sum(grid, rows, held, count) for rows, held in zip(qkv_rows, qkv_held)]
    qkv_held = jnp.concatenate(qkv_held, axis=1)
    query_grad = qkv_held[:, :query_width]
    keyval_grad = qkv_held[:, query_width:]
    keyval_grad = pair(grid.x, keyval_grad, grid.over_x(keyval_grad), 1)
    keyval_grad = keyval_grad.reshape(keyval_grad.shape[0], 2 * head_dim)
    return (
        join(outputs, outputs_other).reshape(inputs.shape),
        join(grad_input, grad_input_other).reshape(inputs.shape),
        small[:width],
        query_grad,
        keyval_grad,
        out_grad,
        small[width : 2 * width],
        gate_grad,
        small[3 * width : 3 * width + ffn],
        up_grad,
        small[3 * width + ffn :],
        down_grad,
        small[2 * width : 3 * width],
    )


def solution(mesh):
    in_specs = (
        P(None, "dp", None),
        P(),
        P("dp", "mp"),
        P("dp", None),
        P("mp", "dp"),
        P(),
        P("dp", "mp"),
        P("mp"),
        P("dp", "mp"),
        P("mp"),
        P("mp", "dp"),
        P(),
        P(None, "dp", None),
        P(None, "dp", None),
    )
    out_specs = (
        P(None, "dp", None),
        P(None, "dp", None),
        P(),
        P("dp", "mp"),
        P("dp", None),
        P("mp", "dp"),
        P(),
        P("dp", "mp"),
        P("mp"),
        P("dp", "mp"),
        P("mp"),
        P("mp", "dp"),
        P(),
    )
    body = partial(shards, total=mesh.shape["dp"])
    return jax.shard_map(body, mesh=mesh, in_specs=in_specs, out_specs=out_specs, check_vma=False)
```

time: 743 us -> 651 us (0.88)
  waiting for transfers between devices: 307 us -> 240 us
  other arithmetic: 79.6 us -> 13.3 us
  Pallas kernels: 145 us -> 168 us
  starting transfers between devices: 91.8 us -> 113 us
  matrix products: 20.1 us -> 0 us
  local copies, waits for them, and re-layouts: 85.5 us -> 103 us
    pallas_call x2 -> x19, Pallas kernels: 3.38 us -> 58.4 us  [in_vmem(): pl.pallas_call(body, out_shape=[jax.ShapeDtypeStruct(shape, dtype) for sh...]
    convert_element_type x30 -> x2, other arithmetic: 51.4 us -> 1.08 us  [the longest x1 0.96 us: shards(): grad_keyval = (grad_own + grad_other).astype(BF16)]
    ppermute x86 -> x104, waiting for transfers between devices: 253 us -> 203 us  [the longest x24 134 us: next_z(): return lax.ppermute(self.gate(value), 'dp', self.ring(step))]
    unnamed x240 -> x291, local copies, waits for them, and re-layouts: 28.7 us -> 73.7 us
    pallas_call x17 -> x40, Pallas kernels: 142 us -> 110 us  [call(): pl.pallas_call(body, out_shape=[jax.ShapeDtypeStruct(shape, dtype) for sh...]
    dot_general x5 -> x0, matrix products: 20.1 us -> none  [the longest x2 11.6 us: mm_nt(): lax.dot_general(left, right, (((1,), (1,)), ((), ())), preferred_element_...]
    ppermute x86 -> x104, starting transfers between devices: 65.5 us -> 85.5 us  [the longest x24 32.8 us: next_z(): return lax.ppermute(self.gate(value), 'dp', self.ring(step))]
    all_to_all x6, waiting for transfers between devices: 54.3 us -> 37.1 us  [along_z(): lax.all_to_all(value, 'dp', 0, 0, axis_index_groups=self.lines, tiled=True)]
  transfers between devices with their start and end apart: 92 -> 110, of which waited for: 37 -> 41; matrix products, arithmetic and copies ran while one was open for 20% -> 7% of each run, Pallas kernels for 20% -> 25%
where the time goes in v3:
time: 651 us; the launch traced here: 641 us
  waiting for transfers between devices  240 us (37%)
  Pallas kernels  168 us (26%)
  starting transfers between devices  113 us (17%)
  local copies, waits for them, and re-layouts  103 us (16%)
  other arithmetic  13.3 us (2%)
    ppermute x24, waiting for transfers between devices, next_z(): return lax.ppermute(self.gate(value), 'dp', self.ring(step))  134 us
    pallas_call x40, Pallas kernels, call(): pl.pallas_call(body, out_shape=[jax.ShapeDtypeStruct(shape, dtype) for sh...  110 us
    unnamed x291, local copies, waits for them, and re-layouts  73.7 us
    pallas_call x19, Pallas kernels, in_vmem(): pl.pallas_call(body, out_shape=[jax.ShapeDtypeStruct(shape, dtype) for sh...  58.4 us
    ppermute x25, waiting for transfers between devices, over_x(): return lax.ppermute(self.gate(value), 'mp', [(0, 1), (1, 0)])  42.7 us
    all_to_all x6, waiting for transfers between devices, along_z(): lax.all_to_all(value, 'dp', 0, 0, axis_index_groups=self.lines, tiled=True)  37.1 us
    ppermute x24, starting transfers between devices, next_z(): return lax.ppermute(self.gate(value), 'dp', self.ring(step))  32.8 us
    ppermute x25, starting transfers between devices, over_x(): return lax.ppermute(self.gate(value), 'mp', [(0, 1), (1, 0)])  30.2 us
  transfers between devices with their start and end apart: 110, of which 41 were waited for; matrix products, arithmetic and copies ran while one was open for 7% of the time, Pallas kernels for 25%

profile of v3, /device:TPU:0, one launch (start us, length us, event | category | flops | bytes accessed | tf_op | source)
XLA Modules:
  0.0 640.8 jit_solution(3612952906088201868)
XLA Ops:
  2.8 3.1 collective-permute-start
  9.0 4.4 reshape.287
  13.4 2.8 copy.61
  16.3 11.6 %collective-permute-done.refs_0_ = bf16[160,2816]{1,0:T(8,128)(2,1)S(1)} collective-permute-done((bf16[160,2816]{1,0:T(8,128)(2,1)S(1)}, bf16[160,2816]{1,0:T(8,128)(2,1)S(1)}, u32[]{:S(2)}, u32[]{:S(2)}) %collective-permute-start) | collective-permute-done | bytes 901152 | tf_op jit(solution)/shard_map/ppermute | solution.py:89
  33.2 4.4 reshape.288
  40.5 4.4 reshape.290
  44.9 2.9 copy.59
  48.5 4.3 shard_map.237
  57.0 4.0 shard_map.238
  62.0 16.4 %collective-permute-done.7.refs_0_ = bf16[160,2816]{1,0:T(8,128)(2,1)} collective-permute-done((bf16[160,2816]{1,0:T(8,128)(2,1)}, bf16[160,2816]{1,0:T(8,128)(2,1)}, u32[]{:S(2)}, u32[]{:S(2)}) %collective-permute-start.7) | collective-permute-done | bytes 901152 | tf_op jit(solution)/shard_map/ppermute | solution.py:89
  78.3 3.5 all-to-all-start
  84.7 4.3 shard_map.239
  89.1 15.7 %collective-permute-done.12.refs_1_ = bf16[160,2816]{1,0:T(8,128)(2,1)} collective-permute-done((bf16[160,2816]{1,0:T(8,128)(2,1)}, bf16[160,2816]{1,0:T(8,128)(2,1)}, u32[]{:S(2)}, u32[]{:S(2)}) %collective-permute-start.12) | collective-permute-done | bytes 901152 | tf_op jit(solution)/shard_map/ppermute | solution.py:80
  104.8 8.1 %all-to-all-done.own = bf16[4,160,960]{2,1,0:T(8,128)(2,1)S(1)} async-done(((bf16[4,160,960]{2,1,0:T(8,128)(2,1)}), bf16[4,160,960]{2,1,0:T(8,128)(2,1)S(1)}, u32[]{:S(2)}, u32[]{:S(2)}) %all-to-all-start) | async-done | bytes 1228832 | tf_op jit(solution)/shard_map/all_to_all | solution.py:93
  112.8 3.8 all-to-all-start.1
  117.2 4.5 shard_map.240
  121.8 3.2 copy-done.2
  125.0 3.2 shard_map.241.q_ref
  130.1 3.4 collective-permute-done.16
  135.5 3.6 shard_map.243
  140.9 8.0 %all-to-all-done.1.own = bf16[4,160,960]{2,1,0:T(8,128)(2,1)S(1)} async-done(((bf16[4,160,960]{2,1,0:T(8,128)(2,1)}), bf16[4,160,960]{2,1,0:T(8,128)(2,1)S(1)}, u32[]{:S(2)}, u32[]{:S(2)}) %all-to-all-start.1) | async-done | bytes 1228832 | tf_op jit(solution)/shard_map/all_to_all | solution.py:93
  148.9 4.3 all-to-all-start.2
  155.8 11.6 %collective-permute-done.17.got_ref = bf16[96,2560]{1,0:T(8,128)(2,1)S(1)} collective-permute-done((bf16[96,2560]{1,0:T(8,128)(2,1)}, bf16[96,2560]{1,0:T(8,128)(2,1)S(1)}, u32[]{:S(2)}, u32[]{:S(2)}) %collective-permute-start.17) | collective-permute-done | bytes 491552 | tf_op jit(solution)/shard_map/ppermute | solution.py:86
  176.5 2.8 shard_map.245
  184.9 20.9 %all-to-all-done.2.own = bf16[4,160,960]{2,1,0:T(8,128)(2,1)} async-done(((bf16[4,160,960]{2,1,0:T(8,128)(2,1)}), bf16[4,160,960]{2,1,0:T(8,128)(2,1)}, u32[]{:S(2)}, u32[]{:S(2)}) %all-to-all-start.2) | async-done | bytes 1228832 | tf_op jit(solution)/shard_map/all_to_all | solution.py:93
  209.0 13.7 %collective-permute-done.30.dyo_ref.refs_4_ = bf16[96,2560]{1,0:T(8,128)(2,1)} collective-permute-done((bf16[96,2560]{1,0:T(8,128)(2,1)}, bf16[96,2560]{1,0:T(8,128)(2,1)}, u32[]{:S(2)}, u32[]{:S(2)}) %collective-permute-start.30) | collective-permute-done | bytes 491552 | tf_op jit(solution)/shard_map/ppermute | solution.py:89
  224.1 3.1 shard_map.246
  229.6 2.8 collective-permute-done.29.own_ref.refs_4_
  246.9 3.1 shard_map.247
  252.1 9.6 %shard_map.248 = (bf16[192,960]{1,0:T(8,128)(2,1)S(1)}, bf16[192,960]{1,0:T(8,128)(2,1)S(1)}, bf16[192,960]{1,0:T(8,128)(2,1)S(1)}, bf16[96,2560]{1,0:T(8,128)(2...) custom-call(bf16[2560,960]{1,0:T(8,128)(2,1)S(1)} %bitcast.71, ...), custom_call_target="tpu_custom_call" | custom-call | flops 2875000064 | bytes 9225000 | tf_op jit(solution)/shard_map/pallas_call | solution.py:484
  263.6 10.9 %shard_map.249 = (bf16[192,960]{1,0:T(8,128)(2,1)S(1)}, bf16[192,960]{1,0:T(8,128)(2,1)S(1)}, bf16[192,960]{1,0:T(8,128)(2,1)S(1)}, bf16[96,2560]{1,0:T(8,128)(2...) custom-call(bf16[2560,960]{1,0:T(8,128)(2,1)S(1)} %bitcast.72, ...), custom_call_target="tpu_custom_call" | custom-call | flops 2875000064 | bytes 9225000 | tf_op jit(solution)/shard_map/pallas_call | solution.py:484
  278.8 9.9 %shard_map.250 = (bf16[192,960]{1,0:T(8,128)(2,1)S(1)}, bf16[192,960]{1,0:T(8,128)(2,1)S(1)}, bf16[192,960]{1,0:T(8,128)(2,1)S(1)}, bf16[96,2560]{1,0:T(8,128)(2...) custom-call(bf16[2560,960]{1,0:T(8,128)(2,1)S(1)} %bitcast.73, ...), custom_call_target="tpu_custom_call" | custom-call | flops 2875000064 | bytes 9225000 | tf_op jit(solution)/shard_map/pallas_call | solution.py:484
  289.6 10.5 %collective-permute-done.38.other_ref.refs_7_ = bf16[96,2560]{1,0:T(8,128)(2,1)S(1)} collective-permute-done((bf16[96,2560]{1,0:T(8,128)(2,1)}, bf16[96,2560]{1,0:T(8,128)(2,1)S(1)}, u32[]{:S(2)}, u32[]{:S(2)}) %collective-permute-start.38) | collective-permute-done | bytes 491552 | tf_op jit(solution)/shard_map/ppermute | solution.py:86
  300.1 9.3 %collective-permute-done.40.refs_1_ = bf16[96,2560]{1,0:T(8,128)(2,1)S(1)} collective-permute-done((bf16[96,2560]{1,0:T(8,128)(2,1)S(1)}, bf16[96,2560]{1,0:T(8,128)(2,1)S(1)}, u32[]{:S(2)}, u32[]{:S(2)}) %collective-permute-start.40) | collective-permute-done | bytes 491552 | tf_op jit(solution)/shard_map/ppermute | solution.py:86
  311.3 10.5 %shard_map.252 = (bf16[192,960]{1,0:T(8,128)(2,1)S(1)}, bf16[192,960]{1,0:T(8,128)(2,1)S(1)}, bf16[192,960]{1,0:T(8,128)(2,1)S(1)}, bf16[96,2560]{1,0:T(8,128)(2...) custom-call(bf16[2560,960]{1,0:T(8,128)(2,1)S(1)} %bitcast.74, ...), custom_call_target="tpu_custom_call" | custom-call | flops 2875000064 | bytes 9225000 | tf_op jit(solution)/shard_map/pallas_call | solution.py:484
  325.2 7.5 %shard_map.254 = (bf16[4,2,160,960]{3,2,1,0:T(8,128)(2,1)S(1)}, bf16[2,160,960]{2,1,0:T(8,128)(2,1)S(1)}, bf16[2,160,960]{2,1,0:T(8,128)(2,1)S(1)}, bf16[2,160,9...) custom-call(s32[4]{0:T(128)S(1)} %pad_add_fusion.ranks_ref, bf16[96,2560]{1,0:T(8,128)(2,1)S(1)} %bitcast.88, ...), custom_call_target="tpu_custom_call" | custom-call | flops 2012499968 | bytes 6457500 | tf_op jit(solution)/shard_map/pallas_call | solution.py:116
  334.8 13.4 %collective-permute-done.43.refs_2_ = bf16[96,2560]{1,0:T(8,128)(2,1)S(1)} collective-permute-done((bf16[96,2560]{1,0:T(8,128)(2,1)S(1)}, bf16[96,2560]{1,0:T(8,128)(2,1)S(1)}, u32[]{:S(2)}, u32[]{:S(2)}) %collective-permute-start.43) | collective-permute-done | bytes 491552 | tf_op jit(solution)/shard_map/ppermute | solution.py:89
  351.2 12.1 %collective-permute-done.50.held_ref = bf16[96,2560]{1,0:T(8,128)(2,1)S(1)} collective-permute-done((bf16[96,2560]{1,0:T(8,128)(2,1)S(1)}, bf16[96,2560]{1,0:T(8,128)(2,1)S(1)}, u32[]{:S(2)}, u32[]{:S(2)}) %collective-permute-start.50) | collective-permute-done | bytes 491552 | tf_op jit(solution)/shard_map/ppermute | solution.py:89
  365.8 14.1 %shard_map.258 = (bf16[4,2,160,960]{3,2,1,0:T(8,128)(2,1)S(1)}, bf16[4,2,160,960]{3,2,1,0:T(8,128)(2,1)S(1)}, bf16[2,160,960]{2,1,0:T(8,128)(2,1)S(1)}, bf16[2,1...) custom-call(s32[4]{0:T(128)S(1)} %pad_add_fusion.ranks_ref, ...), custom_call_target="tpu_custom_call" | custom-call | flops 4024999936 | bytes 12915000 | tf_op jit(solution)/shard_map/pallas_call | solution.py:116
  398.1 3.7 all-to-all-start.3
  405.4 3.2 copy-done.3
  408.6 4.1 shard_map.263
  415.5 5.9 shard_map.265
  431.5 3.8 shard_map.266
  435.3 2.9 collective-permute-done.65.refs_2_
  444.1 7.9 %all-to-all-start.4 = ((bf16[4,160,960]{2,1,0:T(8,128)(2,1)}), bf16[4,160,960]{2,1,0:T(8,128)(2,1)S(1)}, u32[]{:S(2)}, u32[]{:S(2)}) async-start(bf16[4,160,960]{2,1,0:T(8,128)(2,1)} %copy-done.9), calls=%async_computation.4 | async-start | bytes 2621440 | tf_op jit(solution)/shard_map/all_to_all | solution.py:93
  459.5 4.6 shard_map.269
  465.3 3.2 shard_map.271
  469.7 4.1 shard_map.270
  495.3 3.5 shard_map.274
  511.0 4.3 all-to-all-start.5
  527.1 22.6 %collective-permute-done.87.refs_0_ = bf16[160,1280]{1,0:T(8,128)(2,1)} collective-permute-done((bf16[160,1280]{1,0:T(8,128)(2,1)}, bf16[160,1280]{1,0:T(8,128)(2,1)}, u32[]{:S(2)}, u32[]{:S(2)}) %collective-permute-start.87) | collective-permute-done | bytes 409632 | tf_op jit(solution)/shard_map/ppermute | solution.py:89
  553.3 5.8 collective-permute-start.92
  559.1 8.8 %collective-permute-done.92.refs_0_ = bf16[160,1280]{1,0:T(8,128)(2,1)S(1)} collective-permute-done((bf16[160,1280]{1,0:T(8,128)(2,1)S(1)}, bf16[160,1280]{1,0:T(8,128)(2,1)S(1)}, u32[]{:S(2)}, u32[]{:S(2)}) %collective-permute-start.92) | collective-permute-done | bytes 409632 | tf_op jit(solution)/shard_map/ppermute | solution.py:89
  576.4 4.9 copy.50
  583.6 5.5 collective-permute-done.93.refs_0_
  590.1 3.0 shard_map.287
  607.7 3.9 collective-permute-done.98.refs_0_
  611.6 3.7 collective-permute-done.99.refs_0_
  615.5 4.3 collective-permute-done.97
  620.5 4.1 collective-permute-done.101.refs_0_
  625.3 5.8 collective-permute-done.100.refs_0_
  631.2 2.8 collective-permute-done.102.refs_0_
  636.6 2.9 collective-permute-done.103
  (591 shorter events, 218.8 us)
Async XLA Ops:
  2.8 25.1 %collective-permute-start = (bf16[160,2816]{1,0:T(8,128)(2,1)S(1)}, bf16[160,2816]{1,0:T(8,128)(2,1)S(1)}, u32[]{:S(2)}, u32[]{:S(2)}) collective-permute-start(bf16[160,2816]{1,0:T(8,128)(2,1)S(1)} %pad_maximum_fusion.refs_0_), channel_id=1, source_target_pairs={{0,8},{2,10},{4,12},{6,14},{8,16},{10,18},{12,20},{14,22},{16,24},... | collective-permute-start | bytes 2703368 | tf_op jit(solution)/shard_map/ppermute | solution.py:89
  5.9 22.0 %collective-permute-start.2 = (bf16[160,2816]{1,0:T(8,128)(2,1)S(1)}, bf16[160,2816]{1,0:T(8,128)(2,1)}, u32[]{:S(2)}, u32[]{:S(2)}) collective-permute-start(bf16[160,2816]{1,0:T(8,128)(2,1)S(1)} %pad_maximum_fusion.refs_0_), channel_id=1, source_target_pairs={{0,4},{2,6},{4,0},{6,2},{8,12},{10,14},{12,8},{14,10},{16,20},{18,... | collective-permute-start | bytes 2703368 | tf_op jit(solution)/shard_map/ppermute | solution.py:80
  7.4 24.2 %collective-permute-start.3 = (bf16[160,2816]{1,0:T(8,128)(2,1)S(1)}, bf16[160,2816]{1,0:T(8,128)(2,1)}, u32[]{:S(2)}, u32[]{:S(2)}) collective-permute-start(bf16[160,2816]{1,0:T(8,128)(2,1)S(1)} %pad_maximum_fusion.refs_0_), channel_id=1, source_target_pairs={{0,2},{2,0},{4,6},{6,4},{8,10},{10,8},{12,14},{14,12},{16,18},{18,... | collective-permute-start | bytes 2703368 | tf_op jit(solution)/shard_map/ppermute | solution.py:83
  27.9 20.7 %collective-permute-start.4 = (bf16[160,2816]{1,0:T(8,128)(2,1)}, bf16[160,2816]{1,0:T(8,128)(2,1)}, u32[]{:S(2)}, u32[]{:S(2)}) collective-permute-start(bf16[160,2816]{1,0:T(8,128)(2,1)} %collective-permute-done.2.refs_1_), channel_id=1, source_target_pairs={{0,2},{2,0},{4,6},{6,4},{8,10},{10,8},{12,14},{14,12},{16,18},{18,... | collective-permute-start | bytes 2703368 | tf_op jit(solution)/shard_map/ppermute | solution.py:83
  28.0 24.9 %collective-permute-start.5 = (bf16[160,2816]{1,0:T(8,128)(2,1)S(1)}, bf16[160,2816]{1,0:T(8,128)(2,1)}, u32[]{:S(2)}, u32[]{:S(2)}) collective-permute-start(bf16[160,2816]{1,0:T(8,128)(2,1)S(1)} %collective-permute-done.refs_0_), channel_id=1, source_target_pairs={{0,2},{2,0},{4,6},{6,4},{8,10},{10,8},{12,14},{14,12},{16,18},{18,... | collective-permute-start | bytes 2703368 | tf_op jit(solution)/shard_map/ppermute | solution.py:83
  28.6 25.1 %collective-permute-start.8 = (bf16[160,2816]{1,0:T(8,128)(2,1)S(1)}, bf16[160,2816]{1,0:T(8,128)(2,1)}, u32[]{:S(2)}, u32[]{:S(2)}) collective-permute-start(bf16[160,2816]{1,0:T(8,128)(2,1)S(1)} %collective-permute-done.refs_0_), channel_id=1, source_target_pairs={{0,4},{2,6},{4,0},{6,2},{8,12},{10,14},{12,8},{14,10},{16,20},{18,... | collective-permute-start | bytes 2703368 | tf_op jit(solution)/shard_map/ppermute | solution.py:80
  30.1 23.6 %collective-permute-start.1 = (bf16[160,2816]{1,0:T(8,128)(2,1)S(1)}, bf16[160,2816]{1,0:T(8,128)(2,1)}, u32[]{:S(2)}, u32[]{:S(2)}) collective-permute-start(bf16[160,2816]{1,0:T(8,128)(2,1)S(1)} %collective-permute-done.refs_0_), channel_id=1, source_target_pairs={{0,8},{2,10},{4,12},{6,14},{8,16},{10,18},{12,20},{14,22},{16,24},... | collective-permute-start | bytes 2703368 | tf_op jit(solution)/shard_map/ppermute | solution.py:89
  31.5 21.3 %collective-permute-start.6 = (bf16[96,2560]{1,0:T(8,128)(2,1)S(1)}, bf16[96,2560]{1,0:T(8,128)(2,1)S(1)}, u32[]{:S(2)}, u32[]{:S(2)}) collective-permute-start(bf16[96,2560]{1,0:T(8,128)(2,1)S(1)} %bitcast.85), channel_id=1, source_target_pairs={{0,1},{1,0},{2,3},{3,2},{4,5},{5,4},{6,7},{7,6},{8,9},{9,8},{10,11... | collective-permute-start | bytes 1474568 | tf_op jit(solution)/shard_map/ppermute | solution.py:86
  54.2 24.1 %collective-permute-start.7 = (bf16[160,2816]{1,0:T(8,128)(2,1)}, bf16[160,2816]{1,0:T(8,128)(2,1)}, u32[]{:S(2)}, u32[]{:S(2)}) collective-permute-start(bf16[160,2816]{1,0:T(8,128)(2,1)} %collective-permute-done.1.refs_0_), channel_id=1, source_target_pairs={{0,8},{2,10},{4,12},{6,14},{8,16},{10,18},{12,20},{14,22},{16,24},... | collective-permute-start | bytes 2703368 | tf_op jit(solution)/shard_map/ppermute | solution.py:89
  56.5 25.4 %collective-permute-start.11 = (bf16[160,2816]{1,0:T(8,128)(2,1)}, bf16[160,2816]{1,0:T(8,128)(2,1)}, u32[]{:S(2)}, u32[]{:S(2)}) collective-permute-start(bf16[160,2816]{1,0:T(8,128)(2,1)} %collective-permute-done.1.refs_0_), channel_id=1, source_target_pairs={{0,4},{2,6},{4,0},{6,2},{8,12},{10,14},{12,8},{14,10},{16,20},{18,... | collective-permute-start | bytes 2703368 | tf_op jit(solution)/shard_map/ppermute | solution.py:80
  78.3 34.5 %all-to-all-start = ((bf16[4,160,960]{2,1,0:T(8,128)(2,1)}), bf16[4,160,960]{2,1,0:T(8,128)(2,1)S(1)}, u32[]{:S(2)}, u32[]{:S(2)}) async-start(bf16[4,160,960]{2,1,0:T(8,128)(2,1)} %bitcast.105), calls=%async_computation | async-start | bytes 2621440 | tf_op jit(solution)/shard_map/all_to_all | solution.py:93
  82.5 22.3 %collective-permute-start.12 = (bf16[160,2816]{1,0:T(8,128)(2,1)}, bf16[160,2816]{1,0:T(8,128)(2,1)}, u32[]{:S(2)}, u32[]{:S(2)}) collective-permute-start(bf16[160,2816]{1,0:T(8,128)(2,1)} %collective-permute-done.7.refs_0_), channel_id=1, source_target_pairs={{0,4},{2,6},{4,0},{6,2},{8,12},{10,14},{12,8},{14,10},{16,20},{18,... | collective-permute-start | bytes 2703368 | tf_op jit(solution)/shard_map/ppermute | solution.py:80
  112.8 36.0 %all-to-all-start.1 = ((bf16[4,160,960]{2,1,0:T(8,128)(2,1)}), bf16[4,160,960]{2,1,0:T(8,128)(2,1)S(1)}, u32[]{:S(2)}, u32[]{:S(2)}) async-start(bf16[4,160,960]{2,1,0:T(8,128)(2,1)} %bitcast.104), calls=%async_computation.1 | async-start | bytes 2621440 | tf_op jit(solution)/shard_map/all_to_all | solution.py:93
  116.7 36.5 %collective-permute-start.18 = (bf16[4,160,960]{2,1,0:T(8,128)(2,1)S(1)}, bf16[4,160,960]{2,1,0:T(8,128)(2,1)}, u32[]{:S(2)}, u32[]{:S(2)}) collective-permute-start(bf16[4,160,960]{2,1,0:T(8,128)(2,1)S(1)} %all-to-all-done.own), channel_id=1, source_target_pairs={{0,4},{2,6},{4,0},{6,2},{8,12},{10,14},{12,8},{14,10},{16,20},{18,... | collective-permute-start | bytes 3686408 | tf_op jit(solution)/shard_map/ppermute | solution.py:80
  148.9 57.0 %all-to-all-start.2 = ((bf16[4,160,960]{2,1,0:T(8,128)(2,1)}), bf16[4,160,960]{2,1,0:T(8,128)(2,1)}, u32[]{:S(2)}, u32[]{:S(2)}) async-start(bf16[4,160,960]{2,1,0:T(8,128)(2,1)} %bitcast.103), calls=%async_computation.2 | async-start | bytes 2621440 | tf_op jit(solution)/shard_map/all_to_all | solution.py:93
  153.2 21.9 %collective-permute-start.19 = (bf16[4,160,960]{2,1,0:T(8,128)(2,1)S(1)}, bf16[4,160,960]{2,1,0:T(8,128)(2,1)S(1)}, u32[]{:S(2)}, u32[]{:S(2)}) collective-permute-start(bf16[4,160,960]{2,1,0:T(8,128)(2,1)S(1)} %all-to-all-done.own), channel_id=1, source_target_pairs={{0,2},{2,0},{4,6},{6,4},{8,10},{10,8},{12,14},{14,12},{16,18},{18,... | collective-permute-start | bytes 3686408 | tf_op jit(solution)/shard_map/ppermute | solution.py:83
  153.3 23.3 %collective-permute-start.20 = (bf16[4,160,960]{2,1,0:T(8,128)(2,1)}, bf16[4,160,960]{2,1,0:T(8,128)(2,1)S(1)}, u32[]{:S(2)}, u32[]{:S(2)}) collective-permute-start(bf16[4,160,960]{2,1,0:T(8,128)(2,1)} %collective-permute-done.18.side), channel_id=1, source_target_pairs={{0,2},{2,0},{4,6},{6,4},{8,10},{10,8},{12,14},{14,12},{16,18},{18,... | collective-permute-start | bytes 3686408 | tf_op jit(solution)/shard_map/ppermute | solution.py:83
  153.7 52.1 %collective-permute-start.21 = (bf16[4,160,960]{2,1,0:T(8,128)(2,1)S(1)}, bf16[4,160,960]{2,1,0:T(8,128)(2,1)}, u32[]{:S(2)}, u32[]{:S(2)}) collective-permute-start(bf16[4,160,960]{2,1,0:T(8,128)(2,1)S(1)} %all-to-all-done.1.own), channel_id=1, source_target_pairs={{0,4},{2,6},{4,0},{6,2},{8,12},{10,14},{12,8},{14,10},{16,20},{18,... | collective-permute-start | bytes 3686408 | tf_op jit(solution)/shard_map/ppermute | solution.py:80
  173.2 32.6 %collective-permute-start.25 = (bf16[96,2560]{1,0:T(8,128)(2,1)S(1)}, bf16[96,2560]{1,0:T(8,128)(2,1)}, u32[]{:S(2)}, u32[]{:S(2)}) collective-permute-start(bf16[96,2560]{1,0:T(8,128)(2,1)S(1)} %bitcast.86), channel_id=1, source_target_pairs={{0,8},{2,10},{4,12},{6,14},{8,16},{10,18},{12,20},{14,22},{16,24},... | collective-permute-start | bytes 1474568 | tf_op jit(solution)/shard_map/ppermute | solution.py:89
  175.0 30.8 %collective-permute-start.24 = (bf16[96,2560]{1,0:T(8,128)(2,1)}, bf16[96,2560]{1,0:T(8,128)(2,1)}, u32[]{:S(2)}, u32[]{:S(2)}) collective-permute-start(bf16[96,2560]{1,0:T(8,128)(2,1)} %get-tuple-element.488.own_ref.refs_0_), channel_id=1, source_target_pairs={{0,8},{2,10},{4,12},{6,14},{8,16},{10,18},{12,20},{14,22},{16,24},... | collective-permute-start | bytes 1474568 | tf_op jit(solution)/shard_map/ppermute | solution.py:89
  176.5 31.0 %collective-permute-start.22 = (bf16[4,160,960]{2,1,0:T(8,128)(2,1)S(1)}, bf16[4,160,960]{2,1,0:T(8,128)(2,1)}, u32[]{:S(2)}, u32[]{:S(2)}) collective-permute-start(bf16[4,160,960]{2,1,0:T(8,128)(2,1)S(1)} %all-to-all-done.1.own), channel_id=1, source_target_pairs={{0,2},{2,0},{4,6},{6,4},{8,10},{10,8},{12,14},{14,12},{16,18},{18,... | collective-permute-start | bytes 3686408 | tf_op jit(solution)/shard_map/ppermute | solution.py:83
  205.8 18.3 %collective-permute-start.26 = (bf16[4,160,960]{2,1,0:T(8,128)(2,1)}, bf16[4,160,960]{2,1,0:T(8,128)(2,1)S(1)}, u32[]{:S(2)}, u32[]{:S(2)}) collective-permute-start(bf16[4,160,960]{2,1,0:T(8,128)(2,1)} %collective-permute-done.21.side), channel_id=1, source_target_pairs={{0,2},{2,0},{4,6},{6,4},{8,10},{10,8},{12,14},{14,12},{16,18},{18,... | collective-permute-start | bytes 3686408 | tf_op jit(solution)/shard_map/ppermute | solution.py:83
  205.9 31.4 %collective-permute-start.27 = (bf16[4,160,960]{2,1,0:T(8,128)(2,1)}, bf16[4,160,960]{2,1,0:T(8,128)(2,1)S(1)}, u32[]{:S(2)}, u32[]{:S(2)}) collective-permute-start(bf16[4,160,960]{2,1,0:T(8,128)(2,1)} %all-to-all-done.2.own), channel_id=1, source_target_pairs={{0,4},{2,6},{4,0},{6,2},{8,12},{10,14},{12,8},{14,10},{16,20},{18,... | collective-permute-start | bytes 3686408 | tf_op jit(solution)/shard_map/ppermute | solution.py:80
  206.5 16.2 %collective-permute-start.30 = (bf16[96,2560]{1,0:T(8,128)(2,1)}, bf16[96,2560]{1,0:T(8,128)(2,1)}, u32[]{:S(2)}, u32[]{:S(2)}) collective-permute-start(bf16[96,2560]{1,0:T(8,128)(2,1)} %collective-permute-done.25.dyo_ref.refs_2_), channel_id=1, source_target_pairs={{0,8},{2,10},{4,12},{6,14},{8,16},{10,18},{12,20},{14,22},{16,24},... | collective-permute-start | bytes 1474568 | tf_op jit(solution)/shard_map/ppermute | solution.py:89
  206.5 25.9 %collective-permute-start.29 = (bf16[96,2560]{1,0:T(8,128)(2,1)}, bf16[96,2560]{1,0:T(8,128)(2,1)}, u32[]{:S(2)}, u32[]{:S(2)}) collective-permute-start(bf16[96,2560]{1,0:T(8,128)(2,1)} %collective-permute-done.24.own_ref.refs_2_), channel_id=1, source_target_pairs={{0,8},{2,10},{4,12},{6,14},{8,16},{10,18},{12,20},{14,22},{16,24},... | collective-permute-start | bytes 1474568 | tf_op jit(solution)/shard_map/ppermute | solution.py:89
  207.5 24.9 %collective-permute-start.32 = (bf16[96,2560]{1,0:T(8,128)(2,1)}, bf16[96,2560]{1,0:T(8,128)(2,1)S(1)}, u32[]{:S(2)}, u32[]{:S(2)}) collective-permute-start(bf16[96,2560]{1,0:T(8,128)(2,1)} %collective-permute-done.25.dyo_ref.refs_2_), channel_id=1, source_target_pairs={{0,1},{1,0},{2,3},{3,2},{4,5},{5,4},{6,7},{7,6},{8,9},{9,8},{10,11... | collective-permute-start | bytes 1474568 | tf_op jit(solution)/shard_map/ppermute | solution.py:86
  224.1 15.7 %collective-permute-start.28 = (bf16[4,160,960]{2,1,0:T(8,128)(2,1)}, bf16[4,160,960]{2,1,0:T(8,128)(2,1)S(1)}, u32[]{:S(2)}, u32[]{:S(2)}) collective-permute-start(bf16[4,160,960]{2,1,0:T(8,128)(2,1)} %all-to-all-done.2.own), channel_id=1, source_target_pairs={{0,2},{2,0},{4,6},{6,4},{8,10},{10,8},{12,14},{14,12},{16,18},{18,... | collective-permute-start | bytes 3686408 | tf_op jit(solution)/shard_map/ppermute | solution.py:83
  237.3 25.2 %collective-permute-start.35 = (bf16[96,2560]{1,0:T(8,128)(2,1)}, bf16[96,2560]{1,0:T(8,128)(2,1)}, u32[]{:S(2)}, u32[]{:S(2)}) collective-permute-start(bf16[96,2560]{1,0:T(8,128)(2,1)} %collective-permute-done.30.dyo_ref.refs_4_), channel_id=1, source_target_pairs={{0,8},{2,10},{4,12},{6,14},{8,16},{10,18},{12,20},{14,22},{16,24},... | collective-permute-start | bytes 1474568 | tf_op jit(solution)/shard_map/ppermute | solution.py:89
  237.3 26.3 %collective-permute-start.34 = (bf16[96,2560]{1,0:T(8,128)(2,1)}, bf16[96,2560]{1,0:T(8,128)(2,1)}, u32[]{:S(2)}, u32[]{:S(2)}) collective-permute-start(bf16[96,2560]{1,0:T(8,128)(2,1)} %collective-permute-done.29.own_ref.refs_4_), channel_id=1, source_target_pairs={{0,8},{2,10},{4,12},{6,14},{8,16},{10,18},{12,20},{14,22},{16,24},... | collective-permute-start | bytes 1474568 | tf_op jit(solution)/shard_map/ppermute | solution.py:89
  238.4 25.2 %collective-permute-start.37 = (bf16[96,2560]{1,0:T(8,128)(2,1)}, bf16[96,2560]{1,0:T(8,128)(2,1)}, u32[]{:S(2)}, u32[]{:S(2)}) collective-permute-start(bf16[96,2560]{1,0:T(8,128)(2,1)} %collective-permute-done.30.dyo_ref.refs_4_), channel_id=1, source_target_pairs={{0,1},{1,0},{2,3},{3,2},{4,5},{5,4},{6,7},{7,6},{8,9},{9,8},{10,11... | collective-permute-start | bytes 1474568 | tf_op jit(solution)/shard_map/ppermute | solution.py:86
  240.9 22.7 %collective-permute-start.36 = (bf16[96,2560]{1,0:T(8,128)(2,1)}, bf16[96,2560]{1,0:T(8,128)(2,1)}, u32[]{:S(2)}, u32[]{:S(2)}) collective-permute-start(bf16[96,2560]{1,0:T(8,128)(2,1)} %collective-permute-done.29.own_ref.refs_4_), channel_id=1, source_target_pairs={{0,1},{1,0},{2,3},{3,2},{4,5},{5,4},{6,7},{7,6},{8,9},{9,8},{10,11... | collective-permute-start | bytes 1474568 | tf_op jit(solution)/shard_map/ppermute | solution.py:86
  276.7 23.4 %collective-permute-start.38 = (bf16[96,2560]{1,0:T(8,128)(2,1)}, bf16[96,2560]{1,0:T(8,128)(2,1)S(1)}, u32[]{:S(2)}, u32[]{:S(2)}) collective-permute-start(bf16[96,2560]{1,0:T(8,128)(2,1)} %collective-permute-done.34.own_ref.refs_6_), channel_id=1, source_target_pairs={{0,1},{1,0},{2,3},{3,2},{4,5},{5,4},{6,7},{7,6},{8,9},{9,8},{10,11... | collective-permute-start | bytes 1474568 | tf_op jit(solution)/shard_map/ppermute | solution.py:86
  277.3 32.1 %collective-permute-start.40 = (bf16[96,2560]{1,0:T(8,128)(2,1)S(1)}, bf16[96,2560]{1,0:T(8,128)(2,1)S(1)}, u32[]{:S(2)}, u32[]{:S(2)}) collective-permute-start(bf16[96,2560]{1,0:T(8,128)(2,1)S(1)} %get-tuple-element.438), channel_id=1, source_target_pairs={{0,1},{1,0},{2,3},{3,2},{4,5},{5,4},{6,7},{7,6},{8,9},{9,8},{10,11... | collective-permute-start | bytes 1474568 | tf_op jit(solution)/shard_map/ppermute | solution.py:86
  332.8 16.0 %collective-permute-start.48 = (bf16[2,160,960]{2,1,0:T(8,128)(2,1)S(1)}, bf16[2,160,960]{2,1,0:T(8,128)(2,1)S(1)}, u32[]{:S(2)}, u32[]{:S(2)}) collective-permute-start(bf16[2,160,960]{2,1,0:T(8,128)(2,1)S(1)} %get-tuple-element.478), channel_id=1, source_target_pairs={{0,2},{2,0},{4,6},{6,4},{8,10},{10,8},{12,14},{14,12},{16,18},{18,... | collective-permute-start | bytes 1843208 | tf_op jit(solution)/shard_map/ppermute | solution.py:83
  350.7 36.8 %collective-permute-start.56 = (bf16[4,160,960]{2,1,0:T(8,128)(2,1)S(1)}, bf16[4,160,960]{2,1,0:T(8,128)(2,1)S(1)}, u32[]{:S(2)}, u32[]{:S(2)}) collective-permute-start(bf16[4,160,960]{2,1,0:T(8,128)(2,1)S(1)} %get-tuple-element.510), channel_id=1, source_target_pairs={{0,4},{2,6},{4,0},{6,2},{8,12},{10,14},{12,8},{14,10},{16,20},{18,... | collective-permute-start | bytes 3686408 | tf_op jit(solution)/shard_map/ppermute | solution.py:80
  382.1 19.8 %collective-permute-start.58 = (bf16[96,2560]{1,0:T(8,128)(2,1)}, bf16[96,2560]{1,0:T(8,128)(2,1)}, u32[]{:S(2)}, u32[]{:S(2)}) collective-permute-start(bf16[96,2560]{1,0:T(8,128)(2,1)} %get-tuple-element.521), channel_id=1, source_target_pairs={{0,1},{1,0},{2,3},{3,2},{4,5},{5,4},{6,7},{7,6},{8,9},{9,8},{10,11... | collective-permute-start | bytes 1474568 | tf_op jit(solution)/shard_map/ppermute | solution.py:86
  395.4 31.4 %collective-permute-start.63 = (bf16[4,160,960]{2,1,0:T(8,128)(2,1)}, bf16[4,160,960]{2,1,0:T(8,128)(2,1)}, u32[]{:S(2)}, u32[]{:S(2)}) collective-permute-start(bf16[4,160,960]{2,1,0:T(8,128)(2,1)} %get-tuple-element.541), channel_id=1, source_target_pairs={{0,4},{2,6},{4,0},{6,2},{8,12},{10,14},{12,8},{14,10},{16,20},{18,... | collective-permute-start | bytes 3686408 | tf_op jit(solution)/shard_map/ppermute | solution.py:80
  395.9 16.8 %collective-permute-start.62 = (bf16[2,160,960]{2,1,0:T(8,128)(2,1)}, bf16[2,160,960]{2,1,0:T(8,128)(2,1)}, u32[]{:S(2)}, u32[]{:S(2)}) collective-permute-start(bf16[2,160,960]{2,1,0:T(8,128)(2,1)} %get-tuple-element.536), channel_id=1, source_target_pairs={{0,2},{2,0},{4,6},{6,4},{8,10},{10,8},{12,14},{14,12},{16,18},{18,... | collective-permute-start | bytes 1843208 | tf_op jit(solution)/shard_map/ppermute | solution.py:83
  395.9 17.4 %collective-permute-start.61 = (bf16[2,160,960]{2,1,0:T(8,128)(2,1)}, bf16[2,160,960]{2,1,0:T(8,128)(2,1)}, u32[]{:S(2)}, u32[]{:S(2)}) collective-permute-start(bf16[2,160,960]{2,1,0:T(8,128)(2,1)} %get-tuple-element.534), channel_id=1, source_target_pairs={{0,2},{2,0},{4,6},{6,4},{8,10},{10,8},{12,14},{14,12},{16,18},{18,... | collective-permute-start | bytes 1843208 | tf_op jit(solution)/shard_map/ppermute | solution.py:83
  398.1 46.0 %all-to-all-start.3 = ((bf16[4,160,960]{2,1,0:T(8,128)(2,1)}), bf16[4,160,960]{2,1,0:T(8,128)(2,1)S(1)}, u32[]{:S(2)}, u32[]{:S(2)}) async-start(bf16[4,160,960]{2,1,0:T(8,128)(2,1)} %shard_map.262), calls=%async_computation.3 | async-start | bytes 2621440 | tf_op jit(solution)/shard_map/all_to_all | solution.py:93
  401.9 21.3 %collective-permute-start.60 = (bf16[2,160,960]{2,1,0:T(8,128)(2,1)}, bf16[2,160,960]{2,1,0:T(8,128)(2,1)S(1)}, u32[]{:S(2)}, u32[]{:S(2)}) collective-permute-start(bf16[2,160,960]{2,1,0:T(8,128)(2,1)} %copy-done.116), channel_id=1, source_target_pairs={{0,2},{2,0},{4,6},{6,4},{8,10},{10,8},{12,14},{14,12},{16,18},{18,... | collective-permute-start | bytes 1843208 | tf_op jit(solution)/shard_map/ppermute | solution.py:83
  403.9 20.1 %collective-permute-start.59 = (bf16[2,160,960]{2,1,0:T(8,128)(2,1)S(1)}, bf16[2,160,960]{2,1,0:T(8,128)(2,1)S(1)}, u32[]{:S(2)}, u32[]{:S(2)}) collective-permute-start(bf16[2,160,960]{2,1,0:T(8,128)(2,1)S(1)} %copy-done.115), channel_id=1, source_target_pairs={{0,2},{2,0},{4,6},{6,4},{8,10},{10,8},{12,14},{14,12},{16,18},{18,... | collective-permute-start | bytes 1843208 | tf_op jit(solution)/shard_map/ppermute | solution.py:83
  413.3 24.8 %collective-permute-start.65 = (bf16[96,2560]{1,0:T(8,128)(2,1)}, bf16[96,2560]{1,0:T(8,128)(2,1)S(1)}, u32[]{:S(2)}, u32[]{:S(2)}) collective-permute-start(bf16[96,2560]{1,0:T(8,128)(2,1)} %shard_map.264), channel_id=1, source_target_pairs={{0,8},{2,10},{4,12},{6,14},{8,16},{10,18},{12,20},{14,22},{16,24},... | collective-permute-start | bytes 1474568 | tf_op jit(solution)/shard_map/ppermute | solution.py:89
  424.0 28.0 %collective-permute-start.69 = (bf16[2,160,1280]{2,1,0:T(8,128)(2,1)}, bf16[2,160,1280]{2,1,0:T(8,128)(2,1)}, u32[]{:S(2)}, u32[]{:S(2)}) collective-permute-start(bf16[2,160,1280]{2,1,0:T(8,128)(2,1)} %get-tuple-element.559), channel_id=1, source_target_pairs={{0,2},{2,0},{4,6},{6,4},{8,10},{10,8},{12,14},{14,12},{16,18},{18,... | collective-permute-start | bytes 2457608 | tf_op jit(solution)/shard_map/ppermute | solution.py:83
  424.8 32.6 %collective-permute-start.68 = (bf16[2,160,1280]{2,1,0:T(8,128)(2,1)}, bf16[2,160,1280]{2,1,0:T(8,128)(2,1)}, u32[]{:S(2)}, u32[]{:S(2)}) collective-permute-start(bf16[2,160,1280]{2,1,0:T(8,128)(2,1)} %get-tuple-element.557), channel_id=1, source_target_pairs={{0,2},{2,0},{4,6},{6,4},{8,10},{10,8},{12,14},{14,12},{16,18},{18,... | collective-permute-start | bytes 2457608 | tf_op jit(solution)/shard_map/ppermute | solution.py:83
  426.8 30.7 %collective-permute-start.67 = (bf16[2,160,1280]{2,1,0:T(8,128)(2,1)}, bf16[2,160,1280]{2,1,0:T(8,128)(2,1)}, u32[]{:S(2)}, u32[]{:S(2)}) collective-permute-start(bf16[2,160,1280]{2,1,0:T(8,128)(2,1)} %get-tuple-element.555), channel_id=1, source_target_pairs={{0,2},{2,0},{4,6},{6,4},{8,10},{10,8},{12,14},{14,12},{16,18},{18,... | collective-permute-start | bytes 2457608 | tf_op jit(solution)/shard_map/ppermute | solution.py:83
  426.8 30.7 %collective-permute-start.66 = (bf16[2,160,1280]{2,1,0:T(8,128)(2,1)}, bf16[2,160,1280]{2,1,0:T(8,128)(2,1)}, u32[]{:S(2)}, u32[]{:S(2)}) collective-permute-start(bf16[2,160,1280]{2,1,0:T(8,128)(2,1)} %get-tuple-element.553), channel_id=1, source_target_pairs={{0,2},{2,0},{4,6},{6,4},{8,10},{10,8},{12,14},{14,12},{16,18},{18,... | collective-permute-start | bytes 2457608 | tf_op jit(solution)/shard_map/ppermute | solution.py:83
  438.1 38.3 %collective-permute-start.70 = (bf16[4,160,960]{2,1,0:T(8,128)(2,1)}, bf16[4,160,960]{2,1,0:T(8,128)(2,1)}, u32[]{:S(2)}, u32[]{:S(2)}) collective-permute-start(bf16[4,160,960]{2,1,0:T(8,128)(2,1)} %get-tuple-element.566), channel_id=1, source_target_pairs={{0,4},{2,6},{4,0},{6,2},{8,12},{10,14},{12,8},{14,10},{16,20},{18,... | collective-permute-start | bytes 3686408 | tf_op jit(solution)/shard_map/ppermute | solution.py:80
  444.1 60.5 %all-to-all-start.4 = ((bf16[4,160,960]{2,1,0:T(8,128)(2,1)}), bf16[4,160,960]{2,1,0:T(8,128)(2,1)S(1)}, u32[]{:S(2)}, u32[]{:S(2)}) async-start(bf16[4,160,960]{2,1,0:T(8,128)(2,1)} %copy-done.9), calls=%async_computation.4 | async-start | bytes 2621440 | tf_op jit(solution)/shard_map/all_to_all | solution.py:93
  452.0 23.9 %collective-permute-start.71 = (bf16[96,2560]{1,0:T(8,128)(2,1)}, bf16[96,2560]{1,0:T(8,128)(2,1)S(1)}, u32[]{:S(2)}, u32[]{:S(2)}) collective-permute-start(bf16[96,2560]{1,0:T(8,128)(2,1)} %copy-done.118), channel_id=1, source_target_pairs={{0,1},{1,0},{2,3},{3,2},{4,5},{5,4},{6,7},{7,6},{8,9},{9,8},{10,11... | collective-permute-start | bytes 1474568 | tf_op jit(solution)/shard_map/ppermute | solution.py:86
  476.5 38.9 %collective-permute-start.84 = (bf16[4,160,1280]{2,1,0:T(8,128)(2,1)}, bf16[4,160,1280]{2,1,0:T(8,128)(2,1)}, u32[]{:S(2)}, u32[]{:S(2)}) collective-permute-start(bf16[4,160,1280]{2,1,0:T(8,128)(2,1)} %get-tuple-element.600), channel_id=1, source_target_pairs={{0,4},{2,6},{4,0},{6,2},{8,12},{10,14},{12,8},{14,10},{16,20},{18,... | collective-permute-start | bytes 4915208 | tf_op jit(solution)/shard_map/ppermute | solution.py:80
  479.5 15.8 %collective-permute-start.73 = (bf16[2,160,768]{2,1,0:T(8,128)(2,1)}, bf16[2,160,768]{2,1,0:T(8,128)(2,1)}, u32[]{:S(2)}, u32[]{:S(2)}) collective-permute-start(bf16[2,160,768]{2,1,0:T(8,128)(2,1)} %get-tuple-element.575), channel_id=1, source_target_pairs={{0,2},{2,0},{4,6},{6,4},{8,10},{10,8},{12,14},{14,12},{16,18},{18,... | collective-permute-start | bytes 1474568 | tf_op jit(solution)/shard_map/ppermute | solution.py:83
  482.6 20.6 %collective-permute-start.81 = (bf16[96,2560]{1,0:T(8,128)(2,1)}, bf16[96,2560]{1,0:T(8,128)(2,1)}, u32[]{:S(2)}, u32[]{:S(2)}) collective-permute-start(bf16[96,2560]{1,0:T(8,128)(2,1)} %get-tuple-element.594), channel_id=1, source_target_pairs={{0,1},{1,0},{2,3},{3,2},{4,5},{5,4},{6,7},{7,6},{8,9},{9,8},{10,11... | collective-permute-start | bytes 1474568 | tf_op jit(solution)/shard_map/ppermute | solution.py:86
  484.9 18.3 %collective-permute-start.80 = (bf16[96,2560]{1,0:T(8,128)(2,1)}, bf16[96,2560]{1,0:T(8,128)(2,1)}, u32[]{:S(2)}, u32[]{:S(2)}) collective-permute-start(bf16[96,2560]{1,0:T(8,128)(2,1)} %shard_map.272), channel_id=1, source_target_pairs={{0,8},{2,10},{4,12},{6,14},{8,16},{10,18},{12,20},{14,22},{16,24},... | collective-permute-start | bytes 1474568 | tf_op jit(solution)/shard_map/ppermute | solution.py:89
  505.2 19.6 %collective-permute-start.83 = (bf16[96,2560]{1,0:T(8,128)(2,1)S(1)}, bf16[96,2560]{1,0:T(8,128)(2,1)}, u32[]{:S(2)}, u32[]{:S(2)}) collective-permute-start(bf16[96,2560]{1,0:T(8,128)(2,1)S(1)} %shard_map.276), channel_id=1, source_target_pairs={{0,8},{2,10},{4,12},{6,14},{8,16},{10,18},{12,20},{14,22},{16,24},... | collective-permute-start | bytes 1474568 | tf_op jit(solution)/shard_map/ppermute | solution.py:89
  511.0 79.1 %all-to-all-start.5 = ((bf16[4,160,960]{2,1,0:T(8,128)(2,1)}), bf16[4,160,960]{2,1,0:T(8,128)(2,1)}, u32[]{:S(2)}, u32[]{:S(2)}) async-start(bf16[4,160,960]{2,1,0:T(8,128)(2,1)} %copy-done.10), calls=%async_computation.5 | async-start | bytes 2621440 | tf_op jit(solution)/shard_map/all_to_all | solution.py:93
  520.0 32.2 %collective-permute-start.90 = (bf16[4,160,768]{2,1,0:T(8,128)(2,1)}, bf16[4,160,768]{2,1,0:T(8,128)(2,1)S(1)}, u32[]{:S(2)}, u32[]{:S(2)}) collective-permute-start(bf16[4,160,768]{2,1,0:T(8,128)(2,1)} %get-tuple-element.616), channel_id=1, source_target_pairs={{0,4},{2,6},{4,0},{6,2},{8,12},{10,14},{12,8},{14,10},{16,20},{18,... | collective-permute-start | bytes 2949128 | tf_op jit(solution)/shard_map/ppermute | solution.py:80
  522.9 26.9 %collective-permute-start.87 = (bf16[160,1280]{1,0:T(8,128)(2,1)}, bf16[160,1280]{1,0:T(8,128)(2,1)}, u32[]{:S(2)}, u32[]{:S(2)}) collective-permute-start(bf16[160,1280]{1,0:T(8,128)(2,1)} %shard_map.281), channel_id=1, source_target_pairs={{0,8},{2,10},{4,12},{6,14},{8,16},{10,18},{12,20},{14,22},{16,24},... | collective-permute-start | bytes 1228808 | tf_op jit(solution)/shard_map/ppermute | solution.py:89
  526.4 25.8 %collective-permute-start.86 = (bf16[96,2560]{1,0:T(8,128)(2,1)S(1)}, bf16[96,2560]{1,0:T(8,128)(2,1)}, u32[]{:S(2)}, u32[]{:S(2)}) collective-permute-start(bf16[96,2560]{1,0:T(8,128)(2,1)S(1)} %add_convert_fusion), channel_id=1, source_target_pairs={{0,1},{1,0},{2,3},{3,2},{4,5},{5,4},{6,7},{7,6},{8,9},{9,8},{10,11... | collective-permute-start | bytes 1474568 | tf_op jit(solution)/shard_map/ppermute | solution.py:86
  552.2 43.1 %collective-permute-start.95 = (bf16[4,160,768]{2,1,0:T(8,128)(2,1)}, bf16[4,160,768]{2,1,0:T(8,128)(2,1)}, u32[]{:S(2)}, u32[]{:S(2)}) collective-permute-start(bf16[4,160,768]{2,1,0:T(8,128)(2,1)} %get-tuple-element.631), channel_id=1, source_target_pairs={{0,4},{2,6},{4,0},{6,2},{8,12},{10,14},{12,8},{14,10},{16,20},{18,... | collective-permute-start | bytes 2949128 | tf_op jit(solution)/shard_map/ppermute | solution.py:80
  570.3 22.9 %collective-permute-start.94 = (bf16[160,1280]{1,0:T(8,128)(2,1)}, bf16[160,1280]{1,0:T(8,128)(2,1)}, u32[]{:S(2)}, u32[]{:S(2)}) collective-permute-start(bf16[160,1280]{1,0:T(8,128)(2,1)} %shard_map.285), channel_id=1, source_target_pairs={{0,8},{2,10},{4,12},{6,14},{8,16},{10,18},{12,20},{14,22},{16,24},... | collective-permute-start | bytes 1228808 | tf_op jit(solution)/shard_map/ppermute | solution.py:89
  572.8 16.3 %collective-permute-start.93 = (bf16[160,768]{1,0:T(8,128)(2,1)S(1)}, bf16[160,768]{1,0:T(8,128)(2,1)}, u32[]{:S(2)}, u32[]{:S(2)}) collective-permute-start(bf16[160,768]{1,0:T(8,128)(2,1)S(1)} %shard_map.284), channel_id=1, source_target_pairs={{0,8},{2,10},{4,12},{6,14},{8,16},{10,18},{12,20},{14,22},{16,24},... | collective-permute-start | bytes 737288 | tf_op jit(solution)/shard_map/ppermute | solution.py:89
  581.3 24.0 %collective-permute-start.89 = (bf16[96,2560]{1,0:T(8,128)(2,1)S(1)}, bf16[96,2560]{1,0:T(8,128)(2,1)}, u32[]{:S(2)}, u32[]{:S(2)}) collective-permute-start(bf16[96,2560]{1,0:T(8,128)(2,1)S(1)} %copy-done.60), channel_id=1, source_target_pairs={{0,1},{1,0},{2,3},{3,2},{4,5},{5,4},{6,7},{7,6},{8,9},{9,8},{10,11... | collective-permute-start | bytes 1474568 | tf_op jit(solution)/shard_map/ppermute | solution.py:86
  603.1 16.7 %collective-permute-start.97 = (f32[15360]{0:T(1024)S(1)}, f32[15360]{0:T(1024)S(1)}, u32[]{:S(2)}, u32[]{:S(2)}) collective-permute-start(f32[15360]{0:T(1024)S(1)} %add.224), channel_id=1, source_target_pairs={{0,16},{2,18},{4,20},{6,22},{8,24},{10,26},{12,28},{14,30},{16,0},... | collective-permute-start | bytes 184328 | tf_op jit(solution)/shard_map/ppermute | solution.py:852
  (190 other events, 1798.0 us)
